TPU v7x, 128 devices: a whole 4x4x4 slice. The times are simulated.
128 devices in a mesh: section: 4 (over x), dp: 16 (over z, y), mp: 2 (over core).
Axes of the slice: x: 4, y: 4, z: 4, core: 2. Of those that a mesh axis runs over, the one named last changes fastest.
Arguments:
- tokens: bfloat16 [128, 8192], P(None, 'dp'), may hold values from -13 to 13
- keep: int32 [4, 128], replicated, may hold values 0 or 1
- norm_gain: bfloat16 [4, 8192], P('section', 'dp'), may hold values from 0.25 to 1.75
- w_up: bfloat16 [4, 8192, 14336], P('section', 'dp', 'mp'), may hold values from -0.0625 to 0.0625
- w_down: bfloat16 [4, 14336, 8192], P('section', 'mp', 'dp'), may hold values from -0.09375 to 0.09375
- head_gain: bfloat16 [8192], P('dp'), may hold values from 0.25 to 1.75
- w_head: bfloat16 [8192, 65536], P('dp', ('section', 'mp')), may hold values from -2 to 2
- exit_idx: int32 [4, 32], replicated, may hold values from 0 to 127
- exit_count: int32 [4], replicated, may hold values from 1 to 32, 80 in all
- kl_bucket: int32 [4, 32], replicated, may hold values from 0 to 15
Outputs:
- feature_grad: float32 [128, 8192], P(('section', 'mp'), 'dp')
- kl_rows: float32 [128], P('dp')
- histogram: float32 [4, 16], replicated
Inputs may be any that keep to these rules, and one draw needn't show every extreme that they name: Section s's live exits are the first exit_count[s] slots of row s; the largest count equals 32.
All inputs are finite; a program needn't handle non-finite values.
Results may differ from a plain program's by a relative error of at most 0.03405.
Values may be sent and summed in bfloat16 or wider, within the bound.
No kernel may reach another device: no remote copies, remote signals or barrier semaphores. Data moves between devices by JAX's collectives and lax.ppermute only.
A program may use at most 128 MiB of HBM per device.

v0:
```python
import jax
import jax.numpy as jnp
from jax import lax
from jax.sharding import PartitionSpec as P

D = 8192
XS = 32
NB = 16


epsilon = 1e-05


def shifted(value, axis, by):
    count = lax.axis_size(axis)
    pairs = [(i, i + by) for i in range(count) if 0 <= i + by < count]
    return lax.ppermute(value, axis, pairs)


def broadcast(value, axis, root):
    mine = lax.axis_index(axis) == root
    return lax.psum(jnp.where(mine, value, jnp.zeros_like(value)), axis)


def shards(
    tokens, keep, norm_gain, w_up, w_down, head_gain, w_head, exit_idx, exit_count, kl_bucket
):
    sections = lax.axis_size("section")
    section_id = lax.axis_index("section")
    gain_local = norm_gain[0].astype(jnp.float32)
    up_local = w_up[0]
    down_local = w_down[0]
    keep_mine = lax.dynamic_index_in_dim(keep, section_id, 0, keepdims=False)
    current = tokens
    mine = tokens
    for step in range(sections):
        wide = current.astype(jnp.float32)
        normed = (wide * gain_local).astype(jnp.bfloat16)
        layer_squares, raised = lax.psum(
            (
                jnp.sum(wide * wide, axis=-1),
                jnp.dot(normed, up_local, preferred_element_type=jnp.float32),
            ),
            "dp",
        )
        scale = lax.rsqrt(layer_squares / D + epsilon)
        active = jax.nn.silu(raised * scale[:, None]).astype(jnp.bfloat16)
        partial_down = jnp.dot(active, down_local, preferred_element_type=jnp.float32)
        lowered = lax.psum(partial_down, "mp")
        result = (wide + keep_mine[:, None].astype(jnp.float32) * lowered).astype(jnp.bfloat16)
        mine = jnp.where(section_id == step, result, mine)
        if step < sections - 1:
            current = shifted(result, "section", 1)
    own_index = lax.dynamic_index_in_dim(exit_idx, section_id, 0, keepdims=False)
    exits = lax.all_gather(jnp.take(mine, own_index, axis=0), "section", axis=0, tiled=True)
    finals = broadcast(jnp.take(mine, exit_idx.reshape(-1), axis=0), "section", sections - 1)
    paired = jnp.stack([exits, finals], axis=1)
    wide_rows = paired.astype(jnp.float32)
    squares_part = jnp.sum(wide_rows * wide_rows, axis=-1)
    headed = (wide_rows * head_gain.astype(jnp.float32)).astype(jnp.bfloat16)
    count_rows = paired.shape[0]
    groups = lax.axis_size("dp")
    live_all = (jnp.arange(XS)[None, :] < exit_count[:, None]).reshape(-1).astype(jnp.float32)
    bucket_all = kl_bucket.reshape(-1)
    squares = lax.psum(squares_part, "dp")
    share = count_rows // groups
    first_row = lax.axis_index("dp") * share
    part = headed
    totals = lax.psum_scatter(
        jnp.einsum("rkd,dv->rkv", part, w_head, preferred_element_type=jnp.float32),
        "dp",
        scatter_dimension=0,
        tiled=True,
    )
    scale_all = lax.rsqrt(squares / D + epsilon)
    logits = totals * lax.dynamic_slice_in_dim(scale_all, first_row, share, 0)[:, :, None]
    live_here = lax.dynamic_slice_in_dim(live_all, first_row, share, 0)
    bucket_here = lax.dynamic_slice_in_dim(bucket_all, first_row, share, 0)
    spread = logits[:, 1] - logits[:, 0]
    peak_local = jnp.max(logits, axis=-1)
    peak = lax.pmax(peak_local, ("section", "mp"))
    powers = jnp.exp(logits - peak[:, :, None])
    sums, cross = lax.psum(
        (jnp.sum(powers, axis=-1), jnp.sum(powers[:, 1] * spread, axis=-1)), ("section", "mp")
    )
    totals_log = peak + jnp.log(sums)
    kl_here = (cross / sums[:, 1] - totals_log[:, 1] + totals_log[:, 0]) * live_here
    exit_prob = jnp.exp(logits[:, 0] - totals_log[:, 0, None])
    final_prob = jnp.exp(logits[:, 1] - totals_log[:, 1, None])
    gap = ((exit_prob - final_prob) * live_here[:, None]).astype(jnp.bfloat16)
    section_of = (first_row + jnp.arange(share)) // XS
    weighted = (section_of[:, None] == jnp.arange(sections)[None, :]).astype(jnp.float32) * kl_here[
        :, None
    ]
    bucket_hot = (bucket_here[:, None] == jnp.arange(NB)[None, :]).astype(jnp.float32)
    hist_part = jnp.dot(weighted.T, bucket_hot, precision=lax.Precision.HIGHEST)
    histogram = lax.psum(hist_part, "dp")
    gaps = lax.all_gather(gap, "dp", axis=0, tiled=True)
    grad_share = count_rows // (sections * lax.axis_size("mp"))
    part = gaps
    feature = lax.psum_scatter(
        lax.dot_general(
            part, w_head, (((1,), (1,)), ((), ())), preferred_element_type=jnp.float32
        ).astype(jnp.bfloat16),
        ("section", "mp"),
        scatter_dimension=0,
        tiled=True,
    ).astype(jnp.float32)
    grad_first = lax.axis_index(("section", "mp")) * grad_share
    feature_grad = (
        feature * lax.dynamic_slice_in_dim(scale_all[:, 0], grad_first, grad_share, 0)[:, None]
    )
    return (feature_grad, kl_here, histogram)


def solution(mesh):
    return jax.shard_map(
        shards,
        mesh=mesh,
        in_specs=(
            P(None, "dp"),
            P(),
            P("section", "dp"),
            P("section", "dp", "mp"),
            P("section", "mp", "dp"),
            P("dp"),
            P("dp", ("section", "mp")),
            P(),
            P(),
            P(),
        ),
        out_specs=(P(("section", "mp"), "dp"), P("dp"), P()),
        check_vma=False,
    )
```

profile of v0, /device:TPU:1, one launch (start us, length us, event | category | flops | bytes accessed | tf_op | source)
XLA Modules:
  0.0 839.7 jit_solution(7614675460314358804)
XLA Ops:
  7.2 0.7 mul.219
  7.9 6.1 fusion.16
  14.1 0.8 copy-done
  14.9 0.1 fusion.29
  15.0 36.6 %psum.120 = f32[128]{0:T(128)S(1)} all-reduce(f32[128]{0:T(128)S(1)} %fusion.29), channel_id=1, replica_groups=mesh['section'=4,'dp'=16,'mp'=2] {'dp'}, use_global_device_ids=true, to_apply=%region_2.3 | all-reduce | flops 128 | bytes 1024 | tf_op jit(solution)/shard_map/psum | solution.py:39
  51.6 64.8 %all-reduce.11.cloned.1.call-done = f32[128,7168]{1,0:T(8,128)} async-done(((f32[128,7168]{1,0:T(8,128)}), f32[128,7168]{1,0:T(8,128)}) %all-reduce.11.cloned.1.call-update) | async-done | bytes 3670032 | tf_op jit(solution)/shard_map/psum | solution.py:39
  116.5 6.3 fusion.8
  122.8 0.7 fusion.61
  123.5 23.3 %all-reduce.13.cloned.1.call-done = f32[128,512]{1,0:T(8,128)} async-done(((f32[128,512]{1,0:T(8,128)}), f32[128,512]{1,0:T(8,128)}) %all-reduce.13.cloned.1.call-update) | async-done | bytes 262160 | tf_op jit(solution)/shard_map/psum | solution.py:49
  146.8 1.0 fusion.30
  147.8 3.2 collective-permute-start
  151.0 2.7 collective-permute-done
  153.7 6.0 fusion.14
  159.8 0.1 fusion.32
  159.9 34.0 %psum.123 = f32[128]{0:T(128)S(1)} all-reduce(f32[128]{0:T(128)S(1)} %fusion.32), channel_id=1, replica_groups=mesh['section'=4,'dp'=16,'mp'=2] {'dp'}, use_global_device_ids=true, to_apply=%region_6.7 | all-reduce | flops 128 | bytes 1024 | tf_op jit(solution)/shard_map/psum | solution.py:39
  193.9 67.7 %all-reduce.15.cloned.1.call-done = f32[128,7168]{1,0:T(8,128)} async-done(((f32[128,7168]{1,0:T(8,128)}), f32[128,7168]{1,0:T(8,128)}) %all-reduce.15.cloned.1.call-update) | async-done | bytes 3670032 | tf_op jit(solution)/shard_map/psum | solution.py:39
  261.6 6.3 fusion.6
  268.0 23.9 %all-reduce.17.cloned.1.call-done = f32[128,512]{1,0:T(8,128)} async-done(((f32[128,512]{1,0:T(8,128)}), f32[128,512]{1,0:T(8,128)}) %all-reduce.17.cloned.1.call-update) | async-done | bytes 262160 | tf_op jit(solution)/shard_map/psum | solution.py:49
  291.9 1.0 fusion.33
  293.0 3.2 collective-permute-start.1
  296.2 2.7 collective-permute-done.1
  298.9 6.0 fusion.12
  305.0 0.1 fusion.35
  305.1 34.0 %psum.126 = f32[128]{0:T(128)S(1)} all-reduce(f32[128]{0:T(128)S(1)} %fusion.35), channel_id=1, replica_groups=mesh['section'=4,'dp'=16,'mp'=2] {'dp'}, use_global_device_ids=true, to_apply=%region_10.11 | all-reduce | flops 128 | bytes 1024 | tf_op jit(solution)/shard_map/psum | solution.py:39
  339.1 67.7 %all-reduce.19.cloned.1.call-done = f32[128,7168]{1,0:T(8,128)} async-done(((f32[128,7168]{1,0:T(8,128)}), f32[128,7168]{1,0:T(8,128)}) %all-reduce.19.cloned.1.call-update) | async-done | bytes 3670032 | tf_op jit(solution)/shard_map/psum | solution.py:39
  406.7 6.3 fusion.4
  413.1 24.0 %all-reduce.21.cloned.1.call-done = f32[128,512]{1,0:T(8,128)} async-done(((f32[128,512]{1,0:T(8,128)}), f32[128,512]{1,0:T(8,128)}) %all-reduce.21.cloned.1.call-update) | async-done | bytes 262160 | tf_op jit(solution)/shard_map/psum | solution.py:49
  437.1 1.0 fusion.36
  438.1 3.2 collective-permute-start.2
  441.3 2.7 collective-permute-done.2
  444.0 6.0 fusion.10
  450.1 0.6 copy-done.2
  450.8 0.1 fusion.38
  451.0 33.9 %psum.129 = f32[128]{0:T(128)S(1)} all-reduce(f32[128]{0:T(128)S(1)} %fusion.38), channel_id=1, replica_groups=mesh['section'=4,'dp'=16,'mp'=2] {'dp'}, use_global_device_ids=true, to_apply=%region_14.15 | all-reduce | flops 128 | bytes 1024 | tf_op jit(solution)/shard_map/psum | solution.py:39
  484.9 67.0 %all-reduce.23.cloned.1.call-done = f32[128,7168]{1,0:T(8,128)} async-done(((f32[128,7168]{1,0:T(8,128)}), f32[128,7168]{1,0:T(8,128)}) %all-reduce.23.cloned.1.call-update) | async-done | bytes 3670032 | tf_op jit(solution)/shard_map/psum | solution.py:39
  551.9 6.3 fusion.2
  558.2 0.2 all-reduce.27.cloned.1.call-start
  558.5 0.1 reshape.129
  558.6 23.6 %all-reduce.25.cloned.1.call-done = f32[128,512]{1,0:T(8,128)} async-done(((f32[128,512]{1,0:T(8,128)}), f32[128,512]{1,0:T(8,128)}) %all-reduce.25.cloned.1.call-update) | async-done | bytes 262160 | tf_op jit(solution)/shard_map/psum | solution.py:49
  582.2 1.1 fusion.44
  583.3 0.6 gather_fusion
  583.9 0.8 gather_fusion.1
  584.8 0.7 select_bitcast_fusion
  585.6 9.9 %all_gather.6 = bf16[128,512]{1,0:T(8,128)(2,1)S(1)} all-gather(bf16[32,512]{1,0:T(8,128)(2,1)S(1)} %broadcast_select_fusion), channel_id=1, replica_groups=mesh['section'=4,'dp'=16,'mp'=2] {'section'}, dimensions={0}, use_global_device_ids=true | all-gather | bytes 163840 | tf_op jit(solution)/shard_map/all_gather | solution.py:55
  595.6 30.1 %all-reduce.27.cloned.1.call-done = bf16[128,1,512]{2,0,1:T(8,128)(2,1)} async-done(((bf16[128,1,512]{2,0,1:T(8,128)(2,1)}), bf16[128,1,512]{2,0,1:T(8,128)(2,1)}) %all-reduce.27.cloned.1.call-update) | async-done | bytes 131088 | tf_op jit(solution)/shard_map/psum | solution.py:22
  625.6 9.0 %fusion = f32[128,2,8192]{2,0,1:T(8,128)} fusion(bf16[512,8192]{1,0:T(8,128)(2,1)} %param.16, f32[512]{0:T(512)S(1)} %convert_element_type.109, bf16[128,1,512]{2,0,1:T(8,128)(2,1)} %all-reduce.27.cloned.1.call-done, bf16[128,1,512]{2,0,1:T(8,128)(2,1)S(1)} %bitcast.71), kind=kOutput, calls=%fused_computation.2 | convolution fusion | flops 2148007936 | bytes 17041408 | tf_op jit(solution)/shard_map/rkd,dv->rkv/dot_general | solution.py:70
  634.7 0.6 copy-done.5
  635.4 0.1 reshape.133
  635.5 0.1 copy-done.1
  635.6 0.1 fusion.27
  635.7 33.8 %psum.132 = f32[128,2]{0,1:T(2,128)S(1)} all-reduce(f32[128,2]{0,1:T(2,128)S(1)} %fusion.27), channel_id=1, replica_groups=mesh['section'=4,'dp'=16,'mp'=2] {'dp'}, use_global_device_ids=true, to_apply=%region_19.20 | all-reduce | flops 256 | bytes 2048 | tf_op jit(solution)/shard_map/psum | solution.py:65
  669.5 51.5 %reduce-scatter.3.cloned.1.call-done = f32[8,2,8192]{2,0,1:T(8,128)} async-done(((f32[128,2,8192]{2,0,1:T(8,128)}), f32[8,2,8192]{2,0,1:T(8,128)}) %reduce-scatter.3.cloned.1.call-update) | async-done | bytes 524304 | tf_op jit(solution)/shard_map/reduce_scatter | solution.py:69
  721.0 1.3 fusion.73
  722.3 13.6 %pmax.7 = f32[8,2]{0,1:T(2,128)S(1)} all-reduce(f32[8,2]{0,1:T(2,128)S(1)} %get-tuple-element.9), channel_id=1, replica_groups=mesh['section'=4,'dp'=16,'mp'=2] {'section','mp'}, use_global_device_ids=true, to_apply=%region_21.22 | all-reduce | flops 16 | bytes 128 | tf_op jit(solution)/shard_map/pmax | solution.py:81
  735.9 0.3 fusion.72
  736.2 0.2 fusion.42
  736.4 13.3 %all-reduce = (f32[8,2]{0,1:T(2,128)S(1)}, f32[8]{0:T(128)S(1)}) all-reduce(f32[8,2]{0,1:T(2,128)S(1)} %get-tuple-element.7, f32[8]{0:T(128)S(1)} %fusion.42), channel_id=1, replica_groups=mesh['section'=4,'dp'=16,'mp'=2] {'section','mp'}, use_global_device_ids=true, to_apply=%region_23.24 | all-reduce | flops 24 | bytes 192 | tf_op jit(solution)/shard_map/psum | solution.py:83
  749.8 0.8 multiply_convert_fusion.8
  750.7 0.1 reshape.131
  750.8 41.1 %all-gather.2.cloned.1.call-done = bf16[128,8192]{1,0:T(8,128)(2,1)} async-done(((bf16[8,8192]{1,0:T(8,128)(2,1)}), bf16[128,8192]{1,0:T(8,128)(2,1)}) %all-gather.2.cloned.1.call-update) | async-done | bytes 2097168 | tf_op jit(solution)/shard_map/all_gather | solution.py:98
  791.9 7.6 convolution_convert_fusion
  799.6 0.2 fusion.53
  799.9 31.5 %psum.135 = f32[4,16]{1,0:T(4,128)} all-reduce(f32[4,16]{1,0:T(4,128)S(1)} %fusion.53), channel_id=1, replica_groups=mesh['section'=4,'dp'=16,'mp'=2] {'dp'}, use_global_device_ids=true, to_apply=%region_27.28 | all-reduce | flops 64 | bytes 512 | tf_op jit(solution)/shard_map/psum | solution.py:97
  831.4 1.4 convert_multiply_fusion.10
  (57 shorter events, 1.3 us)
Async XLA Ops:
  7.2 109.3 %all-reduce.11.cloned.1.call-start = ((), (), s32[]{:S(2)}) async-start(), calls=%async_computation.2 | async-start | bytes 7340032 | tf_op jit(solution)/shard_map/psum | solution.py:39
  14.0 0.9 copy-start
  14.0 132.7 %all-reduce.13.cloned.1.call-start = ((), (), s32[]{:S(2)}) async-start(), calls=%async_computation.3 | async-start | bytes 524288 | tf_op jit(solution)/shard_map/psum | solution.py:49
  122.8 138.8 %all-reduce.15.cloned.1.call-start = ((), (), s32[]{:S(2)}) async-start(), calls=%async_computation.4 | async-start | bytes 7340032 | tf_op jit(solution)/shard_map/psum | solution.py:39
  147.8 5.9 collective-permute-start
  159.8 132.2 %all-reduce.17.cloned.1.call-start = ((), (), s32[]{:S(2)}) async-start(), calls=%async_computation.5 | async-start | bytes 524288 | tf_op jit(solution)/shard_map/psum | solution.py:49
  267.9 138.8 %all-reduce.19.cloned.1.call-start = ((), (), s32[]{:S(2)}) async-start(), calls=%async_computation.6 | async-start | bytes 7340032 | tf_op jit(solution)/shard_map/psum | solution.py:39
  293.0 5.9 collective-permute-start.1
  304.9 132.1 %all-reduce.21.cloned.1.call-start = ((), (), s32[]{:S(2)}) async-start(), calls=%async_computation.7 | async-start | bytes 524288 | tf_op jit(solution)/shard_map/psum | solution.py:49
  413.1 138.8 %all-reduce.23.cloned.1.call-start = ((), (), s32[]{:S(2)}) async-start(), calls=%async_computation.8 | async-start | bytes 7340032 | tf_op jit(solution)/shard_map/psum | solution.py:39
  438.1 5.9 collective-permute-start.2
  450.0 0.7 copy-start.2
  450.1 132.2 %all-reduce.25.cloned.1.call-start = ((), (), s32[]{:S(2)}) async-start(), calls=%async_computation.9 | async-start | bytes 524288 | tf_op jit(solution)/shard_map/psum | solution.py:49
  484.9 73.7 %copy-start.4 = (bf16[512]{0:T(512)(128)(2,1)S(1)}, bf16[512]{0:T(512)(128)(2,1)}, u32[]{:S(2)}) copy-start(bf16[512]{0:T(512)(128)(2,1)} %param.15) | copy-start | bytes 3076
  558.2 67.4 %all-reduce.27.cloned.1.call-start = ((), (), s32[]{:S(2)}) async-start(), calls=%async_computation.10 | async-start | bytes 262144 | tf_op jit(solution)/shard_map/psum | solution.py:22
  585.5 135.5 %reduce-scatter.3.cloned.1.call-start = ((), (), s32[]{:S(2)}) async-start(), calls=%async_computation.11 | async-start | bytes 8912896 | tf_op jit(solution)/shard_map/reduce_scatter | solution.py:69
  634.6 0.7 copy-start.5
  634.7 0.9 copy-start.1
  634.7 116.0 %copy-start.3 = (s32[4,32]{1,0:T(4,128)S(1)}, s32[4,32]{1,0:T(4,128)}, u32[]{:S(2)}) copy-start(s32[4,32]{1,0:T(4,128)} %param.19) | copy-start | bytes 1540
  634.7 157.2 %all-gather.2.cloned.1.call-start = ((), (), s32[]{:S(2)}) async-start(), calls=%async_computation.12 | async-start | bytes 2228224 | tf_op jit(solution)/shard_map/all_gather | solution.py:98
  749.8 49.9 %copy-start.6 = (f32[8]{0:T(128)}, f32[8]{0:T(128)S(1)}, u32[]{:S(2)}) copy-start(f32[8]{0:T(128)S(1)} %get-tuple-element.5) | copy-start | bytes 100
  750.6 80.8 %reduce-scatter.5.cloned.1.call-start = ((), (), s32[]{:S(2)}) async-start(), calls=%async_computation.13 | async-start | bytes 147456 | tf_op jit(solution)/shard_map/reduce_scatter | solution.py:101
Sparse Core Ops, SparseCore 0:
  14.2 102.2 all-reduce.10
  122.9 23.8 all-reduce.12
  159.9 101.6 all-reduce.14
  268.1 23.8 all-reduce.16
  305.0 101.6 all-reduce.18
  413.2 23.8 all-reduce.20
  450.2 101.6 all-reduce.22
  558.3 23.8 all-reduce.24
  585.6 39.9 all-reduce.26
  634.8 86.1 reduce-scatter.2
  750.7 41.1 all-gather.1
  799.7 28.0 reduce-scatter.4
where the time goes:
time: 848 us; the launch traced here: 840 us
  waiting for transfers between devices  493 us (58%)
  blocking collectives  241 us (28%)
  matrix products  66.3 us (8%)
  between operations  14.4 us (2%)
  other arithmetic  11.1 us (1%)
  starting transfers between devices  10.3 us (1%)
    psum x4, waiting for transfers between devices, shards(): lax.psum((jnp.sum(wide * wide, axis=-1), jnp.dot(normed, up_local, prefer...  267 us
    psum x4, blocking collectives, shards(): lax.psum((jnp.sum(wide * wide, axis=-1), jnp.dot(normed, up_local, prefer...  138 us
    psum x4, waiting for transfers between devices, shards(): lowered = lax.psum(partial_down, 'mp')  94.8 us
    reduce_scatter x1, waiting for transfers between devices, shards(): lax.psum_scatter(jnp.einsum('rkd,dv->rkv', part, w_head, preferred_elemen...  51.5 us
    all_gather x1, waiting for transfers between devices, shards(): gaps = lax.all_gather(gap, 'dp', axis=0, tiled=True)  41.1 us
    psum x1, blocking collectives, shards(): squares = lax.psum(squares_part, 'dp')  33.8 us
    psum x1, blocking collectives, shards(): histogram = lax.psum(hist_part, 'dp')  31.5 us
    psum x1, waiting for transfers between devices, broadcast(): return lax.psum(jnp.where(mine, value, jnp.zeros_like(value)), axis)  30.1 us
  transfers between devices with their start and end apart: 15, of which 14 were waited for; matrix products, arithmetic and copies ran while one was open for 0% of the time, Pallas kernels for 0%

commit v1 on v0

v1 whole, which is shorter than its diff:
```python
import jax
import jax.numpy as jnp
from jax import lax
from jax.experimental import pallas as pl
from jax.experimental.pallas import tpu as pltpu
from jax.sharding import PartitionSpec as P

D = 8192
XS = 32
NB = 16
LIVE = 80
DP = 16
PAIRS = LIVE // DP
HALF = LIVE // 2
FB = 896
NF = 8
COLS = 8192
TILES = COLS // 128
EPS = 1e-05
f32 = jnp.float32
bf16 = jnp.bfloat16
VMEM_LIMIT = 56 * 1024 * 1024


def call(kernel, out_shape, **kw):
    return pl.pallas_call(
        kernel,
        out_shape=out_shape,
        compiler_params=pltpu.CompilerParams(vmem_limit_bytes=VMEM_LIMIT),
        **kw,
    )


def iota(shape, dim):
    return lax.broadcasted_iota(jnp.int32, shape, dim)


def split_sum(column):
    high = column.astype(bf16).astype(f32)
    return high, (column - high).astype(bf16).astype(f32)


def prep_kernel(count, index, keep, tokens, rows, kept, section, slots):
    lane = iota((1, 4 * XS), 1)
    own = lane // XS
    place = lane % XS
    start = jnp.int32(0)
    position = jnp.full((1, 4 * XS), -1, jnp.int32)
    for s in range(4):
        inside = (own == s) & (place < count[s])
        position = jnp.where(inside, place + start, position)
        start = start + count[s]
    hit = iota((LIVE, 4 * XS), 0) == position
    pick = jnp.where(hit, 1.0, 0.0)
    token = jnp.sum(pick * index[...].astype(f32), axis=1, keepdims=True).astype(jnp.int32)
    chosen = jnp.where(iota((LIVE, 128), 1) == token, 1.0, 0.0)
    rows[...] = jnp.dot(chosen.astype(bf16), tokens[...], preferred_element_type=f32).astype(bf16)
    flag = jnp.sum(chosen * keep[...].astype(f32), axis=1, keepdims=True)
    kept[...] = jnp.broadcast_to(flag, kept.shape)
    which = jnp.sum(pick * own.astype(f32), axis=1, keepdims=True)
    section[...] = jnp.broadcast_to(which, section.shape)
    slots[...] = pick


def up_kernel(state, gain, weight, out):
    wide = state[...].astype(f32)
    normed = (wide * gain[...].astype(f32)).astype(bf16)
    high, low = split_sum(jnp.sum(wide * wide, axis=1, keepdims=True))
    lane = iota((LIVE, 128), 1)
    extra = jnp.where(lane == 0, high, jnp.where(lane == 1, low, 0.0))
    part = jnp.dot(normed, weight[...], preferred_element_type=f32)
    for t in range(2):
        out[t, 0, :, :FB] = part[t * HALF : (t + 1) * HALF].astype(bf16)
        out[t, 0, :, FB:] = extra[t * HALF : (t + 1) * HALF].astype(bf16)


def mid_kernel(parts, out):
    total = parts[0].astype(f32)
    for j in range(1, DP):
        total = total + parts[j].astype(f32)
    scale = lax.rsqrt((total[:, FB : FB + 1] + total[:, FB + 1 : FB + 2]) / D + EPS)
    active = jax.nn.silu(total[:, :FB] * scale).astype(bf16)
    for j in range(DP):
        out[j] = active


def down_kernel(active, weight, kept, out):
    step = pl.program_id(0)
    both = jnp.concatenate([active[0, 0].astype(f32), active[1, 0].astype(f32)], axis=0)
    part = jnp.dot(both.astype(bf16), weight[...], preferred_element_type=f32)

    @pl.when(step == 0)
    def _():
        out[...] = part

    @pl.when(step > 0)
    def _():
        out[...] = out[...] + part

    @pl.when(step == NF - 1)
    def _():
        out[...] = out[...] * kept[:, :1]


def head_kernel(exits, finals, gain, weight, out):
    step = pl.program_id(0)
    wide = jnp.concatenate([exits[...].astype(f32), finals[...].astype(f32)], axis=0)
    headed = (wide * gain[...].astype(f32)).astype(bf16)
    part = jnp.dot(headed, weight[...], preferred_element_type=f32)
    tiles = part.reshape(2 * LIVE, 8, 128)
    base = pl.multiple_of(step * 8, 8)
    for i in range(DP):
        for kind in range(2):
            for p in range(PAIRS):
                slot = kind * PAIRS + p
                out[i, pl.ds(slot * TILES + base, 8), :] = tiles[kind * LIVE + i * PAIRS + p]

    @pl.when(step == 0)
    def _():
        squares = jnp.broadcast_to(jnp.sum(wide * wide, axis=1, keepdims=True), (2 * LIVE, 128))
        for i in range(DP):
            for kind in range(2):
                at = kind * LIVE + i * PAIRS
                first = 2 * PAIRS * TILES + kind * 8
                out[i, first : first + PAIRS, :] = squares[at : at + PAIRS]
                out[i, first + PAIRS : first + 8, :] = jnp.zeros((8 - PAIRS, 128), f32)


def peak_kernel(parts, logits, stats, total):
    step = pl.program_id(0)

    @pl.when(step == 0)
    def _():
        total[...] = parts[0]

    @pl.when(step > 0)
    def _():
        total[...] = total[...] + parts[0]

    @pl.when(step == DP - 1)
    def _():
        lane = iota((1, 128), 1)
        for p in range(PAIRS):
            z = []
            for kind in range(2):
                at = 2 * PAIRS * TILES + kind * 8 + p
                scale = lax.rsqrt(total[at : at + 1, :] / D + EPS)
                first = (kind * PAIRS + p) * TILES
                value = total[first : first + TILES, :] * scale
                logits[first : first + TILES, :] = value
                z.append(value)
                if kind == 0:
                    exit_scale = scale
            entries = []
            for value in z:
                peak = jnp.max(jnp.max(value, axis=0, keepdims=True), axis=1, keepdims=True)
                power = jnp.exp(value - peak)
                entries += [peak, jnp.sum(jnp.sum(power, axis=0, keepdims=True), axis=1, keepdims=True)]
            cross = power * (z[1] - z[0])
            entries.append(jnp.sum(jnp.sum(cross, axis=0, keepdims=True), axis=1, keepdims=True))
            entries.append(exit_scale)
            row = jnp.zeros((1, 128), f32)
            for n, entry in enumerate(entries):
                row = jnp.where(lane == n, entry, row)
            for j in range(8):
                stats[j, p : p + 1, :] = row
        for j in range(8):
            stats[j, PAIRS:, :] = jnp.ones((8 - PAIRS, 128), f32)


def gap_kernel(logits, stats, out):
    everyone = stats[...]
    lane = iota((1, 128), 1)
    peaks = jnp.max(everyone, axis=0)
    marks = []
    for column in (0, 2):
        peak = peaks[:, column : column + 1]
        weight = jnp.exp(everyone[:, :, column : column + 1] - peak[None])
        total = jnp.sum(weight * everyone[:, :, column + 1 : column + 2], axis=0)
        marks.append((peak + jnp.log(total), weight, total))
    (log_exit, _, _), (log_final, weight, total) = marks
    cross = jnp.sum(weight * everyone[:, :, 4:5], axis=0)
    kl = cross / total - log_final + log_exit
    exit_scale = peaks[:, 5:6]
    for p in range(PAIRS):
        ze = logits[p * TILES : (p + 1) * TILES, :]
        zf = logits[(PAIRS + p) * TILES : (PAIRS + p + 1) * TILES, :]
        gap = jnp.exp(ze - log_exit[p : p + 1]) - jnp.exp(zf - log_final[p : p + 1])
        gap = (gap * exit_scale[p : p + 1]).astype(bf16)
        for j in range(DP):
            out[j, p * TILES : (p + 1) * TILES, :] = gap
    high, rest = split_sum(kl)
    middle = (kl - high).astype(bf16).astype(f32)
    low = kl - high - middle
    lanes = iota((8, 128), 1)
    carried = jnp.where(lanes == 0, high, jnp.where(lanes == 1, middle, jnp.where(lanes == 2, low, 0.0)))
    extra = jnp.concatenate([carried, jnp.zeros((8, 128), f32)], axis=0).astype(bf16)
    for j in range(DP):
        out[j, PAIRS * TILES :, :] = extra


def grad_kernel(gaps, weight, slots, buckets, out, kl_out, hist, total):
    step = pl.program_id(0)
    base = pl.multiple_of(step * 16, 16)
    rows = [gaps[:, pl.ds(p * TILES + base, 16), :].astype(f32) for p in range(PAIRS)]
    left = jnp.stack(rows, axis=1).reshape(LIVE, 16 * 128).astype(bf16)
    part = lax.dot_general(left, weight[...], (((1,), (1,)), ((), ())), preferred_element_type=f32)

    @pl.when(step == 0)
    def _():
        total[...] = part

    @pl.when(step > 0)
    def _():
        total[...] = total[...] + part

    @pl.when(step == 3)
    def _():
        pick = slots[...]
        out[...] = lax.dot_general(
            pick.astype(bf16),
            total[...].astype(bf16),
            (((0,), (0,)), ((), ())),
            preferred_element_type=f32,
        ).astype(bf16)
        extra = gaps[:, PAIRS * TILES :, :].astype(f32)[:, :PAIRS, :].reshape(LIVE, 128)
        kl = jnp.sum(extra, axis=1, keepdims=True)
        by_slot = jnp.sum(pick * kl, axis=0, keepdims=True)
        kl_out[...] = jnp.broadcast_to(by_slot, (8, 128))
        mine = jnp.where(iota((8, 128), 1) // XS == iota((8, 128), 0), by_slot, 0.0)
        hot = jnp.where(iota((NB, 128), 0) == buckets[...], 1.0, 0.0)
        hist[...] = lax.dot_general(
            mine,
            hot,
            (((1,), (1,)), ((), ())),
            preferred_element_type=f32,
            precision=lax.Precision.HIGHEST,
        )


def exchange(value, axis):
    return lax.all_to_all(value, axis, 0, 0)


def shards(
    tokens, keep, norm_gain, w_up, w_down, head_gain, w_head, exit_idx, exit_count, kl_bucket
):
    sections = lax.axis_size("section")
    section_id = lax.axis_index("section")
    up_local = w_up[0]
    down_local = w_down[0]
    keep_mine = lax.dynamic_slice_in_dim(keep, section_id, 1, 0)
    shape = jax.ShapeDtypeStruct
    vmem = pl.BlockSpec(memory_space=pltpu.VMEM)
    current, kept, section_of, slots = call(
        prep_kernel,
        (
            shape((LIVE, 512), bf16),
            shape((LIVE, 128), f32),
            shape((LIVE, 128), f32),
            shape((LIVE, 128), f32),
        ),
        in_specs=[pl.BlockSpec(memory_space=pltpu.SMEM), vmem, vmem, vmem],
        out_specs=[vmem] * 4,
    )(exit_count, exit_idx.reshape(1, -1), keep_mine, tokens)
    mine = current
    for step in range(sections):
        parts = call(
            up_kernel,
            shape((2, NF, HALF, FB + 128), bf16),
            grid=(NF,),
            in_specs=[
                pl.BlockSpec((LIVE, 512), lambda f: (0, 0)),
                pl.BlockSpec((1, 512), lambda f: (0, 0)),
                pl.BlockSpec((512, FB), lambda f: (0, f)),
            ],
            out_specs=pl.BlockSpec((2, 1, HALF, FB + 128), lambda f: (0, f, 0, 0)),
        )(current, norm_gain, up_local)
        parts = exchange(parts.reshape(DP, HALF, FB + 128), "dp")
        active = call(
            mid_kernel, shape((DP, HALF, FB), bf16), in_specs=[vmem], out_specs=vmem
        )(parts)
        active = exchange(active, "dp")
        lowered = call(
            down_kernel,
            shape((LIVE, 512), f32),
            grid=(NF,),
            in_specs=[
                pl.BlockSpec((2, 1, HALF, FB), lambda f: (0, f, 0, 0)),
                pl.BlockSpec((FB, 512), lambda f: (f, 0)),
                pl.BlockSpec((LIVE, 128), lambda f: (0, 0)),
            ],
            out_specs=pl.BlockSpec((LIVE, 512), lambda f: (0, 0)),
        )(active.reshape(2, NF, HALF, FB), down_local, kept)
        other = lax.ppermute(lowered, "mp", [(0, 1), (1, 0)])
        result = (current.astype(f32) + (lowered + other)).astype(bf16)
        mine = jnp.where(section_id == step, result, mine)
        if step < sections - 1:
            current = lax.ppermute(result, "section", [(i, i + 1) for i in range(sections - 1)])
    zero = jnp.zeros_like(mine)
    own_exit = jnp.where(section_of[:, :1] == section_id.astype(f32), mine, zero)
    own_final = jnp.where(section_id == sections - 1, mine, zero)
    held = jnp.stack([own_exit, own_final])
    spread = held
    for k in range(1, sections):
        spread = spread + lax.ppermute(held, "section", [(i, (i + k) % sections) for i in range(sections)])
    extent = 2 * PAIRS * TILES + 16
    parts = call(
        head_kernel,
        shape((DP, extent, 128), f32),
        grid=(8,),
        in_specs=[
            pl.BlockSpec((LIVE, 512), lambda k: (0, 0)),
            pl.BlockSpec((LIVE, 512), lambda k: (0, 0)),
            pl.BlockSpec((1, 512), lambda k: (0, 0)),
            pl.BlockSpec((512, 1024), lambda k: (0, k)),
        ],
        out_specs=pl.BlockSpec((DP, extent, 128), lambda k: (0, 0, 0)),
    )(spread[0], spread[1], head_gain.reshape(1, -1), w_head)
    parts = exchange(parts, "dp")
    logits, stats = call(
        peak_kernel,
        (shape((2 * PAIRS * TILES, 128), f32), shape((8, 8, 128), f32)),
        grid=(DP,),
        in_specs=[pl.BlockSpec((1, extent, 128), lambda j: (j, 0, 0))],
        out_specs=[
            pl.BlockSpec((2 * PAIRS * TILES, 128), lambda j: (0, 0)),
            pl.BlockSpec((8, 8, 128), lambda j: (0, 0, 0)),
        ],
        scratch_shapes=[pltpu.VMEM((extent, 128), f32)],
    )(parts)
    stats = exchange(stats, ("section", "mp"))
    extent = PAIRS * TILES + 16
    gaps = call(
        gap_kernel, shape((DP, extent, 128), bf16), in_specs=[vmem] * 2, out_specs=vmem
    )(logits, stats)
    gaps = exchange(gaps, "dp")
    feature, kl, hist = call(
        grad_kernel,
        (shape((128, 512), bf16), shape((8, 128), f32), shape((8, NB), f32)),
        grid=(4,),
        in_specs=[
            pl.BlockSpec((DP, extent, 128), lambda k: (0, 0, 0)),
            pl.BlockSpec((512, 2048), lambda k: (0, k)),
            pl.BlockSpec((LIVE, 128), lambda k: (0, 0)),
            pl.BlockSpec((1, 128), lambda k: (0, 0)),
        ],
        out_specs=[
            pl.BlockSpec((128, 512), lambda k: (0, 0)),
            pl.BlockSpec((8, 128), lambda k: (0, 0)),
            pl.BlockSpec((8, NB), lambda k: (0, 0)),
        ],
        scratch_shapes=[pltpu.VMEM((LIVE, 512), f32)],
    )(gaps, w_head, slots, kl_bucket.reshape(1, -1))
    feature = exchange(feature.reshape(8, 16, 512), ("section", "mp"))
    feature_grad = jnp.sum(feature.astype(f32), axis=0)
    kl_here = lax.dynamic_slice_in_dim(kl[0], lax.axis_index("dp") * 8, 8, 0)
    return (feature_grad, kl_here, hist[:4])


def solution(mesh):
    return jax.shard_map(
        shards,
        mesh=mesh,
        in_specs=(
            P(None, "dp"),
            P(),
            P("section", "dp"),
            P("section", "dp", "mp"),
            P("section", "mp", "dp"),
            P("dp"),
            P("dp", ("section", "mp")),
            P(),
            P(),
            P(),
        ),
        out_specs=(P(("section", "mp"), "dp"), P("dp"), P()),
        check_vma=False,
    )
```

time: 848 us -> 454 us (0.54)
  waiting for transfers between devices: 493 us -> 37.9 us
  Pallas kernels: 0 us -> 102 us
  matrix products: 66.3 us -> 0 us
  starting transfers between devices: 10.3 us -> 38.1 us
  blocking collectives: 241 us -> 259 us
  between operations: 14.4 us -> 0.75 us
    psum x9 -> x0, waiting for transfers between devices: 392 us -> none  [the longest x4 267 us: shards(): lax.psum((jnp.sum(wide * wide, axis=-1), jnp.dot(normed, up_local, prefer...]
    all_to_all x0 -> x10, blocking collectives: none -> 259 us  [exchange(): return lax.all_to_all(value, axis, 0, 0)]
    psum x7 -> x0, blocking collectives: 217 us -> none  [the longest x4 138 us: shards(): lax.psum((jnp.sum(wide * wide, axis=-1), jnp.dot(normed, up_local, prefer...]
    pallas_call x0 -> x17, Pallas kernels: none -> 102 us  [the longest x4 30.4 us: shards(): call(up_kernel, shape((2, NF, HALF, FB + 128), bf16), grid=(NF,), in_spec...]
    dot_general x11 -> x0, matrix products: 66.3 us -> none  [the longest x4 25.2 us: shards(): jnp.dot(active, down_local, preferred_element_type=jnp.float32)]
    reduce_scatter x2 -> x0, waiting for transfers between devices: 51.5 us -> none  [the longest x1 51.5 us: shards(): lax.psum_scatter(jnp.einsum('rkd,dv->rkv', part, w_head, preferred_elemen...]
    all_gather x1 -> x0, waiting for transfers between devices: 41.1 us -> none  [shards(): gaps = lax.all_gather(gap, 'dp', axis=0, tiled=True)]
    all_to_all x0 -> x2, waiting for transfers between devices: none -> 23 us  [exchange(): return lax.all_to_all(value, axis, 0, 0)]
  transfers between devices with their start and end apart: 15 -> 12, of which waited for: 14 -> 11; matrix products, arithmetic and copies ran while one was open for 0% -> 1% of each run, Pallas kernels for 0% -> 0%
where the time goes in v1:
time: 454 us; the launch traced here: 451 us
  blocking collectives  259 us (57%)
  Pallas kernels  102 us (22%)
  starting transfers between devices  38.1 us (8%)
  waiting for transfers between devices  37.9 us (8%)
  local copies, waits for them, and re-layouts  9.19 us (2%)
  other arithmetic  4.67 us (1%)
    all_to_all x10, blocking collectives, exchange(): return lax.all_to_all(value, axis, 0, 0)  259 us
    pallas_call x4, Pallas kernels, shards(): call(up_kernel, shape((2, NF, HALF, FB + 128), bf16), grid=(NF,), in_spec...  30.4 us
    pallas_call x4, Pallas kernels, shards(): call(down_kernel, shape((LIVE, 512), f32), grid=(NF,), in_specs=[pl.Block...  30.2 us
    all_to_all x2, waiting for transfers between devices, exchange(): return lax.all_to_all(value, axis, 0, 0)  23 us
    ppermute x4, starting transfers between devices, shards(): other = lax.ppermute(lowered, 'mp', [(0, 1), (1, 0)])  11.6 us
    ppermute x3, starting transfers between devices, shards(): lax.ppermute(result, 'section', [(i, i + 1) for i in range(sections - 1)])  11.3 us
    pallas_call x4, Pallas kernels, shards(): call(mid_kernel, shape((DP, HALF, FB), bf16), in_specs=[vmem], out_specs=...  10.8 us
    pallas_call x1, Pallas kernels, shards(): call(head_kernel, shape((DP, extent, 128), f32), grid=(8,), in_specs=[pl....  9.61 us
  transfers between devices with their start and end apart: 12, of which 11 were waited for; matrix products, arithmetic and copies ran while one was open for 1% of the time, Pallas kernels for 0%

profile of v1, /device:TPU:1, one launch (start us, length us, event | category | flops | bytes accessed | tf_op | source)
XLA Modules:
  0.0 451.1 jit_solution(17350273889830133752)
XLA Ops:
  0.7 1.3 reshape.43.index
  2.4 1.8 shard_map.121
  4.3 7.6 %shard_map.122 = bf16[2,8,40,1024]{3,2,1,0:T(8,128)(2,1)} custom-call(bf16[80,512]{1,0:T(8,128)(2,1)} %get-tuple-element.13.state, bf16[1,512]{1,0:T(2,128)(2,1)} %gain.7, bf16[512,7168]{1,0:T(8,128)(2,1)} %bitcast.25), custom_call_target="tpu_custom_call" | custom-call | tf_op jit(solution)/shard_map/pallas_call | solution.py:268
  11.9 27.8 %all_to_all.60.parts = bf16[16,40,1024]{2,1,0:T(8,128)(2,1)} all-to-all(bf16[16,40,1024]{2,1,0:T(8,128)(2,1)} %bitcast.29), channel_id=1, replica_groups=mesh['section'=4,'dp'=16,'mp'=2] {'dp'}, dimensions={0} | all-to-all | bytes 2621440 | tf_op jit(solution)/shard_map/all_to_all | solution.py:242
  39.7 2.7 shard_map.123
  42.4 21.0 %all_to_all.61 = bf16[16,40,896]{2,1,0:T(8,128)(2,1)} all-to-all(bf16[16,40,896]{2,1,0:T(8,128)(2,1)} %shard_map.123), channel_id=1, replica_groups=mesh['section'=4,'dp'=16,'mp'=2] {'dp'}, dimensions={0} | all-to-all | bytes 2293760 | tf_op jit(solution)/shard_map/all_to_all | solution.py:242
  63.3 7.5 %shard_map.124 = f32[80,512]{1,0:T(8,128)} custom-call(bf16[2,8,40,896]{3,2,1,0:T(8,128)(2,1)} %bitcast.34, bf16[7168,512]{1,0:T(8,128)(2,1)} %bitcast.21, f32[80,128]{1,0:T(8,128)} %get-tuple-element.14.kept), custom_call_target="tpu_custom_call" | custom-call | tf_op jit(solution)/shard_map/pallas_call | solution.py:284
  70.9 2.7 collective-permute-start
  73.6 1.2 collective-permute-done
  74.8 1.0 add_convert_fusion.3
  75.8 3.1 collective-permute-start.1
  78.9 1.5 collective-permute-done.1.state
  80.3 0.6 copy-done.5
  81.0 7.6 %shard_map.125 = bf16[2,8,40,1024]{3,2,1,0:T(8,128)(2,1)} custom-call(bf16[80,512]{1,0:T(8,128)(2,1)} %copy-done.5, bf16[1,512]{1,0:T(2,128)(2,1)} %gain.7, bf16[512,7168]{1,0:T(8,128)(2,1)} %bitcast.26), custom_call_target="tpu_custom_call" | custom-call | tf_op jit(solution)/shard_map/pallas_call | solution.py:268
  88.6 23.2 %all_to_all.62.parts = bf16[16,40,1024]{2,1,0:T(8,128)(2,1)} all-to-all(bf16[16,40,1024]{2,1,0:T(8,128)(2,1)} %bitcast.30), channel_id=1, replica_groups=mesh['section'=4,'dp'=16,'mp'=2] {'dp'}, dimensions={0} | all-to-all | bytes 2621440 | tf_op jit(solution)/shard_map/all_to_all | solution.py:242
  111.8 2.7 shard_map.126
  114.5 20.8 %all_to_all.63 = bf16[16,40,896]{2,1,0:T(8,128)(2,1)} all-to-all(bf16[16,40,896]{2,1,0:T(8,128)(2,1)} %shard_map.126), channel_id=1, replica_groups=mesh['section'=4,'dp'=16,'mp'=2] {'dp'}, dimensions={0} | all-to-all | bytes 2293760 | tf_op jit(solution)/shard_map/all_to_all | solution.py:242
  135.3 7.5 %shard_map.127 = f32[80,512]{1,0:T(8,128)} custom-call(bf16[2,8,40,896]{3,2,1,0:T(8,128)(2,1)} %bitcast.35, bf16[7168,512]{1,0:T(8,128)(2,1)} %bitcast.22, f32[80,128]{1,0:T(8,128)} %get-tuple-element.14.kept), custom_call_target="tpu_custom_call" | custom-call | tf_op jit(solution)/shard_map/pallas_call | solution.py:284
  142.8 3.0 collective-permute-start.2
  145.8 1.2 collective-permute-done.2
  147.1 1.0 add_convert_fusion.2
  148.0 4.1 collective-permute-start.3
  152.1 1.5 collective-permute-done.3.state
  153.6 0.6 copy-done.7
  154.2 7.6 %shard_map.128 = bf16[2,8,40,1024]{3,2,1,0:T(8,128)(2,1)} custom-call(bf16[80,512]{1,0:T(8,128)(2,1)} %copy-done.7, bf16[1,512]{1,0:T(2,128)(2,1)} %gain.7, bf16[512,7168]{1,0:T(8,128)(2,1)} %bitcast.27), custom_call_target="tpu_custom_call" | custom-call | tf_op jit(solution)/shard_map/pallas_call | solution.py:268
  161.8 23.2 %all_to_all.64.parts = bf16[16,40,1024]{2,1,0:T(8,128)(2,1)} all-to-all(bf16[16,40,1024]{2,1,0:T(8,128)(2,1)} %bitcast.31), channel_id=1, replica_groups=mesh['section'=4,'dp'=16,'mp'=2] {'dp'}, dimensions={0} | all-to-all | bytes 2621440 | tf_op jit(solution)/shard_map/all_to_all | solution.py:242
  185.0 2.7 shard_map.129
  187.7 20.8 %all_to_all.65 = bf16[16,40,896]{2,1,0:T(8,128)(2,1)} all-to-all(bf16[16,40,896]{2,1,0:T(8,128)(2,1)} %shard_map.129), channel_id=1, replica_groups=mesh['section'=4,'dp'=16,'mp'=2] {'dp'}, dimensions={0} | all-to-all | bytes 2293760 | tf_op jit(solution)/shard_map/all_to_all | solution.py:242
  208.5 7.5 %shard_map.130 = f32[80,512]{1,0:T(8,128)} custom-call(bf16[2,8,40,896]{3,2,1,0:T(8,128)(2,1)} %bitcast.36, bf16[7168,512]{1,0:T(8,128)(2,1)} %bitcast.23, f32[80,128]{1,0:T(8,128)} %get-tuple-element.14.kept), custom_call_target="tpu_custom_call" | custom-call | tf_op jit(solution)/shard_map/pallas_call | solution.py:284
  216.1 3.0 collective-permute-start.4
  219.0 1.2 collective-permute-done.4
  220.3 1.0 add_convert_fusion.1
  221.2 4.1 collective-permute-start.5
  225.3 1.5 collective-permute-done.5.state
  226.8 0.6 copy-done.3
  227.4 7.6 %shard_map.131 = bf16[2,8,40,1024]{3,2,1,0:T(8,128)(2,1)} custom-call(bf16[80,512]{1,0:T(8,128)(2,1)} %copy-done.3, bf16[1,512]{1,0:T(2,128)(2,1)} %gain.7, bf16[512,7168]{1,0:T(8,128)(2,1)} %bitcast.28), custom_call_target="tpu_custom_call" | custom-call | tf_op jit(solution)/shard_map/pallas_call | solution.py:268
  235.0 23.2 %all_to_all.66.parts = bf16[16,40,1024]{2,1,0:T(8,128)(2,1)} all-to-all(bf16[16,40,1024]{2,1,0:T(8,128)(2,1)} %bitcast.32), channel_id=1, replica_groups=mesh['section'=4,'dp'=16,'mp'=2] {'dp'}, dimensions={0} | all-to-all | bytes 2621440 | tf_op jit(solution)/shard_map/all_to_all | solution.py:242
  258.2 2.7 shard_map.132
  260.9 20.8 %all_to_all.67 = bf16[16,40,896]{2,1,0:T(8,128)(2,1)} all-to-all(bf16[16,40,896]{2,1,0:T(8,128)(2,1)} %shard_map.132), channel_id=1, replica_groups=mesh['section'=4,'dp'=16,'mp'=2] {'dp'}, dimensions={0} | all-to-all | bytes 2293760 | tf_op jit(solution)/shard_map/all_to_all | solution.py:242
  281.8 7.6 %shard_map.133 = f32[80,512]{1,0:T(8,128)} custom-call(bf16[2,8,40,896]{3,2,1,0:T(8,128)(2,1)} %bitcast.33, bf16[7168,512]{1,0:T(8,128)(2,1)} %bitcast.24, f32[80,128]{1,0:T(8,128)} %get-tuple-element.14.kept), custom_call_target="tpu_custom_call" | custom-call | tf_op jit(solution)/shard_map/pallas_call | solution.py:284
  289.3 3.0 collective-permute-start.6
  292.4 1.1 collective-permute-done.6
  293.5 1.0 select_bitcast_fusion.1
  294.6 2.2 collective-permute-start.7
  296.8 2.5 collective-permute-start.8
  299.3 1.1 collective-permute-start.9
  301.0 1.4 collective-permute-done.7
  302.4 4.4 collective-permute-done.8
  306.8 0.7 slice_bitcast_fusion
  307.5 9.6 %shard_map.134 = f32[16,656,128]{2,1,0:T(8,128)} custom-call(bf16[80,512]{1,0:T(8,128)(2,1)} %get-tuple-element.24.exits, bf16[80,512]{1,0:T(8,128)(2,1)} %get-tuple-element.23.finals, bf16[1,512]{1,0:T(2,128)(2,1)} %reshape.52.gain, bf16[512,8192]{1,0:T(8,128)(2,1)} %weight.3), custom_call_target="tpu_custom_call" | custom-call | tf_op jit(solution)/shard_map/pallas_call | solution.py:308
  317.1 66.7 %all_to_all.68.parts = f32[16,656,128]{2,1,0:T(8,128)} all-to-all(f32[16,656,128]{2,1,0:T(8,128)} %shard_map.134), channel_id=1, replica_groups=mesh['section'=4,'dp'=16,'mp'=2] {'dp'}, dimensions={0} | all-to-all | bytes 10747904 | tf_op jit(solution)/shard_map/all_to_all | solution.py:242
  383.8 9.5 %shard_map.135 = (f32[640,128]{1,0:T(8,128)}, f32[8,8,128]{2,1,0:T(8,128)}) custom-call(f32[16,656,128]{2,1,0:T(8,128)} %all_to_all.68.parts), custom_call_target="tpu_custom_call" | custom-call | tf_op jit(solution)/shard_map/pallas_call | solution.py:321
  393.2 11.2 %all_to_all.69.stats = f32[8,8,128]{2,1,0:T(8,128)} all-to-all(f32[8,8,128]{2,1,0:T(8,128)} %get-tuple-element.16), channel_id=1, replica_groups=mesh['section'=4,'dp'=16,'mp'=2] {'section','mp'}, dimensions={0} | all-to-all | bytes 65536 | tf_op jit(solution)/shard_map/all_to_all | solution.py:242
  404.5 2.4 shard_map.136
  406.8 3.8 all-to-all-start.10
  410.7 0.6 reshape.53.buckets
  411.3 20.2 %all-to-all-done.10.gaps = bf16[16,336,128]{2,1,0:T(8,128)(2,1)S(1)} async-done(((bf16[16,336,128]{2,1,0:T(8,128)(2,1)}), bf16[16,336,128]{2,1,0:T(8,128)(2,1)S(1)}, u32[]{:S(2)}, u32[]{:S(2)}) %all-to-all-start.10) | async-done | bytes 1376288 | tf_op jit(solution)/shard_map/all_to_all | solution.py:242
  431.5 1.1 copy-done.1
  432.6 7.1 %shard_map.137 = (bf16[128,512]{1,0:T(8,128)(2,1)}, f32[8,128]{1,0:T(8,128)}, f32[8,16]{1,0:T(8,128)}) custom-call(bf16[16,336,128]{2,1,0:T(8,128)(2,1)} %copy-done.1, bf16[512,8192]{1,0:T(8,128)(2,1)} %weight.3, f32[80,128]{1,0:T(8,128)} %get-tuple-element.17.slots, s32[1,128]{1,0:T(1,128)} %reshape.53.buckets), custom_call_target="tpu_custom_call" | custom-call | tf_op jit(solution)/shard_map/pallas_call | solution.py:338
  439.7 5.5 %all-to-all-start.11 = ((bf16[8,16,512]{2,1,0:T(8,128)(2,1)}), bf16[8,16,512]{2,1,0:T(8,128)(2,1)S(1)}, u32[]{:S(2)}, u32[]{:S(2)}) async-start(bf16[8,16,512]{2,1,0:T(8,128)(2,1)} %bitcast.37), calls=%async_computation.11 | async-start | bytes 262144 | tf_op jit(solution)/shard_map/all_to_all | solution.py:242
  445.1 0.7 slice.18
  445.8 1.3 slice.19
  447.7 2.8 all-to-all-done.11
  450.4 0.6 convert_reduce_fusion
  (28 shorter events, 1.9 us)
Async XLA Ops:
  0.6 1.3 copy-start
  63.3 11.5 %copy-start.2 = (bf16[80,512]{1,0:T(8,128)(2,1)S(1)}, bf16[80,512]{1,0:T(8,128)(2,1)}, u32[]{:S(2)}) copy-start(bf16[80,512]{1,0:T(8,128)(2,1)} %get-tuple-element.13.state) | copy-start | bytes 245764
  70.9 3.9 collective-permute-start
  75.8 4.6 %collective-permute-start.1 = (bf16[80,512]{1,0:T(8,128)(2,1)S(1)}, bf16[80,512]{1,0:T(8,128)(2,1)S(1)}, u32[]{:S(2)}, u32[]{:S(2)}) collective-permute-start(bf16[80,512]{1,0:T(8,128)(2,1)S(1)} %add_convert_fusion.3), channel_id=1, source_target_pairs={{0,32},{32,64},{64,96},{1,33},{33,65},{65,97},{2,34},{34,66},{66,9... | collective-permute-start | bytes 245768 | tf_op jit(solution)/shard_map/ppermute | solution.py:299
  80.3 0.6 copy-start.5
  135.3 11.8 %copy-start.6 = (bf16[80,512]{1,0:T(8,128)(2,1)S(1)}, bf16[80,512]{1,0:T(8,128)(2,1)}, u32[]{:S(2)}) copy-start(bf16[80,512]{1,0:T(8,128)(2,1)} %copy-done.5) | copy-start | bytes 245764
  142.8 4.2 collective-permute-start.2
  148.0 5.6 %collective-permute-start.3 = (bf16[80,512]{1,0:T(8,128)(2,1)S(1)}, bf16[80,512]{1,0:T(8,128)(2,1)S(1)}, u32[]{:S(2)}, u32[]{:S(2)}) collective-permute-start(bf16[80,512]{1,0:T(8,128)(2,1)S(1)} %add_convert_fusion.2), channel_id=1, source_target_pairs={{0,32},{32,64},{64,96},{1,33},{33,65},{65,97},{2,34},{34,66},{66,9... | collective-permute-start | bytes 245768 | tf_op jit(solution)/shard_map/ppermute | solution.py:299
  153.6 0.6 copy-start.7
  208.5 11.8 %copy-start.8 = (bf16[80,512]{1,0:T(8,128)(2,1)S(1)}, bf16[80,512]{1,0:T(8,128)(2,1)}, u32[]{:S(2)}) copy-start(bf16[80,512]{1,0:T(8,128)(2,1)} %copy-done.7) | copy-start | bytes 245764
  216.1 4.2 collective-permute-start.4
  221.2 5.6 %collective-permute-start.5 = (bf16[80,512]{1,0:T(8,128)(2,1)S(1)}, bf16[80,512]{1,0:T(8,128)(2,1)S(1)}, u32[]{:S(2)}, u32[]{:S(2)}) collective-permute-start(bf16[80,512]{1,0:T(8,128)(2,1)S(1)} %add_convert_fusion.1), channel_id=1, source_target_pairs={{0,32},{32,64},{64,96},{1,33},{33,65},{65,97},{2,34},{34,66},{66,9... | collective-permute-start | bytes 245768 | tf_op jit(solution)/shard_map/ppermute | solution.py:299
  226.8 0.6 copy-start.3
  281.7 10.6 %copy-start.9 = (f32[80,128]{1,0:T(8,128)S(1)}, f32[80,128]{1,0:T(8,128)}, u32[]{:S(2)}) copy-start(f32[80,128]{1,0:T(8,128)} %get-tuple-element.12) | copy-start | bytes 122884
  281.7 11.8 %copy-start.4 = (bf16[80,512]{1,0:T(8,128)(2,1)S(1)}, bf16[80,512]{1,0:T(8,128)(2,1)}, u32[]{:S(2)}) copy-start(bf16[80,512]{1,0:T(8,128)(2,1)} %copy-done.3) | copy-start | bytes 245764
  289.3 11.1 %copy-start.11 = (bf16[512]{0:T(512)(128)(2,1)S(1)}, bf16[512]{0:T(512)(128)(2,1)}, u32[]{:S(2)}) copy-start(bf16[512]{0:T(512)(128)(2,1)} %param.15) | copy-start | bytes 3076
  289.3 4.2 collective-permute-start.6
  294.6 7.8 %collective-permute-start.7 = (bf16[2,80,512]{2,1,0:T(8,128)(2,1)S(1)}, bf16[2,80,512]{2,1,0:T(8,128)(2,1)S(1)}, u32[]{:S(2)}, u32[]{:S(2)}) collective-permute-start(bf16[2,80,512]{2,1,0:T(8,128)(2,1)S(1)} %pad_maximum_fusion), channel_id=1, source_target_pairs={{0,32},{32,64},{64,96},{96,0},{1,33},{33,65},{65,97},{97,1},{2,34}... | collective-permute-start | bytes 491528 | tf_op jit(solution)/shard_map/ppermute | solution.py:306
  296.8 9.9 %collective-permute-start.8 = (bf16[2,80,512]{2,1,0:T(8,128)(2,1)S(1)}, bf16[2,80,512]{2,1,0:T(8,128)(2,1)S(1)}, u32[]{:S(2)}, u32[]{:S(2)}) collective-permute-start(bf16[2,80,512]{2,1,0:T(8,128)(2,1)S(1)} %pad_maximum_fusion), channel_id=1, source_target_pairs={{0,64},{32,96},{64,0},{96,32},{1,65},{33,97},{65,1},{97,33},{2,66}... | collective-permute-start | bytes 491528 | tf_op jit(solution)/shard_map/ppermute | solution.py:306
  299.3 7.5 %collective-permute-start.9 = (bf16[2,80,512]{2,1,0:T(8,128)(2,1)S(1)}, bf16[2,80,512]{2,1,0:T(8,128)(2,1)S(1)}, u32[]{:S(2)}, u32[]{:S(2)}) collective-permute-start(bf16[2,80,512]{2,1,0:T(8,128)(2,1)S(1)} %pad_maximum_fusion), channel_id=1, source_target_pairs={{0,96},{32,0},{64,32},{96,64},{1,97},{33,1},{65,33},{97,65},{2,98}... | collective-permute-start | bytes 491528 | tf_op jit(solution)/shard_map/ppermute | solution.py:306
  406.8 3.8 copy-start.10
  406.8 24.6 %all-to-all-start.10 = ((bf16[16,336,128]{2,1,0:T(8,128)(2,1)}), bf16[16,336,128]{2,1,0:T(8,128)(2,1)S(1)}, u32[]{:S(2)}, u32[]{:S(2)}) async-start(bf16[16,336,128]{2,1,0:T(8,128)(2,1)} %shard_map.136), calls=%async_computation.10 | async-start | bytes 2752512 | tf_op jit(solution)/shard_map/all_to_all | solution.py:242
  431.5 1.1 copy-start.1
  439.7 10.8 %all-to-all-start.11 = ((bf16[8,16,512]{2,1,0:T(8,128)(2,1)}), bf16[8,16,512]{2,1,0:T(8,128)(2,1)S(1)}, u32[]{:S(2)}, u32[]{:S(2)}) async-start(bf16[8,16,512]{2,1,0:T(8,128)(2,1)} %bitcast.37), calls=%async_computation.11 | async-start | bytes 262144 | tf_op jit(solution)/shard_map/all_to_all | solution.py:242

commit v2 on v1

--- a/solution.py
+++ b/solution.py
@@ -16,10 +16,14 @@
 NF = 8
 COLS = 8192
 TILES = COLS // 128
+BLOCK = 2048
+BLOCKS = COLS // BLOCK
+SENDERS = 4
+STEPS = 32767.0 / 32768.0
 EPS = 1e-05
 f32 = jnp.float32
 bf16 = jnp.bfloat16
-VMEM_LIMIT = 56 * 1024 * 1024
+VMEM_LIMIT = 16 * 1024 * 1024
 
 
 def call(kernel, out_shape, **kw):
@@ -68,10 +72,11 @@
     high, low = split_sum(jnp.sum(wide * wide, axis=1, keepdims=True))
     lane = iota((LIVE, 128), 1)
     extra = jnp.where(lane == 0, high, jnp.where(lane == 1, low, 0.0))
-    part = jnp.dot(normed, weight[...], preferred_element_type=f32)
-    for t in range(2):
-        out[t, 0, :, :FB] = part[t * HALF : (t + 1) * HALF].astype(bf16)
-        out[t, 0, :, FB:] = extra[t * HALF : (t + 1) * HALF].astype(bf16)
+    for f in range(NF):
+        part = jnp.dot(normed, weight[:, f * FB : (f + 1) * FB], preferred_element_type=f32)
+        for t in range(2):
+            out[t, f, :, :FB] = part[t * HALF : (t + 1) * HALF].astype(bf16)
+            out[t, f, :, FB:] = extra[t * HALF : (t + 1) * HALF].astype(bf16)
 
 
 def mid_kernel(parts, out):
@@ -85,59 +90,79 @@
 
 
 def down_kernel(active, weight, kept, out):
+    total = jnp.zeros((LIVE, 512), f32)
+    for f in range(NF):
+        both = jnp.concatenate([active[0, f].astype(f32), active[1, f].astype(f32)], axis=0)
+        total = total + jnp.dot(
+            both.astype(bf16), weight[f * FB : (f + 1) * FB, :], preferred_element_type=f32
+        )
+    out[...] = total * kept[:, :1]
+
+
+def power_above(value):
+    return jnp.ceil(jnp.log2(jnp.maximum(value, 1e-30)))
+
+
+def head_kernel(exits, finals, gain, weight, out, parts):
+    wide = jnp.concatenate([exits[...].astype(f32), finals[...].astype(f32)], axis=0)
+    headed = (wide * gain[...].astype(f32)).astype(bf16)
+    peak = jnp.zeros((2 * LIVE, BLOCK), f32)
+    for k in range(BLOCKS):
+        part = jnp.dot(headed, weight[:, k * BLOCK : (k + 1) * BLOCK], preferred_element_type=f32)
+        parts[k] = part
+        peak = jnp.maximum(peak, jnp.abs(part))
+    power = power_above(jnp.max(peak, axis=1, keepdims=True))
+    factor = jnp.exp2(15.0 - power) * STEPS
+    for k in range(BLOCKS):
+        scaled = jnp.clip(jnp.round(parts[k] * factor), -32767.0, 32767.0)
+        tiles = scaled.reshape(2 * LIVE, 16, 128).astype(jnp.int32).astype(jnp.int16)
+        for i in range(DP):
+            for kind in range(2):
+                for p in range(PAIRS):
+                    first = (kind * PAIRS + p) * TILES + 16 * k
+                    out[i, first : first + 16, :] = tiles[kind * LIVE + i * PAIRS + p]
+    squares = jnp.sum(wide * wide, axis=1, keepdims=True)
+    square_power = power_above(squares)
+    whole = jnp.round(squares * jnp.exp2(29.0 - square_power)).astype(jnp.int32)
+    lane = iota((2 * LIVE, 128), 1)
+    extra = jnp.where(lane == 0, power.astype(jnp.int32), 0)
+    extra = jnp.where(lane == 1, whole >> 15, extra)
+    extra = jnp.where(lane == 2, whole & 32767, extra)
+    extra = jnp.where(lane == 3, square_power.astype(jnp.int32), extra)
+    gap = jnp.zeros((8 - PAIRS, 128), jnp.int32)
+    for i in range(DP):
+        mine = [extra[kind * LIVE + i * PAIRS : kind * LIVE + (i + 1) * PAIRS] for kind in range(2)]
+        rows = jnp.concatenate([mine[0], gap, mine[1], gap], axis=0)
+        out[i, 2 * PAIRS * TILES :, :] = rows.astype(jnp.int16)
+
+
+def peak_kernel(parts, logits, stats, total):
     step = pl.program_id(0)
-    both = jnp.concatenate([active[0, 0].astype(f32), active[1, 0].astype(f32)], axis=0)
-    part = jnp.dot(both.astype(bf16), weight[...], preferred_element_type=f32)
 
     @pl.when(step == 0)
     def _():
-        out[...] = part
-
-    @pl.when(step > 0)
-    def _():
-        out[...] = out[...] + part
-
-    @pl.when(step == NF - 1)
-    def _():
-        out[...] = out[...] * kept[:, :1]
-
-
-def head_kernel(exits, finals, gain, weight, out):
-    step = pl.program_id(0)
-    wide = jnp.concatenate([exits[...].astype(f32), finals[...].astype(f32)], axis=0)
-    headed = (wide * gain[...].astype(f32)).astype(bf16)
-    part = jnp.dot(headed, weight[...], preferred_element_type=f32)
-    tiles = part.reshape(2 * LIVE, 8, 128)
-    base = pl.multiple_of(step * 8, 8)
-    for i in range(DP):
-        for kind in range(2):
-            for p in range(PAIRS):
-                slot = kind * PAIRS + p
-                out[i, pl.ds(slot * TILES + base, 8), :] = tiles[kind * LIVE + i * PAIRS + p]
-
-    @pl.when(step == 0)
-    def _():
-        squares = jnp.broadcast_to(jnp.sum(wide * wide, axis=1, keepdims=True), (2 * LIVE, 128))
-        for i in range(DP):
-            for kind in range(2):
-                at = kind * LIVE + i * PAIRS
-                first = 2 * PAIRS * TILES + kind * 8
-                out[i, first : first + PAIRS, :] = squares[at : at + PAIRS]
-                out[i, first + PAIRS : first + 8, :] = jnp.zeros((8 - PAIRS, 128), f32)
-
-
-def peak_kernel(parts, logits, stats, total):
-    step = pl.program_id(0)
-
-    @pl.when(step == 0)
-    def _():
-        total[...] = parts[0]
-
-    @pl.when(step > 0)
-    def _():
-        total[...] = total[...] + parts[0]
-
-    @pl.when(step == DP - 1)
+        total[...] = jnp.zeros_like(total)
+
+    sums = []
+    for j in range(SENDERS):
+        extra = parts[j, 2 * PAIRS * TILES :, :].astype(jnp.int32).astype(f32)
+        factor = jnp.exp2(extra[:, 0:1] - 15.0) * (1.0 / STEPS)
+        squares = (extra[:, 1:2] * 32768.0 + extra[:, 2:3]) * jnp.exp2(extra[:, 3:4] - 29.0)
+        sums.append((factor, squares))
+    for slot in range(2 * PAIRS):
+        row = slot // PAIRS * 8 + slot % PAIRS
+        first = slot * TILES
+        value = total[first : first + TILES, :]
+        for j in range(SENDERS):
+            whole = parts[j, first : first + TILES, :].astype(jnp.int32).astype(f32)
+            value = value + whole * sums[j][0][row : row + 1]
+        total[first : first + TILES, :] = value
+    extra = total[2 * PAIRS * TILES :, :]
+    for j in range(SENDERS):
+        extra = extra + sums[j][1]
+    total[2 * PAIRS * TILES :, :] = extra
+
+    @pl.when(step == DP // SENDERS - 1)
     def _():
         lane = iota((1, 128), 1)
         for p in range(PAIRS):
@@ -199,43 +224,34 @@
         out[j, PAIRS * TILES :, :] = extra
 
 
-def grad_kernel(gaps, weight, slots, buckets, out, kl_out, hist, total):
-    step = pl.program_id(0)
-    base = pl.multiple_of(step * 16, 16)
-    rows = [gaps[:, pl.ds(p * TILES + base, 16), :].astype(f32) for p in range(PAIRS)]
-    left = jnp.stack(rows, axis=1).reshape(LIVE, 16 * 128).astype(bf16)
-    part = lax.dot_general(left, weight[...], (((1,), (1,)), ((), ())), preferred_element_type=f32)
-
-    @pl.when(step == 0)
-    def _():
-        total[...] = part
-
-    @pl.when(step > 0)
-    def _():
-        total[...] = total[...] + part
-
-    @pl.when(step == 3)
-    def _():
-        pick = slots[...]
-        out[...] = lax.dot_general(
-            pick.astype(bf16),
-            total[...].astype(bf16),
-            (((0,), (0,)), ((), ())),
-            preferred_element_type=f32,
-        ).astype(bf16)
-        extra = gaps[:, PAIRS * TILES :, :].astype(f32)[:, :PAIRS, :].reshape(LIVE, 128)
-        kl = jnp.sum(extra, axis=1, keepdims=True)
-        by_slot = jnp.sum(pick * kl, axis=0, keepdims=True)
-        kl_out[...] = jnp.broadcast_to(by_slot, (8, 128))
-        mine = jnp.where(iota((8, 128), 1) // XS == iota((8, 128), 0), by_slot, 0.0)
-        hot = jnp.where(iota((NB, 128), 0) == buckets[...], 1.0, 0.0)
-        hist[...] = lax.dot_general(
-            mine,
-            hot,
+def grad_kernel(gaps, weight, slots, buckets, out, kl_out, hist):
+    total = jnp.zeros((LIVE, 512), f32)
+    for k in range(BLOCKS):
+        rows = [gaps[:, p * TILES + 16 * k : p * TILES + 16 * k + 16, :].astype(f32) for p in range(PAIRS)]
+        left = jnp.stack(rows, axis=1).reshape(LIVE, BLOCK).astype(bf16)
+        total = total + lax.dot_general(
+            left,
+            weight[:, k * BLOCK : (k + 1) * BLOCK],
             (((1,), (1,)), ((), ())),
             preferred_element_type=f32,
-            precision=lax.Precision.HIGHEST,
         )
+    pick = slots[...]
+    out[...] = lax.dot_general(
+        pick.astype(bf16), total.astype(bf16), (((0,), (0,)), ((), ())), preferred_element_type=f32
+    ).astype(bf16)
+    extra = gaps[:, PAIRS * TILES :, :].astype(f32)[:, :PAIRS, :].reshape(LIVE, 128)
+    kl = jnp.sum(extra, axis=1, keepdims=True)
+    by_slot = jnp.sum(pick * kl, axis=0, keepdims=True)
+    kl_out[...] = jnp.broadcast_to(by_slot, (8, 128))
+    mine = jnp.where(iota((8, 128), 1) // XS == iota((8, 128), 0), by_slot, 0.0)
+    hot = jnp.where(iota((NB, 128), 0) == buckets[...], 1.0, 0.0)
+    hist[...] = lax.dot_general(
+        mine,
+        hot,
+        (((1,), (1,)), ((), ())),
+        preferred_element_type=f32,
+        precision=lax.Precision.HIGHEST,
+    )
 
 
 def exchange(value, axis):
@@ -247,8 +263,9 @@
 ):
     sections = lax.axis_size("section")
     section_id = lax.axis_index("section")
-    up_local = w_up[0]
-    down_local = w_down[0]
+    up_local = pltpu.with_memory_space_constraint(w_up[0], pltpu.VMEM)
+    down_local = pltpu.with_memory_space_constraint(w_down[0], pltpu.VMEM)
+    head_local = pltpu.with_memory_space_constraint(w_head, pltpu.VMEM)
     keep_mine = lax.dynamic_slice_in_dim(keep, section_id, 1, 0)
     shape = jax.ShapeDtypeStruct
     vmem = pl.BlockSpec(memory_space=pltpu.VMEM)
@@ -268,13 +285,8 @@
         parts = call(
             up_kernel,
             shape((2, NF, HALF, FB + 128), bf16),
-            grid=(NF,),
-            in_specs=[
-                pl.BlockSpec((LIVE, 512), lambda f: (0, 0)),
-                pl.BlockSpec((1, 512), lambda f: (0, 0)),
-                pl.BlockSpec((512, FB), lambda f: (0, f)),
-            ],
-            out_specs=pl.BlockSpec((2, 1, HALF, FB + 128), lambda f: (0, f, 0, 0)),
+            in_specs=[vmem] * 3,
+            out_specs=vmem,
         )(current, norm_gain, up_local)
         parts = exchange(parts.reshape(DP, HALF, FB + 128), "dp")
         active = call(
@@ -282,15 +294,7 @@
         )(parts)
         active = exchange(active, "dp")
         lowered = call(
-            down_kernel,
-            shape((LIVE, 512), f32),
-            grid=(NF,),
-            in_specs=[
-                pl.BlockSpec((2, 1, HALF, FB), lambda f: (0, f, 0, 0)),
-                pl.BlockSpec((FB, 512), lambda f: (f, 0)),
-                pl.BlockSpec((LIVE, 128), lambda f: (0, 0)),
-            ],
-            out_specs=pl.BlockSpec((LIVE, 512), lambda f: (0, 0)),
+            down_kernel, shape((LIVE, 512), f32), in_specs=[vmem] * 3, out_specs=vmem
         )(active.reshape(2, NF, HALF, FB), down_local, kept)
         other = lax.ppermute(lowered, "mp", [(0, 1), (1, 0)])
         result = (current.astype(f32) + (lowered + other)).astype(bf16)
@@ -307,22 +311,17 @@
     extent = 2 * PAIRS * TILES + 16
     parts = call(
         head_kernel,
-        shape((DP, extent, 128), f32),
-        grid=(8,),
-        in_specs=[
-            pl.BlockSpec((LIVE, 512), lambda k: (0, 0)),
-            pl.BlockSpec((LIVE, 512), lambda k: (0, 0)),
-            pl.BlockSpec((1, 512), lambda k: (0, 0)),
-            pl.BlockSpec((512, 1024), lambda k: (0, k)),
-        ],
-        out_specs=pl.BlockSpec((DP, extent, 128), lambda k: (0, 0, 0)),
-    )(spread[0], spread[1], head_gain.reshape(1, -1), w_head)
+        shape((DP, extent, 128), jnp.int16),
+        in_specs=[vmem] * 4,
+        out_specs=vmem,
+        scratch_shapes=[pltpu.VMEM((BLOCKS, 2 * LIVE, BLOCK), f32)],
+    )(spread[0], spread[1], head_gain.reshape(1, -1), head_local)
     parts = exchange(parts, "dp")
     logits, stats = call(
         peak_kernel,
         (shape((2 * PAIRS * TILES, 128), f32), shape((8, 8, 128), f32)),
-        grid=(DP,),
-        in_specs=[pl.BlockSpec((1, extent, 128), lambda j: (j, 0, 0))],
+        grid=(DP // SENDERS,),
+        in_specs=[pl.BlockSpec((SENDERS, extent, 128), lambda j: (j, 0, 0))],
         out_specs=[
             pl.BlockSpec((2 * PAIRS * TILES, 128), lambda j: (0, 0)),
             pl.BlockSpec((8, 8, 128), lambda j: (0, 0, 0)),
@@ -338,20 +337,9 @@
     feature, kl, hist = call(
         grad_kernel,
         (shape((128, 512), bf16), shape((8, 128), f32), shape((8, NB), f32)),
-        grid=(4,),
-        in_specs=[
-            pl.BlockSpec((DP, extent, 128), lambda k: (0, 0, 0)),
-            pl.BlockSpec((512, 2048), lambda k: (0, k)),
-            pl.BlockSpec((LIVE, 128), lambda k: (0, 0)),
-            pl.BlockSpec((1, 128), lambda k: (0, 0)),
-        ],
-        out_specs=[
-            pl.BlockSpec((128, 512), lambda k: (0, 0)),
-            pl.BlockSpec((8, 128), lambda k: (0, 0)),
-            pl.BlockSpec((8, NB), lambda k: (0, 0)),
-        ],
-        scratch_shapes=[pltpu.VMEM((LIVE, 512), f32)],
-    )(gaps, w_head, slots, kl_bucket.reshape(1, -1))
+        in_specs=[vmem] * 4,
+        out_specs=[vmem] * 3,
+    )(gaps, head_local, slots, kl_bucket.reshape(1, -1))
     feature = exchange(feature.reshape(8, 16, 512), ("section", "mp"))
     feature_grad = jnp.sum(feature.astype(f32), axis=0)
     kl_here = lax.dynamic_slice_in_dim(kl[0], lax.axis_index("dp") * 8, 8, 0)

time: 454 us -> 334 us (0.74)
  Pallas kernels: 102 us -> 23.4 us
  blocking collectives: 259 us -> 214 us
  local copies, waits for them, and re-layouts: 9.19 us -> 14.1 us
    pallas_call x9, Pallas kernels: 70.2 us -> 14.8 us  [the longest x4 5.78 us: shards(): call(down_kernel, shape((LIVE, 512), f32), in_specs=[vmem] * 3, out_specs...]
    all_to_all x10, blocking collectives: 259 us -> 214 us  [exchange(): return lax.all_to_all(value, axis, 0, 0)]
    pallas_call x4, Pallas kernels: 10.8 us -> 1.45 us  [shards(): call(mid_kernel, shape((DP, HALF, FB), bf16), in_specs=[vmem], out_specs=...]
    unnamed x24 -> x26, local copies, waits for them, and re-layouts: 3.02 us -> 12.1 us
    pallas_call x1, Pallas kernels: 9.46 us -> 1.33 us  [shards(): call(peak_kernel, (shape((2 * PAIRS * TILES, 128), f32), shape((8, 8, 128...]
  transfers between devices with their start and end apart: 12 -> 12, of which waited for: 11 -> 11; matrix products, arithmetic and copies ran while one was open for 1% -> 0% of each run, Pallas kernels for 0% -> 0%
where the time goes in v2:
time: 334 us; the launch traced here: 333 us
  blocking collectives  214 us (64%)
  starting transfers between devices  40.1 us (12%)
  waiting for transfers between devices  39.5 us (12%)
  Pallas kernels  23.4 us (7%)
  local copies, waits for them, and re-layouts  14.1 us (4%)
    all_to_all x10, blocking collectives, exchange(): return lax.all_to_all(value, axis, 0, 0)  214 us
    all_to_all x2, waiting for transfers between devices, exchange(): return lax.all_to_all(value, axis, 0, 0)  24.8 us
    ppermute x4, starting transfers between devices, shards(): other = lax.ppermute(lowered, 'mp', [(0, 1), (1, 0)])  13.4 us
    unnamed x26, local copies, waits for them, and re-layouts  12.1 us
    ppermute x3, starting transfers between devices, shards(): lax.ppermute(result, 'section', [(i, i + 1) for i in range(sections - 1)])  11.5 us
    all_to_all x2, starting transfers between devices, exchange(): return lax.all_to_all(value, axis, 0, 0)  9.3 us
  transfers between devices with their start and end apart: 12, of which 11 were waited for; matrix products, arithmetic and copies ran while one was open for 0% of the time, Pallas kernels for 0%

profile of v2, /device:TPU:1, one launch (start us, length us, event | category | flops | bytes accessed | tf_op | source)
XLA Modules:
  0.0 333.1 jit_solution(18442654088873866573)
XLA Ops:
  0.6 0.0 copy-start
  0.7 0.8 reshape.43.index
  1.4 0.9 copy-done.5
  2.3 0.7 copy-done.8
  3.0 0.8 shard_map.121
  3.8 3.1 copy-done.2
  6.8 0.7 copy-done.6
  7.5 1.3 shard_map.122
  8.8 27.8 %all_to_all.60.parts = bf16[16,40,1024]{2,1,0:T(8,128)(2,1)S(1)} all-to-all(bf16[16,40,1024]{2,1,0:T(8,128)(2,1)S(1)} %bitcast.31), channel_id=1, replica_groups=mesh['section'=4,'dp'=16,'mp'=2] {'dp'}, dimensions={0} | all-to-all | bytes 2621440 | tf_op jit(solution)/shard_map/all_to_all | solution.py:258
  36.6 0.4 shard_map.123
  37.0 20.0 %all_to_all.61 = bf16[16,40,896]{2,1,0:T(8,128)(2,1)S(1)} all-to-all(bf16[16,40,896]{2,1,0:T(8,128)(2,1)S(1)} %shard_map.123), channel_id=1, replica_groups=mesh['section'=4,'dp'=16,'mp'=2] {'dp'}, dimensions={0} | all-to-all | bytes 2293760 | tf_op jit(solution)/shard_map/all_to_all | solution.py:258
  57.0 1.4 shard_map.124
  58.4 2.5 collective-permute-start
  61.0 1.0 collective-permute-done
  62.0 3.1 collective-permute-start.1
  65.2 1.5 collective-permute-done.1.state
  66.6 1.3 shard_map.125
  67.9 21.3 %all_to_all.62.parts = bf16[16,40,1024]{2,1,0:T(8,128)(2,1)S(1)} all-to-all(bf16[16,40,1024]{2,1,0:T(8,128)(2,1)S(1)} %bitcast.32), channel_id=1, replica_groups=mesh['section'=4,'dp'=16,'mp'=2] {'dp'}, dimensions={0} | all-to-all | bytes 2621440 | tf_op jit(solution)/shard_map/all_to_all | solution.py:258
  89.2 0.4 shard_map.126
  89.6 18.5 %all_to_all.63 = bf16[16,40,896]{2,1,0:T(8,128)(2,1)S(1)} all-to-all(bf16[16,40,896]{2,1,0:T(8,128)(2,1)S(1)} %shard_map.126), channel_id=1, replica_groups=mesh['section'=4,'dp'=16,'mp'=2] {'dp'}, dimensions={0} | all-to-all | bytes 2293760 | tf_op jit(solution)/shard_map/all_to_all | solution.py:258
  108.1 1.4 shard_map.127
  109.5 3.6 %collective-permute-start.2 = (f32[80,512]{1,0:T(8,128)S(1)}, f32[80,512]{1,0:T(8,128)S(1)}, u32[]{:S(2)}, u32[]{:S(2)}) collective-permute-start(f32[80,512]{1,0:T(8,128)S(1)} %shard_map.127), channel_id=1, source_target_pairs={{0,1},{1,0},{2,3},{3,2},{4,5},{5,4},{6,7},{7,6},{8,9},{9,8},{10,11... | collective-permute-start | bytes 491528 | tf_op jit(solution)/shard_map/ppermute | solution.py:299
  113.2 1.0 collective-permute-done.2
  114.2 4.2 %collective-permute-start.3 = (bf16[80,512]{1,0:T(8,128)(2,1)S(1)}, bf16[80,512]{1,0:T(8,128)(2,1)S(1)}, u32[]{:S(2)}, u32[]{:S(2)}) collective-permute-start(bf16[80,512]{1,0:T(8,128)(2,1)S(1)} %add_convert_fusion.2), channel_id=1, source_target_pairs={{0,32},{32,64},{64,96},{1,33},{33,65},{65,97},{2,34},{34,66},{66,9... | collective-permute-start | bytes 245768 | tf_op jit(solution)/shard_map/ppermute | solution.py:303
  118.4 1.5 collective-permute-done.3.state
  119.9 1.3 shard_map.128
  121.2 21.3 %all_to_all.64.parts = bf16[16,40,1024]{2,1,0:T(8,128)(2,1)S(1)} all-to-all(bf16[16,40,1024]{2,1,0:T(8,128)(2,1)S(1)} %bitcast.33), channel_id=1, replica_groups=mesh['section'=4,'dp'=16,'mp'=2] {'dp'}, dimensions={0} | all-to-all | bytes 2621440 | tf_op jit(solution)/shard_map/all_to_all | solution.py:258
  142.4 0.4 shard_map.129
  142.8 18.5 %all_to_all.65 = bf16[16,40,896]{2,1,0:T(8,128)(2,1)S(1)} all-to-all(bf16[16,40,896]{2,1,0:T(8,128)(2,1)S(1)} %shard_map.129), channel_id=1, replica_groups=mesh['section'=4,'dp'=16,'mp'=2] {'dp'}, dimensions={0} | all-to-all | bytes 2293760 | tf_op jit(solution)/shard_map/all_to_all | solution.py:258
  161.3 1.4 shard_map.130
  162.8 3.6 %collective-permute-start.4 = (f32[80,512]{1,0:T(8,128)S(1)}, f32[80,512]{1,0:T(8,128)S(1)}, u32[]{:S(2)}, u32[]{:S(2)}) collective-permute-start(f32[80,512]{1,0:T(8,128)S(1)} %shard_map.130), channel_id=1, source_target_pairs={{0,1},{1,0},{2,3},{3,2},{4,5},{5,4},{6,7},{7,6},{8,9},{9,8},{10,11... | collective-permute-start | bytes 491528 | tf_op jit(solution)/shard_map/ppermute | solution.py:299
  166.4 1.0 collective-permute-done.4
  167.4 4.2 %collective-permute-start.5 = (bf16[80,512]{1,0:T(8,128)(2,1)S(1)}, bf16[80,512]{1,0:T(8,128)(2,1)S(1)}, u32[]{:S(2)}, u32[]{:S(2)}) collective-permute-start(bf16[80,512]{1,0:T(8,128)(2,1)S(1)} %add_convert_fusion.1), channel_id=1, source_target_pairs={{0,32},{32,64},{64,96},{1,33},{33,65},{65,97},{2,34},{34,66},{66,9... | collective-permute-start | bytes 245768 | tf_op jit(solution)/shard_map/ppermute | solution.py:303
  171.6 1.5 collective-permute-done.5.state
  173.1 1.3 shard_map.131
  174.4 21.3 %all_to_all.66.parts = bf16[16,40,1024]{2,1,0:T(8,128)(2,1)S(1)} all-to-all(bf16[16,40,1024]{2,1,0:T(8,128)(2,1)S(1)} %bitcast.34), channel_id=1, replica_groups=mesh['section'=4,'dp'=16,'mp'=2] {'dp'}, dimensions={0} | all-to-all | bytes 2621440 | tf_op jit(solution)/shard_map/all_to_all | solution.py:258
  195.6 0.4 shard_map.132
  196.0 18.5 %all_to_all.67 = bf16[16,40,896]{2,1,0:T(8,128)(2,1)S(1)} all-to-all(bf16[16,40,896]{2,1,0:T(8,128)(2,1)S(1)} %shard_map.132), channel_id=1, replica_groups=mesh['section'=4,'dp'=16,'mp'=2] {'dp'}, dimensions={0} | all-to-all | bytes 2293760 | tf_op jit(solution)/shard_map/all_to_all | solution.py:258
  214.5 1.4 shard_map.133
  216.0 3.6 %collective-permute-start.6 = (f32[80,512]{1,0:T(8,128)S(1)}, f32[80,512]{1,0:T(8,128)S(1)}, u32[]{:S(2)}, u32[]{:S(2)}) collective-permute-start(f32[80,512]{1,0:T(8,128)S(1)} %shard_map.133), channel_id=1, source_target_pairs={{0,1},{1,0},{2,3},{3,2},{4,5},{5,4},{6,7},{7,6},{8,9},{9,8},{10,11... | collective-permute-start | bytes 491528 | tf_op jit(solution)/shard_map/ppermute | solution.py:299
  219.6 0.1 fusion.1
  219.7 0.9 collective-permute-done.6
  220.6 0.1 select_bitcast_fusion.1
  220.7 2.3 collective-permute-start.7
  223.1 2.4 collective-permute-start.8
  225.5 1.2 collective-permute-start.9
  226.7 1.9 collective-permute-done.7
  228.6 4.4 %collective-permute-done.8 = bf16[2,80,512]{2,1,0:T(8,128)(2,1)S(1)} collective-permute-done((bf16[2,80,512]{2,1,0:T(8,128)(2,1)S(1)}, bf16[2,80,512]{2,1,0:T(8,128)(2,1)S(1)}, u32[]{:S(2)}, u32[]{:S(2)}) %collective-permute-start.8) | collective-permute-done | bytes 163872 | tf_op jit(solution)/shard_map/ppermute | solution.py:310
  233.0 3.4 %copy-done.3 = bf16[512,8192]{1,0:T(8,128)(2,1)S(1)} copy-done((bf16[512,8192]{1,0:T(8,128)(2,1)S(1)}, bf16[512,8192]{1,0:T(8,128)(2,1)}, u32[]{:S(2)}) %copy-start.3) | copy-done | bytes 8388632
  236.4 3.9 %shard_map.134 = s16[16,656,128]{2,1,0:T(8,128)(2,1)S(1)} custom-call(bf16[80,512]{1,0:T(8,128)(2,1)S(1)} %get-tuple-element.24.exits, bf16[80,512]{1,0:T(8,128)(2,1)S(1)} %get-tuple-element.23.finals, bf16[1,512]{1,0:T(2,128)(2,1)S(1)} %reshape.52.gain, bf16[512,8192]{1,0:T(8,128)(2,1)S(1)} %copy-done.3), custom_call_target="tpu_custom_call" | custom-call | tf_op jit(solution)/shard_map/pallas_call | solution.py:312
  240.4 36.4 %all_to_all.68.parts = s16[16,656,128]{2,1,0:T(8,128)(2,1)S(1)} all-to-all(s16[16,656,128]{2,1,0:T(8,128)(2,1)S(1)} %shard_map.134), channel_id=1, replica_groups=mesh['section'=4,'dp'=16,'mp'=2] {'dp'}, dimensions={0} | all-to-all | bytes 5373952 | tf_op jit(solution)/shard_map/all_to_all | solution.py:258
  276.8 1.3 shard_map.135
  278.1 10.6 %all_to_all.69.stats = f32[8,8,128]{2,1,0:T(8,128)S(1)} all-to-all(f32[8,8,128]{2,1,0:T(8,128)S(1)} %get-tuple-element.16), channel_id=1, replica_groups=mesh['section'=4,'dp'=16,'mp'=2] {'section','mp'}, dimensions={0} | all-to-all | bytes 65536 | tf_op jit(solution)/shard_map/all_to_all | solution.py:258
  288.7 1.4 shard_map.136
  290.1 3.8 %all-to-all-start.10 = ((bf16[16,336,128]{2,1,0:T(8,128)(2,1)}), bf16[16,336,128]{2,1,0:T(8,128)(2,1)S(1)}, u32[]{:S(2)}, u32[]{:S(2)}) async-start(bf16[16,336,128]{2,1,0:T(8,128)(2,1)} %shard_map.136), calls=%async_computation.10 | async-start | bytes 2752512 | tf_op jit(solution)/shard_map/all_to_all | solution.py:258
  293.9 0.1 reshape.53.buckets
  294.0 20.7 %all-to-all-done.10.gaps = bf16[16,336,128]{2,1,0:T(8,128)(2,1)S(1)} async-done(((bf16[16,336,128]{2,1,0:T(8,128)(2,1)}), bf16[16,336,128]{2,1,0:T(8,128)(2,1)S(1)}, u32[]{:S(2)}, u32[]{:S(2)}) %all-to-all-start.10) | async-done | bytes 1376288 | tf_op jit(solution)/shard_map/all_to_all | solution.py:258
  314.7 3.4 %copy-done.4 = bf16[512,8192]{1,0:T(8,128)(2,1)S(1)} copy-done((bf16[512,8192]{1,0:T(8,128)(2,1)S(1)}, bf16[512,8192]{1,0:T(8,128)(2,1)}, u32[]{:S(2)}) %copy-start.4) | copy-done | bytes 8388632
  318.1 3.6 %shard_map.137 = (bf16[128,512]{1,0:T(8,128)(2,1)}, f32[8,128]{1,0:T(8,128)S(1)}, f32[8,16]{1,0:T(8,128)S(1)}) custom-call(bf16[16,336,128]{2,1,0:T(8,128)(2,1)S(1)} %all-to-all-done.10.gaps, bf16[512,8192]{1,0:T(8,128)(2,1)S(1)} %copy-done.4, f32[80,128]{1,0:T(8,128)S(1)} %get-tuple-element.17.slots, s32[1,128]{1,0:T(1,128)S(1)} %reshape.53.buckets), custom_call_target="tpu_custom_call" | custom-call | tf_op jit(solution)/shard_map/pallas_call | solution.py:337
  321.7 5.5 %all-to-all-start.11 = ((bf16[8,16,512]{2,1,0:T(8,128)(2,1)}), bf16[8,16,512]{2,1,0:T(8,128)(2,1)S(1)}, u32[]{:S(2)}, u32[]{:S(2)}) async-start(bf16[8,16,512]{2,1,0:T(8,128)(2,1)} %bitcast.14), calls=%async_computation.11 | async-start | bytes 262144 | tf_op jit(solution)/shard_map/all_to_all | solution.py:258
  327.2 0.6 slice.19
  327.8 0.6 dynamic-slice_bitcast_fusion
  328.3 4.1 %all-to-all-done.11 = bf16[8,16,512]{2,1,0:T(8,128)(2,1)S(1)} async-done(((bf16[8,16,512]{2,1,0:T(8,128)(2,1)}), bf16[8,16,512]{2,1,0:T(8,128)(2,1)S(1)}, u32[]{:S(2)}, u32[]{:S(2)}) %all-to-all-start.11) | async-done | bytes 131104 | tf_op jit(solution)/shard_map/all_to_all | solution.py:258
  332.5 0.6 convert_reduce_fusion
  (31 shorter events, 0.2 us)
Async XLA Ops:
  0.6 0.8 copy-start
  1.4 0.9 copy-start.5
  2.3 0.7 copy-start.8
  3.8 3.1 copy-start.2
  6.8 0.7 copy-start.6
  7.5 59.1 %slice-start = ((s8[7340032]{0:T(1024)(128)(4,1)}), s8[4194304]{0:T(1024)(128)(4,1)S(1)}, s32[]{:S(2)}) async-start(s8[7340032]{0:T(1024)(128)(4,1)} %bitcast.26), calls=%async_computation.12 | async-start | bytes 8388608
  8.8 48.2 %copy-start.1 = (bf16[1,7168,512]{2,1,0:T(8,128)(2,1)S(1)}, bf16[1,7168,512]{2,1,0:T(8,128)(2,1)}, u32[]{:S(2)}) copy-start(bf16[1,7168,512]{2,1,0:T(8,128)(2,1)} %param.14) | copy-start | bytes 22020100
  36.6 30.0 %slice-start.1 = ((s8[7340032]{0:T(1024)(128)(4,1)}), s8[3145728]{0:T(1024)(128)(4,1)S(1)}, s32[]{:S(2)}) async-start(s8[7340032]{0:T(1024)(128)(4,1)} %bitcast.26), calls=%async_computation.13 | async-start | bytes 6291456
  57.0 9.6 %copy-start.7 = (bf16[1,512]{1,0:T(2,128)(2,1)S(1)}, bf16[1,512]{1,0:T(2,128)(2,1)}, u32[]{:S(2)}) copy-start(bf16[1,512]{1,0:T(2,128)(2,1)} %gain.7) | copy-start | bytes 3076
  58.4 3.6 %collective-permute-start = (f32[80,512]{1,0:T(8,128)S(1)}, f32[80,512]{1,0:T(8,128)S(1)}, u32[]{:S(2)}, u32[]{:S(2)}) collective-permute-start(f32[80,512]{1,0:T(8,128)S(1)} %shard_map.124), channel_id=1, source_target_pairs={{0,1},{1,0},{2,3},{3,2},{4,5},{5,4},{6,7},{7,6},{8,9},{9,8},{10,11... | collective-permute-start | bytes 491528 | tf_op jit(solution)/shard_map/ppermute | solution.py:299
  62.0 4.6 %collective-permute-start.1 = (bf16[80,512]{1,0:T(8,128)(2,1)S(1)}, bf16[80,512]{1,0:T(8,128)(2,1)S(1)}, u32[]{:S(2)}, u32[]{:S(2)}) collective-permute-start(bf16[80,512]{1,0:T(8,128)(2,1)S(1)} %add_convert_fusion.3), channel_id=1, source_target_pairs={{0,32},{32,64},{64,96},{1,33},{33,65},{65,97},{2,34},{34,66},{66,9... | collective-permute-start | bytes 245768 | tf_op jit(solution)/shard_map/ppermute | solution.py:303
  109.5 4.7 %collective-permute-start.2 = (f32[80,512]{1,0:T(8,128)S(1)}, f32[80,512]{1,0:T(8,128)S(1)}, u32[]{:S(2)}, u32[]{:S(2)}) collective-permute-start(f32[80,512]{1,0:T(8,128)S(1)} %shard_map.127), channel_id=1, source_target_pairs={{0,1},{1,0},{2,3},{3,2},{4,5},{5,4},{6,7},{7,6},{8,9},{9,8},{10,11... | collective-permute-start | bytes 491528 | tf_op jit(solution)/shard_map/ppermute | solution.py:299
  114.2 5.6 %collective-permute-start.3 = (bf16[80,512]{1,0:T(8,128)(2,1)S(1)}, bf16[80,512]{1,0:T(8,128)(2,1)S(1)}, u32[]{:S(2)}, u32[]{:S(2)}) collective-permute-start(bf16[80,512]{1,0:T(8,128)(2,1)S(1)} %add_convert_fusion.2), channel_id=1, source_target_pairs={{0,32},{32,64},{64,96},{1,33},{33,65},{65,97},{2,34},{34,66},{66,9... | collective-permute-start | bytes 245768 | tf_op jit(solution)/shard_map/ppermute | solution.py:303
  162.8 4.6 %collective-permute-start.4 = (f32[80,512]{1,0:T(8,128)S(1)}, f32[80,512]{1,0:T(8,128)S(1)}, u32[]{:S(2)}, u32[]{:S(2)}) collective-permute-start(f32[80,512]{1,0:T(8,128)S(1)} %shard_map.130), channel_id=1, source_target_pairs={{0,1},{1,0},{2,3},{3,2},{4,5},{5,4},{6,7},{7,6},{8,9},{9,8},{10,11... | collective-permute-start | bytes 491528 | tf_op jit(solution)/shard_map/ppermute | solution.py:299
  167.4 5.6 %collective-permute-start.5 = (bf16[80,512]{1,0:T(8,128)(2,1)S(1)}, bf16[80,512]{1,0:T(8,128)(2,1)S(1)}, u32[]{:S(2)}, u32[]{:S(2)}) collective-permute-start(bf16[80,512]{1,0:T(8,128)(2,1)S(1)} %add_convert_fusion.1), channel_id=1, source_target_pairs={{0,32},{32,64},{64,96},{1,33},{33,65},{65,97},{2,34},{34,66},{66,9... | collective-permute-start | bytes 245768 | tf_op jit(solution)/shard_map/ppermute | solution.py:303
  216.0 10.7 %copy-start.10 = (bf16[512]{0:T(512)(128)(2,1)S(1)}, bf16[512]{0:T(512)(128)(2,1)}, u32[]{:S(2)}) copy-start(bf16[512]{0:T(512)(128)(2,1)} %param.15) | copy-start | bytes 3076
  216.0 4.6 %collective-permute-start.6 = (f32[80,512]{1,0:T(8,128)S(1)}, f32[80,512]{1,0:T(8,128)S(1)}, u32[]{:S(2)}, u32[]{:S(2)}) collective-permute-start(f32[80,512]{1,0:T(8,128)S(1)} %shard_map.133), channel_id=1, source_target_pairs={{0,1},{1,0},{2,3},{3,2},{4,5},{5,4},{6,7},{7,6},{8,9},{9,8},{10,11... | collective-permute-start | bytes 491528 | tf_op jit(solution)/shard_map/ppermute | solution.py:299
  220.7 7.9 %collective-permute-start.7 = (bf16[2,80,512]{2,1,0:T(8,128)(2,1)S(1)}, bf16[2,80,512]{2,1,0:T(8,128)(2,1)S(1)}, u32[]{:S(2)}, u32[]{:S(2)}) collective-permute-start(bf16[2,80,512]{2,1,0:T(8,128)(2,1)S(1)} %pad_maximum_fusion), channel_id=1, source_target_pairs={{0,32},{32,64},{64,96},{96,0},{1,33},{33,65},{65,97},{97,1},{2,34}... | collective-permute-start | bytes 491528 | tf_op jit(solution)/shard_map/ppermute | solution.py:310
  223.1 9.9 %collective-permute-start.8 = (bf16[2,80,512]{2,1,0:T(8,128)(2,1)S(1)}, bf16[2,80,512]{2,1,0:T(8,128)(2,1)S(1)}, u32[]{:S(2)}, u32[]{:S(2)}) collective-permute-start(bf16[2,80,512]{2,1,0:T(8,128)(2,1)S(1)} %pad_maximum_fusion), channel_id=1, source_target_pairs={{0,64},{32,96},{64,0},{96,32},{1,65},{33,97},{65,1},{97,33},{2,66}... | collective-permute-start | bytes 491528 | tf_op jit(solution)/shard_map/ppermute | solution.py:310
  225.5 7.5 %collective-permute-start.9 = (bf16[2,80,512]{2,1,0:T(8,128)(2,1)S(1)}, bf16[2,80,512]{2,1,0:T(8,128)(2,1)S(1)}, u32[]{:S(2)}, u32[]{:S(2)}) collective-permute-start(bf16[2,80,512]{2,1,0:T(8,128)(2,1)S(1)} %pad_maximum_fusion), channel_id=1, source_target_pairs={{0,96},{32,0},{64,32},{96,64},{1,97},{33,1},{65,33},{97,65},{2,98}... | collective-permute-start | bytes 491528 | tf_op jit(solution)/shard_map/ppermute | solution.py:310
  233.0 3.4 %copy-start.3 = (bf16[512,8192]{1,0:T(8,128)(2,1)S(1)}, bf16[512,8192]{1,0:T(8,128)(2,1)}, u32[]{:S(2)}) copy-start(bf16[512,8192]{1,0:T(8,128)(2,1)} %weight.3) | copy-start | bytes 25165828
  290.1 3.8 %copy-start.9 = (s32[4,32]{1,0:T(4,128)S(1)}, s32[4,32]{1,0:T(4,128)}, u32[]{:S(2)}) copy-start(s32[4,32]{1,0:T(4,128)} %param.19) | copy-start | bytes 1540
  290.1 24.6 %all-to-all-start.10 = ((bf16[16,336,128]{2,1,0:T(8,128)(2,1)}), bf16[16,336,128]{2,1,0:T(8,128)(2,1)S(1)}, u32[]{:S(2)}, u32[]{:S(2)}) async-start(bf16[16,336,128]{2,1,0:T(8,128)(2,1)} %shard_map.136), calls=%async_computation.10 | async-start | bytes 2752512 | tf_op jit(solution)/shard_map/all_to_all | solution.py:258
  314.7 3.4 %copy-start.4 = (bf16[512,8192]{1,0:T(8,128)(2,1)S(1)}, bf16[512,8192]{1,0:T(8,128)(2,1)}, u32[]{:S(2)}) copy-start(bf16[512,8192]{1,0:T(8,128)(2,1)} %weight.3) | copy-start | bytes 25165828
  321.7 10.8 %all-to-all-start.11 = ((bf16[8,16,512]{2,1,0:T(8,128)(2,1)}), bf16[8,16,512]{2,1,0:T(8,128)(2,1)S(1)}, u32[]{:S(2)}, u32[]{:S(2)}) async-start(bf16[8,16,512]{2,1,0:T(8,128)(2,1)} %bitcast.14), calls=%async_computation.11 | async-start | bytes 262144 | tf_op jit(solution)/shard_map/all_to_all | solution.py:258

commit v3 on v2

--- a/solution.py
+++ b/solution.py
@@ -14,6 +14,8 @@
 HALF = LIVE // 2
 FB = 896
 NF = 8
+ROW_TILES = HALF // 8
+COL_TILES = FB // 128
 COLS = 8192
 TILES = COLS // 128
 BLOCK = 2048
@@ -21,6 +23,7 @@
 SENDERS = 4
 STEPS = 32767.0 / 32768.0
 EPS = 1e-05
+WEIGHT_COPIES = 4
 f32 = jnp.float32
 bf16 = jnp.bfloat16
 VMEM_LIMIT = 16 * 1024 * 1024
@@ -44,7 +47,23 @@
     return high, (column - high).astype(bf16).astype(f32)
 
 
-def prep_kernel(count, index, keep, tokens, rows, kept, section, slots):
+def prep_kernel(
+    count, index_in, keep_in, buckets_in, tokens_in, gain_in, weight_in,
+    rows, kept, planes, exits_here, slots, bucket, gain, weight,
+    index, keep, buckets, tokens, small, large,
+):
+    depth = weight.shape[0] // WEIGHT_COPIES
+    copies = [
+        pltpu.make_async_copy(weight_in.at[pl.ds(n * depth, depth)], weight.at[pl.ds(n * depth, depth)], large.at[n])
+        for n in range(WEIGHT_COPIES)
+    ]
+    pairs = ((index_in, index), (keep_in, keep), (buckets_in, buckets), (tokens_in, tokens), (gain_in, gain))
+    fetches = [pltpu.make_async_copy(*pair, small.at[n]) for n, pair in enumerate(pairs)]
+    for copy in fetches + copies:
+        copy.start()
+    for copy in fetches:
+        copy.wait()
+    here = lax.axis_index("section")
     lane = iota((1, 4 * XS), 1)
     own = lane // XS
     place = lane % XS
@@ -56,35 +75,59 @@
         start = start + count[s]
     hit = iota((LIVE, 4 * XS), 0) == position
     pick = jnp.where(hit, 1.0, 0.0)
-    token = jnp.sum(pick * index[...].astype(f32), axis=1, keepdims=True).astype(jnp.int32)
+    flat = jnp.concatenate([index[s : s + 1, :] for s in range(4)], axis=1)
+    token = jnp.sum(pick * flat.astype(f32), axis=1, keepdims=True).astype(jnp.int32)
     chosen = jnp.where(iota((LIVE, 128), 1) == token, 1.0, 0.0)
     rows[...] = jnp.dot(chosen.astype(bf16), tokens[...], preferred_element_type=f32).astype(bf16)
-    flag = jnp.sum(chosen * keep[...].astype(f32), axis=1, keepdims=True)
+    flag = jnp.sum(chosen * keep[pl.ds(here, 1), :].astype(f32), axis=1, keepdims=True)
     kept[...] = jnp.broadcast_to(flag, kept.shape)
-    which = jnp.sum(pick * own.astype(f32), axis=1, keepdims=True)
-    section[...] = jnp.broadcast_to(which, section.shape)
+    planes[...] = jnp.where(iota((8, 128), 0) == here, 1.0, 0.0)
+    mine = jnp.sum(jnp.where(own == here, pick, 0.0), axis=1, keepdims=True)
+    exits_here[...] = jnp.broadcast_to(mine, exits_here.shape)
     slots[...] = pick
+    bucket[...] = jnp.concatenate([buckets[s : s + 1, :] for s in range(4)], axis=1)
+    for copy in copies:
+        copy.wait()
 
 
 def up_kernel(state, gain, weight, out):
     wide = state[...].astype(f32)
     normed = (wide * gain[...].astype(f32)).astype(bf16)
     high, low = split_sum(jnp.sum(wide * wide, axis=1, keepdims=True))
-    lane = iota((LIVE, 128), 1)
-    extra = jnp.where(lane == 0, high, jnp.where(lane == 1, low, 0.0))
+    lane = iota((8, 128), 1)
+    for t in range(2):
+        extra = jnp.zeros((8, 128), f32)
+        for r in range(ROW_TILES):
+            at = t * HALF + r * 8
+            extra = jnp.where(lane == 2 * r, high[at : at + 8], extra)
+            extra = jnp.where(lane == 2 * r + 1, low[at : at + 8], extra)
+        for f in range(NF):
+            out[t * NF + f, ROW_TILES * COL_TILES] = extra.astype(bf16)
     for f in range(NF):
         part = jnp.dot(normed, weight[:, f * FB : (f + 1) * FB], preferred_element_type=f32)
         for t in range(2):
-            out[t, f, :, :FB] = part[t * HALF : (t + 1) * HALF].astype(bf16)
-            out[t, f, :, FB:] = extra[t * HALF : (t + 1) * HALF].astype(bf16)
+            for r in range(ROW_TILES):
+                at = t * HALF + r * 8
+                for c in range(COL_TILES):
+                    tile = part[at : at + 8, c * 128 : (c + 1) * 128]
+                    out[t * NF + f, r * COL_TILES + c] = tile.astype(bf16)
 
 
 def mid_kernel(parts, out):
-    total = parts[0].astype(f32)
-    for j in range(1, DP):
-        total = total + parts[j].astype(f32)
-    scale = lax.rsqrt((total[:, FB : FB + 1] + total[:, FB + 1 : FB + 2]) / D + EPS)
-    active = jax.nn.silu(total[:, :FB] * scale).astype(bf16)
+    def total(tile):
+        value = parts[0, tile].astype(f32)
+        for j in range(1, DP):
+            value = value + parts[j, tile].astype(f32)
+        return value
+
+    squares = total(ROW_TILES * COL_TILES)
+    rows = []
+    for r in range(ROW_TILES):
+        square = squares[:, 2 * r : 2 * r + 1] + squares[:, 2 * r + 1 : 2 * r + 2]
+        scale = lax.rsqrt(square / D + EPS)
+        tiles = [jax.nn.silu(total(r * COL_TILES + c) * scale) for c in range(COL_TILES)]
+        rows.append(jnp.concatenate(tiles, axis=1))
+    active = jnp.concatenate(rows, axis=0).astype(bf16)
     for j in range(DP):
         out[j] = active
 
@@ -99,12 +142,22 @@
     out[...] = total * kept[:, :1]
 
 
+def finish_kernel(state, lowered, other, first, second, third, planes, exits_here, held):
+    result = (state[...].astype(f32) + (lowered[...] + other[...])).astype(bf16)
+    mine = jnp.zeros((LIVE, 512), f32)
+    for s, value in enumerate((first[...], second[...], third[...], result)):
+        mine = mine + value.astype(f32) * planes[s : s + 1, :1]
+    held[0] = (mine * exits_here[:, :1]).astype(bf16)
+    held[1] = (result.astype(f32) * planes[3:4, :1]).astype(bf16)
+
+
 def power_above(value):
     return jnp.ceil(jnp.log2(jnp.maximum(value, 1e-30)))
 
 
-def head_kernel(exits, finals, gain, weight, out, parts):
-    wide = jnp.concatenate([exits[...].astype(f32), finals[...].astype(f32)], axis=0)
+def head_kernel(held, one, two, three, gain, weight, out, parts):
+    total = held[...].astype(f32) + one[...].astype(f32) + two[...].astype(f32) + three[...].astype(f32)
+    wide = total.reshape(2 * LIVE, 512)
     headed = (wide * gain[...].astype(f32)).astype(bf16)
     peak = jnp.zeros((2 * LIVE, BLOCK), f32)
     for k in range(BLOCKS):
@@ -242,8 +295,16 @@
     extra = gaps[:, PAIRS * TILES :, :].astype(f32)[:, :PAIRS, :].reshape(LIVE, 128)
     kl = jnp.sum(extra, axis=1, keepdims=True)
     by_slot = jnp.sum(pick * kl, axis=0, keepdims=True)
-    kl_out[...] = jnp.broadcast_to(by_slot, (8, 128))
-    mine = jnp.where(iota((8, 128), 1) // XS == iota((8, 128), 0), by_slot, 0.0)
+    first = lax.axis_index("dp") * 8
+    own = jnp.where(iota((8, 128), 1) == iota((8, 128), 0) + first, 1.0, 0.0)
+    kl_out[...] = lax.dot_general(
+        by_slot,
+        own,
+        (((1,), (1,)), ((), ())),
+        preferred_element_type=f32,
+        precision=lax.Precision.HIGHEST,
+    )
+    mine = jnp.where(iota((4, 128), 1) // XS == iota((4, 128), 0), by_slot, 0.0)
     hot = jnp.where(iota((NB, 128), 0) == buckets[...], 1.0, 0.0)
     hist[...] = lax.dot_general(
         mine,
@@ -258,37 +319,54 @@
     return lax.all_to_all(value, axis, 0, 0)
 
 
+def around(value, by):
+    count = lax.axis_size("section")
+    return lax.ppermute(value, "section", [(i, (i + by) % count) for i in range(count)])
+
+
 def shards(
     tokens, keep, norm_gain, w_up, w_down, head_gain, w_head, exit_idx, exit_count, kl_bucket
 ):
     sections = lax.axis_size("section")
-    section_id = lax.axis_index("section")
-    up_local = pltpu.with_memory_space_constraint(w_up[0], pltpu.VMEM)
     down_local = pltpu.with_memory_space_constraint(w_down[0], pltpu.VMEM)
     head_local = pltpu.with_memory_space_constraint(w_head, pltpu.VMEM)
-    keep_mine = lax.dynamic_slice_in_dim(keep, section_id, 1, 0)
     shape = jax.ShapeDtypeStruct
     vmem = pl.BlockSpec(memory_space=pltpu.VMEM)
-    current, kept, section_of, slots = call(
+    far = pl.BlockSpec(memory_space=pltpu.HBM)
+    fetched = (exit_idx, keep, kl_bucket, tokens, norm_gain, w_up[0])
+    current, kept, planes, exits_here, slots, bucket, gain, up_local = call(
         prep_kernel,
         (
             shape((LIVE, 512), bf16),
             shape((LIVE, 128), f32),
+            shape((8, 128), f32),
             shape((LIVE, 128), f32),
             shape((LIVE, 128), f32),
+            shape((1, 128), jnp.int32),
+            shape((1, 512), bf16),
+            pltpu.VMEM(w_up.shape[1:], bf16),
         ),
-        in_specs=[pl.BlockSpec(memory_space=pltpu.SMEM), vmem, vmem, vmem],
-        out_specs=[vmem] * 4,
-    )(exit_count, exit_idx.reshape(1, -1), keep_mine, tokens)
-    mine = current
+        in_specs=[pl.BlockSpec(memory_space=pltpu.SMEM)] + [far] * 6,
+        out_specs=[vmem] * 8,
+        scratch_shapes=[
+            pltpu.VMEM((4, XS), jnp.int32),
+            pltpu.VMEM((4, 128), jnp.int32),
+            pltpu.VMEM((4, XS), jnp.int32),
+            pltpu.VMEM((128, 512), bf16),
+            pltpu.SemaphoreType.DMA((5,)),
+            pltpu.SemaphoreType.DMA((WEIGHT_COPIES,)),
+        ],
+    )(exit_count, *[pltpu.with_memory_space_constraint(x, pltpu.HBM) for x in fetched])
+    up_local = pltpu.with_memory_space_constraint(up_local, pltpu.VMEM)
+    results = []
     for step in range(sections):
         parts = call(
             up_kernel,
-            shape((2, NF, HALF, FB + 128), bf16),
+            shape((DP, ROW_TILES * COL_TILES + 1, 8, 128), bf16),
             in_specs=[vmem] * 3,
             out_specs=vmem,
-        )(current, norm_gain, up_local)
-        parts = exchange(parts.reshape(DP, HALF, FB + 128), "dp")
+        )(current, gain, up_local)
+        parts = exchange(parts, "dp")
         active = call(
             mid_kernel, shape((DP, HALF, FB), bf16), in_specs=[vmem], out_specs=vmem
         )(parts)
@@ -297,25 +375,22 @@
             down_kernel, shape((LIVE, 512), f32), in_specs=[vmem] * 3, out_specs=vmem
         )(active.reshape(2, NF, HALF, FB), down_local, kept)
         other = lax.ppermute(lowered, "mp", [(0, 1), (1, 0)])
-        result = (current.astype(f32) + (lowered + other)).astype(bf16)
-        mine = jnp.where(section_id == step, result, mine)
         if step < sections - 1:
-            current = lax.ppermute(result, "section", [(i, i + 1) for i in range(sections - 1)])
-    zero = jnp.zeros_like(mine)
-    own_exit = jnp.where(section_of[:, :1] == section_id.astype(f32), mine, zero)
-    own_final = jnp.where(section_id == sections - 1, mine, zero)
-    held = jnp.stack([own_exit, own_final])
-    spread = held
-    for k in range(1, sections):
-        spread = spread + lax.ppermute(held, "section", [(i, (i + k) % sections) for i in range(sections)])
+            result = (current.astype(f32) + (lowered + other)).astype(bf16)
+            results.append(result)
+            current = around(result, 1)
+    held = call(
+        finish_kernel, shape((2, LIVE, 512), bf16), in_specs=[vmem] * 8, out_specs=vmem
+    )(current, lowered, other, *results, planes, exits_here)
+    spread = [around(held, k) for k in (2, 1, 3)]
     extent = 2 * PAIRS * TILES + 16
     parts = call(
         head_kernel,
         shape((DP, extent, 128), jnp.int16),
-        in_specs=[vmem] * 4,
+        in_specs=[vmem] * 6,
         out_specs=vmem,
         scratch_shapes=[pltpu.VMEM((BLOCKS, 2 * LIVE, BLOCK), f32)],
-    )(spread[0], spread[1], head_gain.reshape(1, -1), head_local)
+    )(held, *spread, head_gain.reshape(1, -1), head_local)
     parts = exchange(parts, "dp")
     logits, stats = call(
         peak_kernel,
@@ -336,14 +411,13 @@
     gaps = exchange(gaps, "dp")
     feature, kl, hist = call(
         grad_kernel,
-        (shape((128, 512), bf16), shape((8, 128), f32), shape((8, NB), f32)),
+        (shape((128, 512), bf16), shape((1, 8), f32), shape((4, NB), f32)),
         in_specs=[vmem] * 4,
         out_specs=[vmem] * 3,
-    )(gaps, head_local, slots, kl_bucket.reshape(1, -1))
+    )(gaps, head_local, slots, bucket)
     feature = exchange(feature.reshape(8, 16, 512), ("section", "mp"))
     feature_grad = jnp.sum(feature.astype(f32), axis=0)
-    kl_here = lax.dynamic_slice_in_dim(kl[0], lax.axis_index("dp") * 8, 8, 0)
-    return (feature_grad, kl_here, hist[:4])
+    return (feature_grad, kl.reshape(8), hist)
 
 
 def solution(mesh):

time: 334 us -> 310 us (0.928)
  blocking collectives: 214 us -> 238 us
  starting transfers between devices: 40.1 us -> 18.7 us
  waiting for transfers between devices: 39.5 us -> 25.4 us
  local copies, waits for them, and re-layouts: 14.1 us -> 0.68 us
    all_to_all x2 -> x0, waiting for transfers between devices: 24.8 us -> none  [exchange(): return lax.all_to_all(value, axis, 0, 0)]
    all_to_all x10 -> x12, blocking collectives: 214 us -> 238 us  [exchange(): return lax.all_to_all(value, axis, 0, 0)]
    ppermute x6, starting transfers between devices: 17.4 us -> 4.26 us  [around(): lax.ppermute(value, 'section', [(i, (i + by) % count) for i in range(coun...]
    unnamed x26 -> x12, local copies, waits for them, and re-layouts: 12.1 us -> 0.68 us
    ppermute x6, waiting for transfers between devices: 10.7 us -> 21.3 us  [around(): lax.ppermute(value, 'section', [(i, (i + by) % count) for i in range(coun...]
    all_to_all x2 -> x0, starting transfers between devices: 9.3 us -> none  [exchange(): return lax.all_to_all(value, axis, 0, 0)]
    pallas_call x5 -> x6, Pallas kernels: 8.71 us -> 8.8 us  [the longest x4 5.13 us: shards(): call(up_kernel, shape((DP, ROW_TILES * COL_TILES + 1, 8, 128), bf16), in_...]
  transfers between devices with their start and end apart: 12 -> 10, of which waited for: 11 -> 9; matrix products, arithmetic and copies ran while one was open for 0% -> 0% of each run, Pallas kernels for 0% -> 0%
where the time goes in v3:
time: 310 us
  blocking collectives  238 us (77%)
  waiting for transfers between devices  25.4 us (8%)
  Pallas kernels  25.3 us (8%)
  starting transfers between devices  18.7 us (6%)
    all_to_all x12, blocking collectives, exchange(): return lax.all_to_all(value, axis, 0, 0)  238 us
    ppermute x6, waiting for transfers between devices, around(): lax.ppermute(value, 'section', [(i, (i + by) % count) for i in range(coun...  21.3 us
    ppermute x4, starting transfers between devices, shards(): other = lax.ppermute(lowered, 'mp', [(0, 1), (1, 0)])  14.5 us
  transfers between devices with their start and end apart: 10, of which 9 were waited for; matrix products, arithmetic and copies ran while one was open for 0% of the time, Pallas kernels for 0%

profile of v3, /device:TPU:1, one launch (start us, length us, event | category | flops | bytes accessed | tf_op | source)
XLA Modules:
  0.0 310.0 jit_solution(7727924909212259668)
XLA Ops:
  0.6 0.0 copy-start
  0.6 0.6 copy-done
  1.3 3.9 %shard_map.121 = (bf16[80,512]{1,0:T(8,128)(2,1)S(1)}, f32[80,128]{1,0:T(8,128)S(1)}, f32[8,128]{1,0:T(8,128)S(1)}, f32[80,128]{1,0:T(8,128)S(1)}, f32[80,128]{1...) custom-call(s32[4]{0:T(128)S(1)} %copy-done, s32[4,32]{1,0:T(4,128)} %index_in.1, ...), custom_call_target="tpu_custom_call" | custom-call | tf_op jit(solution)/shard_map/pallas_call | solution.py:337
  5.2 0.0 slice-start
  5.2 0.0 slice-start.1
  5.2 1.3 shard_map.122
  6.5 26.1 %all_to_all.60.parts = bf16[16,36,8,128]{3,2,1,0:T(8,128)(2,1)S(1)} all-to-all(bf16[16,36,8,128]{3,2,1,0:T(8,128)(2,1)S(1)} %shard_map.122), channel_id=1, replica_groups=mesh['section'=4,'dp'=16,'mp'=2] {'dp'}, dimensions={0} | all-to-all | bytes 2359296 | tf_op jit(solution)/shard_map/all_to_all | solution.py:319
  32.6 0.3 shard_map.123
  32.9 19.5 %all_to_all.61 = bf16[16,40,896]{2,1,0:T(8,128)(2,1)S(1)} all-to-all(bf16[16,40,896]{2,1,0:T(8,128)(2,1)S(1)} %shard_map.123), channel_id=1, replica_groups=mesh['section'=4,'dp'=16,'mp'=2] {'dp'}, dimensions={0} | all-to-all | bytes 2293760 | tf_op jit(solution)/shard_map/all_to_all | solution.py:319
  52.3 0.0 slice-done
  52.3 0.0 slice-done.1
  52.3 1.4 shard_map.124
  53.8 3.1 %collective-permute-start = (f32[80,512]{1,0:T(8,128)S(1)}, f32[80,512]{1,0:T(8,128)S(1)}, u32[]{:S(2)}, u32[]{:S(2)}) collective-permute-start(f32[80,512]{1,0:T(8,128)S(1)} %shard_map.124), channel_id=1, source_target_pairs={{0,1},{1,0},{2,3},{3,2},{4,5},{5,4},{6,7},{7,6},{8,9},{9,8},{10,11... | collective-permute-start | bytes 491528 | tf_op jit(solution)/shard_map/ppermute | solution.py:377
  56.9 1.0 collective-permute-done
  58.0 1.3 collective-permute-start.1
  59.2 3.7 %collective-permute-done.1.state = bf16[80,512]{1,0:T(8,128)(2,1)S(1)} collective-permute-done((bf16[80,512]{1,0:T(8,128)(2,1)S(1)}, bf16[80,512]{1,0:T(8,128)(2,1)S(1)}, u32[]{:S(2)}, u32[]{:S(2)}) %collective-permute-start.1) | collective-permute-done | bytes 81952 | tf_op jit(solution)/shard_map/ppermute | solution.py:324
  62.9 1.3 shard_map.125
  64.2 19.9 %all_to_all.62.parts = bf16[16,36,8,128]{3,2,1,0:T(8,128)(2,1)S(1)} all-to-all(bf16[16,36,8,128]{3,2,1,0:T(8,128)(2,1)S(1)} %shard_map.125), channel_id=1, replica_groups=mesh['section'=4,'dp'=16,'mp'=2] {'dp'}, dimensions={0} | all-to-all | bytes 2359296 | tf_op jit(solution)/shard_map/all_to_all | solution.py:319
  84.1 0.3 shard_map.126
  84.4 18.2 %all_to_all.63 = bf16[16,40,896]{2,1,0:T(8,128)(2,1)S(1)} all-to-all(bf16[16,40,896]{2,1,0:T(8,128)(2,1)S(1)} %shard_map.126), channel_id=1, replica_groups=mesh['section'=4,'dp'=16,'mp'=2] {'dp'}, dimensions={0} | all-to-all | bytes 2293760 | tf_op jit(solution)/shard_map/all_to_all | solution.py:319
  102.7 1.4 shard_map.127
  104.1 3.8 %collective-permute-start.2 = (f32[80,512]{1,0:T(8,128)S(1)}, f32[80,512]{1,0:T(8,128)S(1)}, u32[]{:S(2)}, u32[]{:S(2)}) collective-permute-start(f32[80,512]{1,0:T(8,128)S(1)} %shard_map.127), channel_id=1, source_target_pairs={{0,1},{1,0},{2,3},{3,2},{4,5},{5,4},{6,7},{7,6},{8,9},{9,8},{10,11... | collective-permute-start | bytes 491528 | tf_op jit(solution)/shard_map/ppermute | solution.py:377
  107.9 1.0 collective-permute-done.2
  108.9 0.1 collective-permute-start.3
  109.0 4.9 %collective-permute-done.3.state = bf16[80,512]{1,0:T(8,128)(2,1)S(1)} collective-permute-done((bf16[80,512]{1,0:T(8,128)(2,1)S(1)}, bf16[80,512]{1,0:T(8,128)(2,1)S(1)}, u32[]{:S(2)}, u32[]{:S(2)}) %collective-permute-start.3) | collective-permute-done | bytes 81952 | tf_op jit(solution)/shard_map/ppermute | solution.py:324
  113.9 1.3 shard_map.128
  115.2 20.0 %all_to_all.64.parts = bf16[16,36,8,128]{3,2,1,0:T(8,128)(2,1)S(1)} all-to-all(bf16[16,36,8,128]{3,2,1,0:T(8,128)(2,1)S(1)} %shard_map.128), channel_id=1, replica_groups=mesh['section'=4,'dp'=16,'mp'=2] {'dp'}, dimensions={0} | all-to-all | bytes 2359296 | tf_op jit(solution)/shard_map/all_to_all | solution.py:319
  135.1 0.3 shard_map.129
  135.5 18.2 %all_to_all.65 = bf16[16,40,896]{2,1,0:T(8,128)(2,1)S(1)} all-to-all(bf16[16,40,896]{2,1,0:T(8,128)(2,1)S(1)} %shard_map.129), channel_id=1, replica_groups=mesh['section'=4,'dp'=16,'mp'=2] {'dp'}, dimensions={0} | all-to-all | bytes 2293760 | tf_op jit(solution)/shard_map/all_to_all | solution.py:319
  153.7 1.4 shard_map.130
  155.1 3.8 %collective-permute-start.4 = (f32[80,512]{1,0:T(8,128)S(1)}, f32[80,512]{1,0:T(8,128)S(1)}, u32[]{:S(2)}, u32[]{:S(2)}) collective-permute-start(f32[80,512]{1,0:T(8,128)S(1)} %shard_map.130), channel_id=1, source_target_pairs={{0,1},{1,0},{2,3},{3,2},{4,5},{5,4},{6,7},{7,6},{8,9},{9,8},{10,11... | collective-permute-start | bytes 491528 | tf_op jit(solution)/shard_map/ppermute | solution.py:377
  158.9 1.0 collective-permute-done.4
  160.0 0.1 collective-permute-start.5
  160.1 4.9 %collective-permute-done.5.state = bf16[80,512]{1,0:T(8,128)(2,1)S(1)} collective-permute-done((bf16[80,512]{1,0:T(8,128)(2,1)S(1)}, bf16[80,512]{1,0:T(8,128)(2,1)S(1)}, u32[]{:S(2)}, u32[]{:S(2)}) %collective-permute-start.5) | collective-permute-done | bytes 81952 | tf_op jit(solution)/shard_map/ppermute | solution.py:324
  164.9 1.3 shard_map.131
  166.2 0.0 slice-start.2
  166.2 20.2 %all_to_all.66.parts = bf16[16,36,8,128]{3,2,1,0:T(8,128)(2,1)S(1)} all-to-all(bf16[16,36,8,128]{3,2,1,0:T(8,128)(2,1)S(1)} %shard_map.131), channel_id=1, replica_groups=mesh['section'=4,'dp'=16,'mp'=2] {'dp'}, dimensions={0} | all-to-all | bytes 2359296 | tf_op jit(solution)/shard_map/all_to_all | solution.py:319
  186.5 0.3 shard_map.132
  186.8 18.4 %all_to_all.67 = bf16[16,40,896]{2,1,0:T(8,128)(2,1)S(1)} all-to-all(bf16[16,40,896]{2,1,0:T(8,128)(2,1)S(1)} %shard_map.132), channel_id=1, replica_groups=mesh['section'=4,'dp'=16,'mp'=2] {'dp'}, dimensions={0} | all-to-all | bytes 2293760 | tf_op jit(solution)/shard_map/all_to_all | solution.py:319
  205.2 0.0 copy-start.1
  205.2 0.0 slice-start.3
  205.2 1.4 shard_map.133.lowered
  206.7 3.8 %collective-permute-start.6 = (f32[80,512]{1,0:T(8,128)S(1)}, f32[80,512]{1,0:T(8,128)S(1)}, u32[]{:S(2)}, u32[]{:S(2)}) collective-permute-start(f32[80,512]{1,0:T(8,128)S(1)} %shard_map.133.lowered), channel_id=1, source_target_pairs={{0,1},{1,0},{2,3},{3,2},{4,5},{5,4},{6,7},{7,6},{8,9},{9,8},{10,11... | collective-permute-start | bytes 491528 | tf_op jit(solution)/shard_map/ppermute | solution.py:377
  210.4 1.0 collective-permute-done.6.other
  211.5 0.1 shard_map.134.held
  211.6 0.1 collective-permute-start.7
  211.7 0.1 collective-permute-start.8
  211.8 2.7 collective-permute-start.9
  214.4 0.0 copy-done.1
  214.4 4.2 %collective-permute-done.7.one = bf16[2,80,512]{2,1,0:T(8,128)(2,1)S(1)} collective-permute-done((bf16[2,80,512]{2,1,0:T(8,128)(2,1)S(1)}, bf16[2,80,512]{2,1,0:T(8,128)(2,1)S(1)}, u32[]{:S(2)}, u32[]{:S(2)}) %collective-permute-start.7) | collective-permute-done | bytes 163872 | tf_op jit(solution)/shard_map/ppermute | solution.py:324
  218.6 3.7 %collective-permute-done.8.two = bf16[2,80,512]{2,1,0:T(8,128)(2,1)S(1)} collective-permute-done((bf16[2,80,512]{2,1,0:T(8,128)(2,1)S(1)}, bf16[2,80,512]{2,1,0:T(8,128)(2,1)S(1)}, u32[]{:S(2)}, u32[]{:S(2)}) %collective-permute-start.8) | collective-permute-done | bytes 163872 | tf_op jit(solution)/shard_map/ppermute | solution.py:324
  222.4 0.0 collective-permute-done.9.three
  222.4 0.0 slice-done.2
  222.4 0.0 slice-done.3
  222.4 4.0 %shard_map.135 = s16[16,656,128]{2,1,0:T(8,128)(2,1)S(1)} custom-call(bf16[2,80,512]{2,1,0:T(8,128)(2,1)S(1)} %shard_map.134.held, bf16[2,80,512]{2,1,0:T(8,128)(2,1)S(1)} %collective-permute-done.7.one, bf16[2,80,512]{2,1,0:T(8,128)(2,1)S(1)} %collective-permute-done.8.two, bf16[2,80,512]{2,1,0:T(8,128)(2,1)S(1)} %collective-permute-done.9.three, ...), custom_call_target="tpu_custom_call" | custom-call | tf_op jit(solution)/shard_map/pallas_call | solution.py:387
  226.4 36.6 %all_to_all.68.parts = s16[16,656,128]{2,1,0:T(8,128)(2,1)S(1)} all-to-all(s16[16,656,128]{2,1,0:T(8,128)(2,1)S(1)} %shard_map.135), channel_id=1, replica_groups=mesh['section'=4,'dp'=16,'mp'=2] {'dp'}, dimensions={0} | all-to-all | bytes 5373952 | tf_op jit(solution)/shard_map/all_to_all | solution.py:319
  263.0 1.3 shard_map.136
  264.3 9.0 %all_to_all.69.stats = f32[8,8,128]{2,1,0:T(8,128)S(1)} all-to-all(f32[8,8,128]{2,1,0:T(8,128)S(1)} %get-tuple-element.23), channel_id=1, replica_groups=mesh['section'=4,'dp'=16,'mp'=2] {'section','mp'}, dimensions={0} | all-to-all | bytes 65536 | tf_op jit(solution)/shard_map/all_to_all | solution.py:319
  273.4 0.3 shard_map.137
  273.7 22.6 %all_to_all.70.gaps = bf16[16,336,128]{2,1,0:T(8,128)(2,1)S(1)} all-to-all(bf16[16,336,128]{2,1,0:T(8,128)(2,1)S(1)} %shard_map.137), channel_id=1, replica_groups=mesh['section'=4,'dp'=16,'mp'=2] {'dp'}, dimensions={0} | all-to-all | bytes 2752512 | tf_op jit(solution)/shard_map/all_to_all | solution.py:319
  296.2 3.5 %shard_map.138 = (bf16[128,512]{1,0:T(8,128)(2,1)S(1)}, f32[1,8]{1,0:T(1,128)}, f32[4,16]{1,0:T(4,128)}) custom-call(bf16[16,336,128]{2,1,0:T(8,128)(2,1)S(1)} %all_to_all.70.gaps, bf16[512,8192]{1,0:T(8,128)(2,1)S(1)} %bitcast.15, f32[80,128]{1,0:T(8,128)S(1)} %get-tuple-element.24.slots, s32[1,128]{1,0:T(1,128)S(1)} %get-tuple-element.25.buckets), custom_call_target="tpu_custom_call" | custom-call | tf_op jit(solution)/shard_map/pallas_call | solution.py:412
  299.8 9.5 %all_to_all.71 = bf16[8,16,512]{2,1,0:T(8,128)(2,1)S(1)} all-to-all(bf16[8,16,512]{2,1,0:T(8,128)(2,1)S(1)} %bitcast.20), channel_id=1, replica_groups=mesh['section'=4,'dp'=16,'mp'=2] {'section','mp'}, dimensions={0} | all-to-all | bytes 262144 | tf_op jit(solution)/shard_map/all_to_all | solution.py:319
  309.3 0.6 convert_reduce_fusion
  (6 shorter events, 0.1 us)
Async XLA Ops:
  0.6 0.7 copy-start
  5.2 47.2 %slice-start = ((s8[7340032]{0:T(1024)(128)(4,1)}), s8[4194304]{0:T(1024)(128)(4,1)S(1)}, s32[]{:S(2)}) async-start(s8[7340032]{0:T(1024)(128)(4,1)} %bitcast.8), calls=%async_computation.12 | async-start | bytes 8388608
  5.2 47.2 %slice-start.1 = ((s8[7340032]{0:T(1024)(128)(4,1)}), s8[3145728]{0:T(1024)(128)(4,1)S(1)}, s32[]{:S(2)}) async-start(s8[7340032]{0:T(1024)(128)(4,1)} %bitcast.8), calls=%async_computation.13 | async-start | bytes 6291456
  53.8 4.1 %collective-permute-start = (f32[80,512]{1,0:T(8,128)S(1)}, f32[80,512]{1,0:T(8,128)S(1)}, u32[]{:S(2)}, u32[]{:S(2)}) collective-permute-start(f32[80,512]{1,0:T(8,128)S(1)} %shard_map.124), channel_id=1, source_target_pairs={{0,1},{1,0},{2,3},{3,2},{4,5},{5,4},{6,7},{7,6},{8,9},{9,8},{10,11... | collective-permute-start | bytes 491528 | tf_op jit(solution)/shard_map/ppermute | solution.py:377
  58.0 4.9 %collective-permute-start.1 = (bf16[80,512]{1,0:T(8,128)(2,1)S(1)}, bf16[80,512]{1,0:T(8,128)(2,1)S(1)}, u32[]{:S(2)}, u32[]{:S(2)}) collective-permute-start(bf16[80,512]{1,0:T(8,128)(2,1)S(1)} %add_convert_fusion.2.first), channel_id=1, source_target_pairs={{0,32},{32,64},{64,96},{96,0},{1,33},{33,65},{65,97},{97,1},{2,34}... | collective-permute-start | bytes 245768 | tf_op jit(solution)/shard_map/ppermute | solution.py:324
  104.1 4.8 %collective-permute-start.2 = (f32[80,512]{1,0:T(8,128)S(1)}, f32[80,512]{1,0:T(8,128)S(1)}, u32[]{:S(2)}, u32[]{:S(2)}) collective-permute-start(f32[80,512]{1,0:T(8,128)S(1)} %shard_map.127), channel_id=1, source_target_pairs={{0,1},{1,0},{2,3},{3,2},{4,5},{5,4},{6,7},{7,6},{8,9},{9,8},{10,11... | collective-permute-start | bytes 491528 | tf_op jit(solution)/shard_map/ppermute | solution.py:377
  108.9 4.9 %collective-permute-start.3 = (bf16[80,512]{1,0:T(8,128)(2,1)S(1)}, bf16[80,512]{1,0:T(8,128)(2,1)S(1)}, u32[]{:S(2)}, u32[]{:S(2)}) collective-permute-start(bf16[80,512]{1,0:T(8,128)(2,1)S(1)} %add_convert_fusion.1.second), channel_id=1, source_target_pairs={{0,32},{32,64},{64,96},{96,0},{1,33},{33,65},{65,97},{97,1},{2,34}... | collective-permute-start | bytes 245768 | tf_op jit(solution)/shard_map/ppermute | solution.py:324
  155.1 4.8 %collective-permute-start.4 = (f32[80,512]{1,0:T(8,128)S(1)}, f32[80,512]{1,0:T(8,128)S(1)}, u32[]{:S(2)}, u32[]{:S(2)}) collective-permute-start(f32[80,512]{1,0:T(8,128)S(1)} %shard_map.130), channel_id=1, source_target_pairs={{0,1},{1,0},{2,3},{3,2},{4,5},{5,4},{6,7},{7,6},{8,9},{9,8},{10,11... | collective-permute-start | bytes 491528 | tf_op jit(solution)/shard_map/ppermute | solution.py:377
  160.0 4.9 %collective-permute-start.5 = (bf16[80,512]{1,0:T(8,128)(2,1)S(1)}, bf16[80,512]{1,0:T(8,128)(2,1)S(1)}, u32[]{:S(2)}, u32[]{:S(2)}) collective-permute-start(bf16[80,512]{1,0:T(8,128)(2,1)S(1)} %add_convert_fusion.third), channel_id=1, source_target_pairs={{0,32},{32,64},{64,96},{96,0},{1,33},{33,65},{65,97},{97,1},{2,34}... | collective-permute-start | bytes 245768 | tf_op jit(solution)/shard_map/ppermute | solution.py:324
  166.2 56.2 %slice-start.2 = ((s8[8388608]{0:T(1024)(128)(4,1)}), s8[4194304]{0:T(1024)(128)(4,1)S(1)}, s32[]{:S(2)}) async-start(s8[8388608]{0:T(1024)(128)(4,1)} %bitcast.14), calls=%async_computation.14 | async-start | bytes 8388608
  205.2 9.2 %copy-start.1 = (bf16[512]{0:T(512)(128)(2,1)S(1)}, bf16[512]{0:T(512)(128)(2,1)}, u32[]{:S(2)}) copy-start(bf16[512]{0:T(512)(128)(2,1)} %param.15) | copy-start | bytes 3076
  205.2 17.2 %slice-start.3 = ((s8[8388608]{0:T(1024)(128)(4,1)}), s8[4194304]{0:T(1024)(128)(4,1)S(1)}, s32[]{:S(2)}) async-start(s8[8388608]{0:T(1024)(128)(4,1)} %bitcast.14), calls=%async_computation.15 | async-start | bytes 8388608
  206.7 4.8 %collective-permute-start.6 = (f32[80,512]{1,0:T(8,128)S(1)}, f32[80,512]{1,0:T(8,128)S(1)}, u32[]{:S(2)}, u32[]{:S(2)}) collective-permute-start(f32[80,512]{1,0:T(8,128)S(1)} %shard_map.133.lowered), channel_id=1, source_target_pairs={{0,1},{1,0},{2,3},{3,2},{4,5},{5,4},{6,7},{7,6},{8,9},{9,8},{10,11... | collective-permute-start | bytes 491528 | tf_op jit(solution)/shard_map/ppermute | solution.py:377
  211.6 7.0 %collective-permute-start.7 = (bf16[2,80,512]{2,1,0:T(8,128)(2,1)S(1)}, bf16[2,80,512]{2,1,0:T(8,128)(2,1)S(1)}, u32[]{:S(2)}, u32[]{:S(2)}) collective-permute-start(bf16[2,80,512]{2,1,0:T(8,128)(2,1)S(1)} %shard_map.134.held), channel_id=1, source_target_pairs={{0,64},{32,96},{64,0},{96,32},{1,65},{33,97},{65,1},{97,33},{2,66}... | collective-permute-start | bytes 491528 | tf_op jit(solution)/shard_map/ppermute | solution.py:324
  211.7 10.7 %collective-permute-start.8 = (bf16[2,80,512]{2,1,0:T(8,128)(2,1)S(1)}, bf16[2,80,512]{2,1,0:T(8,128)(2,1)S(1)}, u32[]{:S(2)}, u32[]{:S(2)}) collective-permute-start(bf16[2,80,512]{2,1,0:T(8,128)(2,1)S(1)} %shard_map.134.held), channel_id=1, source_target_pairs={{0,32},{32,64},{64,96},{96,0},{1,33},{33,65},{65,97},{97,1},{2,34}... | collective-permute-start | bytes 491528 | tf_op jit(solution)/shard_map/ppermute | solution.py:324
  211.8 10.6 %collective-permute-start.9 = (bf16[2,80,512]{2,1,0:T(8,128)(2,1)S(1)}, bf16[2,80,512]{2,1,0:T(8,128)(2,1)S(1)}, u32[]{:S(2)}, u32[]{:S(2)}) collective-permute-start(bf16[2,80,512]{2,1,0:T(8,128)(2,1)S(1)} %shard_map.134.held), channel_id=1, source_target_pairs={{0,96},{32,0},{64,32},{96,64},{1,97},{33,1},{65,33},{97,65},{2,98}... | collective-permute-start | bytes 491528 | tf_op jit(solution)/shard_map/ppermute | solution.py:324

commit v4 on v3

--- a/solution.py
+++ b/solution.py
@@ -1,3 +1,5 @@
+import functools
+
 import jax
 import jax.numpy as jnp
 from jax import lax
@@ -10,18 +12,20 @@
 NB = 16
 LIVE = 80
 DP = 16
+ORDER = (2, 1, 3)
+ARRIVAL = (3, 1, 2)
 PAIRS = LIVE // DP
-HALF = LIVE // 2
-FB = 896
-NF = 8
-ROW_TILES = HALF // 8
-COL_TILES = FB // 128
+QUARTER = 1792
+ROW_TILES = LIVE // 8
+COL_TILES = QUARTER // 128
+TILE_COUNT = ROW_TILES * COL_TILES
 COLS = 8192
 TILES = COLS // 128
 BLOCK = 2048
 BLOCKS = COLS // BLOCK
 SENDERS = 4
-STEPS = 32767.0 / 32768.0
+STEPS = 32760.0 / 32768.0
+ROUND = 1.5 * 2.0**23
 EPS = 1e-05
 WEIGHT_COPIES = 4
 f32 = jnp.float32
@@ -49,7 +53,7 @@
 
 def prep_kernel(
     count, index_in, keep_in, buckets_in, tokens_in, gain_in, weight_in,
-    rows, kept, planes, exits_here, slots, bucket, gain, weight,
+    rows, kept, planes, slots, bucket, gain, weight,
     index, keep, buckets, tokens, small, large,
 ):
     depth = weight.shape[0] // WEIGHT_COPIES
@@ -82,82 +86,109 @@
     flag = jnp.sum(chosen * keep[pl.ds(here, 1), :].astype(f32), axis=1, keepdims=True)
     kept[...] = jnp.broadcast_to(flag, kept.shape)
     planes[...] = jnp.where(iota((8, 128), 0) == here, 1.0, 0.0)
-    mine = jnp.sum(jnp.where(own == here, pick, 0.0), axis=1, keepdims=True)
-    exits_here[...] = jnp.broadcast_to(mine, exits_here.shape)
     slots[...] = pick
     bucket[...] = jnp.concatenate([buckets[s : s + 1, :] for s in range(4)], axis=1)
     for copy in copies:
         copy.wait()
 
 
-def up_kernel(state, gain, weight, out):
+def place_along(first):
+    place = lax.axis_index("dp")
+    z, y = place // 4, lax.rem(place, 4)
+    return jnp.where((lax.axis_index("mp") == 0) == first, y, z)
+
+
+def quarter_at(shift):
+    part = lax.rem(place_along(True) + shift + 4, 4)
+    return pl.ds(pl.multiple_of(part * QUARTER, QUARTER), QUARTER)
+
+
+def carry_squares(column_of, out):
+    lane = iota((8, 128), 1)
+    extra = jnp.zeros((8, 128), f32)
+    for r in range(ROW_TILES):
+        high, low = split_sum(column_of(r))
+        extra = jnp.where(lane == r, high, jnp.where(lane == 64 + r, low, extra))
+    out[TILE_COUNT] = extra.astype(bf16)
+
+
+def square_of(extra, r):
+    return extra[:, r : r + 1] + extra[:, 64 + r : 65 + r]
+
+
+def up_kernel(shift, state, gain, weight, out):
     wide = state[...].astype(f32)
+    squares = jnp.sum(wide * wide, axis=1, keepdims=True)
+    carry_squares(lambda r: squares[r * 8 : r * 8 + 8], out)
     normed = (wide * gain[...].astype(f32)).astype(bf16)
-    high, low = split_sum(jnp.sum(wide * wide, axis=1, keepdims=True))
-    lane = iota((8, 128), 1)
-    for t in range(2):
-        extra = jnp.zeros((8, 128), f32)
-        for r in range(ROW_TILES):
-            at = t * HALF + r * 8
-            extra = jnp.where(lane == 2 * r, high[at : at + 8], extra)
-            extra = jnp.where(lane == 2 * r + 1, low[at : at + 8], extra)
-        for f in range(NF):
-            out[t * NF + f, ROW_TILES * COL_TILES] = extra.astype(bf16)
-    for f in range(NF):
-        part = jnp.dot(normed, weight[:, f * FB : (f + 1) * FB], preferred_element_type=f32)
-        for t in range(2):
-            for r in range(ROW_TILES):
-                at = t * HALF + r * 8
-                for c in range(COL_TILES):
-                    tile = part[at : at + 8, c * 128 : (c + 1) * 128]
-                    out[t * NF + f, r * COL_TILES + c] = tile.astype(bf16)
-
-
-def mid_kernel(parts, out):
-    def total(tile):
-        value = parts[0, tile].astype(f32)
-        for j in range(1, DP):
-            value = value + parts[j, tile].astype(f32)
-        return value
-
-    squares = total(ROW_TILES * COL_TILES)
+    part = jnp.dot(normed, weight[:, quarter_at(shift)], preferred_element_type=f32)
+    for r in range(ROW_TILES):
+        for c in range(COL_TILES):
+            out[r * COL_TILES + c] = part[r * 8 : r * 8 + 8, c * 128 : (c + 1) * 128].astype(bf16)
+
+
+def add_four(parts, tile):
+    value = parts[0][tile].astype(f32)
+    for part in parts[1:]:
+        value = value + part[tile].astype(f32)
+    return value
+
+
+def sum_kernel(own, one, two, three, out):
+    parts = (own, one, two, three)
+    for tile in range(TILE_COUNT):
+        out[tile] = add_four(parts, tile).astype(bf16)
+    extra = add_four(parts, TILE_COUNT)
+    carry_squares(lambda r: square_of(extra, r), out)
+
+
+def mid_kernel(own, one, two, three, out):
+    parts = (own, one, two, three)
+    extra = add_four(parts, TILE_COUNT)
     rows = []
     for r in range(ROW_TILES):
-        square = squares[:, 2 * r : 2 * r + 1] + squares[:, 2 * r + 1 : 2 * r + 2]
-        scale = lax.rsqrt(square / D + EPS)
-        tiles = [jax.nn.silu(total(r * COL_TILES + c) * scale) for c in range(COL_TILES)]
+        scale = lax.rsqrt(square_of(extra, r) / D + EPS)
+        tiles = [jax.nn.silu(add_four(parts, r * COL_TILES + c) * scale) for c in range(COL_TILES)]
         rows.append(jnp.concatenate(tiles, axis=1))
-    active = jnp.concatenate(rows, axis=0).astype(bf16)
-    for j in range(DP):
-        out[j] = active
-
-
-def down_kernel(active, weight, kept, out):
-    total = jnp.zeros((LIVE, 512), f32)
-    for f in range(NF):
-        both = jnp.concatenate([active[0, f].astype(f32), active[1, f].astype(f32)], axis=0)
-        total = total + jnp.dot(
-            both.astype(bf16), weight[f * FB : (f + 1) * FB, :], preferred_element_type=f32
-        )
-    out[...] = total * kept[:, :1]
-
-
-def finish_kernel(state, lowered, other, first, second, third, planes, exits_here, held):
+    out[...] = jnp.concatenate(rows, axis=0).astype(bf16)
+
+
+def down_kernel(shift, active, weight, kept, out):
+    part = jnp.dot(active[...], weight[quarter_at(-shift), :], preferred_element_type=f32)
+    out[...] = part * kept[:, :1]
+
+
+def down_more_kernel(shift, active, weight, kept, before, out):
+    part = jnp.dot(active[...], weight[quarter_at(-shift), :], preferred_element_type=f32)
+    out[...] = before[...] + part * kept[:, :1]
+
+
+def finish_kernel(state, lowered, other, first, second, third, planes, slots, held, spread):
     result = (state[...].astype(f32) + (lowered[...] + other[...])).astype(bf16)
     mine = jnp.zeros((LIVE, 512), f32)
     for s, value in enumerate((first[...], second[...], third[...], result)):
         mine = mine + value.astype(f32) * planes[s : s + 1, :1]
-    held[0] = (mine * exits_here[:, :1]).astype(bf16)
-    held[1] = (result.astype(f32) * planes[3:4, :1]).astype(bf16)
+    spread[...] = lax.dot_general(
+        slots[...].astype(bf16), mine.astype(bf16), (((0,), (0,)), ((), ())), preferred_element_type=f32
+    )
+    first_slot = pl.multiple_of(lax.axis_index("section") * XS, XS)
+    held[:XS, :] = spread[pl.ds(first_slot, XS), :].astype(bf16)
+    held[XS:, :] = (result.astype(f32) * planes[3:4, :1]).astype(bf16)
 
 
 def power_above(value):
     return jnp.ceil(jnp.log2(jnp.maximum(value, 1e-30)))
 
 
-def head_kernel(held, one, two, three, gain, weight, out, parts):
-    total = held[...].astype(f32) + one[...].astype(f32) + two[...].astype(f32) + three[...].astype(f32)
-    wide = total.reshape(2 * LIVE, 512)
+def head_kernel(held, one, two, three, slots, gain, weight, out, parts, spread):
+    here = lax.axis_index("section")
+    finals = jnp.zeros((LIVE, 512), f32)
+    for k, source in enumerate((held, one, two, three)):
+        plane = lax.rem(here + 4 - k, 4)
+        spread[pl.ds(pl.multiple_of(plane * XS, XS), XS), :] = source[:XS, :].astype(f32)
+        finals = finals + source[XS:, :].astype(f32)
+    exits = jnp.dot(slots[...].astype(bf16), spread[...].astype(bf16), preferred_element_type=f32)
+    wide = jnp.concatenate([exits, finals], axis=0)
     headed = (wide * gain[...].astype(f32)).astype(bf16)
     peak = jnp.zeros((2 * LIVE, BLOCK), f32)
     for k in range(BLOCKS):
@@ -167,7 +198,7 @@
     power = power_above(jnp.max(peak, axis=1, keepdims=True))
     factor = jnp.exp2(15.0 - power) * STEPS
     for k in range(BLOCKS):
-        scaled = jnp.clip(jnp.round(parts[k] * factor), -32767.0, 32767.0)
+        scaled = (parts[k] * factor + ROUND) - ROUND
         tiles = scaled.reshape(2 * LIVE, 16, 128).astype(jnp.int32).astype(jnp.int16)
         for i in range(DP):
             for kind in range(2):
@@ -319,6 +350,16 @@
     return lax.all_to_all(value, axis, 0, 0)
 
 
+def around_four(value, by, first):
+    pairs = []
+    for z in range(4):
+        for y in range(4):
+            for core in range(2):
+                to = (z, (y + by) % 4) if (core == 0) == first else ((z + by) % 4, y)
+                pairs.append(((z * 4 + y) * 2 + core, (to[0] * 4 + to[1]) * 2 + core))
+    return lax.ppermute(value, ("dp", "mp"), pairs)
+
+
 def around(value, by):
     count = lax.axis_size("section")
     return lax.ppermute(value, "section", [(i, (i + by) % count) for i in range(count)])
@@ -334,20 +375,20 @@
     vmem = pl.BlockSpec(memory_space=pltpu.VMEM)
     far = pl.BlockSpec(memory_space=pltpu.HBM)
     fetched = (exit_idx, keep, kl_bucket, tokens, norm_gain, w_up[0])
-    current, kept, planes, exits_here, slots, bucket, gain, up_local = call(
+    tiles = shape((TILE_COUNT + 1, 8, 128), bf16)
+    current, kept, planes, slots, bucket, gain, up_local = call(
         prep_kernel,
         (
             shape((LIVE, 512), bf16),
             shape((LIVE, 128), f32),
             shape((8, 128), f32),
             shape((LIVE, 128), f32),
-            shape((LIVE, 128), f32),
             shape((1, 128), jnp.int32),
             shape((1, 512), bf16),
             pltpu.VMEM(w_up.shape[1:], bf16),
         ),
         in_specs=[pl.BlockSpec(memory_space=pltpu.SMEM)] + [far] * 6,
-        out_specs=[vmem] * 8,
+        out_specs=[vmem] * 7,
         scratch_shapes=[
             pltpu.VMEM((4, XS), jnp.int32),
             pltpu.VMEM((4, 128), jnp.int32),
@@ -360,37 +401,50 @@
     up_local = pltpu.with_memory_space_constraint(up_local, pltpu.VMEM)
     results = []
     for step in range(sections):
-        parts = call(
-            up_kernel,
-            shape((DP, ROW_TILES * COL_TILES + 1, 8, 128), bf16),
-            in_specs=[vmem] * 3,
-            out_specs=vmem,
-        )(current, gain, up_local)
-        parts = exchange(parts, "dp")
-        active = call(
-            mid_kernel, shape((DP, HALF, FB), bf16), in_specs=[vmem], out_specs=vmem
-        )(parts)
-        active = exchange(active, "dp")
+        part, received = {}, {}
+        for k in ORDER + (0,):
+            part[k] = call(
+                functools.partial(up_kernel, k), tiles, in_specs=[vmem] * 3, out_specs=vmem
+            )(current, gain, up_local)
+            if k:
+                received[k] = around_four(part[k], k, True)
+        quarter = call(sum_kernel, tiles, in_specs=[vmem] * 4, out_specs=vmem)(
+            part[0], *[received[k] for k in ORDER]
+        )
+        received = {k: around_four(quarter, k, False) for k in ORDER}
+        active = call(mid_kernel, shape((LIVE, QUARTER), bf16), in_specs=[vmem] * 4, out_specs=vmem)(
+            quarter, *[received[k] for k in ORDER]
+        )
+        received = {k: around_four(active, k, True) for k in ORDER}
+        wide = shape((LIVE, 512), f32)
         lowered = call(
-            down_kernel, shape((LIVE, 512), f32), in_specs=[vmem] * 3, out_specs=vmem
-        )(active.reshape(2, NF, HALF, FB), down_local, kept)
+            functools.partial(down_kernel, 0), wide, in_specs=[vmem] * 3, out_specs=vmem
+        )(active, down_local, kept)
+        for k in ARRIVAL:
+            lowered = call(
+                functools.partial(down_more_kernel, k), wide, in_specs=[vmem] * 4, out_specs=vmem
+            )(received[k], down_local, kept, lowered)
         other = lax.ppermute(lowered, "mp", [(0, 1), (1, 0)])
         if step < sections - 1:
             result = (current.astype(f32) + (lowered + other)).astype(bf16)
             results.append(result)
             current = around(result, 1)
     held = call(
-        finish_kernel, shape((2, LIVE, 512), bf16), in_specs=[vmem] * 8, out_specs=vmem
-    )(current, lowered, other, *results, planes, exits_here)
-    spread = [around(held, k) for k in (2, 1, 3)]
+        finish_kernel,
+        shape((XS + LIVE, 512), bf16),
+        in_specs=[vmem] * 8,
+        out_specs=vmem,
+        scratch_shapes=[pltpu.VMEM((4 * XS, 512), f32)],
+    )(current, lowered, other, *results, planes, slots)
+    spread = [around(held, k) for k in (1, 2, 3)]
     extent = 2 * PAIRS * TILES + 16
     parts = call(
         head_kernel,
         shape((DP, extent, 128), jnp.int16),
-        in_specs=[vmem] * 6,
+        in_specs=[vmem] * 7,
         out_specs=vmem,
-        scratch_shapes=[pltpu.VMEM((BLOCKS, 2 * LIVE, BLOCK), f32)],
-    )(held, *spread, head_gain.reshape(1, -1), head_local)
+        scratch_shapes=[pltpu.VMEM((BLOCKS, 2 * LIVE, BLOCK), f32), pltpu.VMEM((4 * XS, 512), f32)],
+    )(held, *spread, slots, head_gain.reshape(1, -1), head_local)
     parts = exchange(parts, "dp")
     logits, stats = call(
         peak_kernel,

time: 310 us -> 281 us (0.906)
  blocking collectives: 238 us -> 80.8 us
  waiting for transfers between devices: 25.4 us -> 111 us
  starting transfers between devices: 18.7 us -> 56.2 us
  Pallas kernels: 25.3 us -> 30.1 us
    all_to_all x12 -> x4, blocking collectives: 238 us -> 80.8 us  [exchange(): return lax.all_to_all(value, axis, 0, 0)]
    ppermute x0 -> x36, waiting for transfers between devices: none -> 88 us  [around_four(): return lax.ppermute(value, ('dp', 'mp'), pairs)]
    ppermute x0 -> x36, starting transfers between devices: none -> 42.1 us  [around_four(): return lax.ppermute(value, ('dp', 'mp'), pairs)]
    pallas_call x13 -> x41, Pallas kernels: 12.3 us -> 17 us  [the longest x16 7.29 us: shards(): call(functools.partial(up_kernel, k), tiles, in_specs=[vmem] * 3, out_spe...]
    ppermute x4, starting transfers between devices: 14.5 us -> 9.9 us  [shards(): other = lax.ppermute(lowered, 'mp', [(0, 1), (1, 0)])]
  transfers between devices with their start and end apart: 10 -> 46, of which waited for: 9 -> 32; matrix products, arithmetic and copies ran while one was open for 0% -> 0% of each run, Pallas kernels for 0% -> 4%
where the time goes in v4:
time: 281 us
  waiting for transfers between devices  111 us (40%)
  blocking collectives  80.8 us (29%)
  starting transfers between devices  56.2 us (20%)
  Pallas kernels  30.1 us (11%)
    ppermute x36, waiting for transfers between devices, around_four(): return lax.ppermute(value, ('dp', 'mp'), pairs)  88 us
    all_to_all x4, blocking collectives, exchange(): return lax.all_to_all(value, axis, 0, 0)  80.8 us
    ppermute x36, starting transfers between devices, around_four(): return lax.ppermute(value, ('dp', 'mp'), pairs)  42.1 us
    ppermute x6, waiting for transfers between devices, around(): lax.ppermute(value, 'section', [(i, (i + by) % count) for i in range(coun...  19.1 us
    ppermute x4, starting transfers between devices, shards(): other = lax.ppermute(lowered, 'mp', [(0, 1), (1, 0)])  9.9 us
    pallas_call x16, Pallas kernels, shards(): call(functools.partial(up_kernel, k), tiles, in_specs=[vmem] * 3, out_spe...  7.29 us
  transfers between devices with their start and end apart: 46, of which 32 were waited for; matrix products, arithmetic and copies ran while one was open for 0% of the time, Pallas kernels for 4%

profile of v4, /device:TPU:1, one launch (start us, length us, event | category | flops | bytes accessed | tf_op | source)
XLA Modules:
  0.0 280.6 jit_solution(14606522364693134194)
XLA Ops:
  1.3 3.9 %shard_map.121 = (bf16[80,512]{1,0:T(8,128)(2,1)S(1)}, f32[80,128]{1,0:T(8,128)S(1)}, f32[8,128]{1,0:T(8,128)S(1)}, f32[80,128]{1,0:T(8,128)S(1)}, s32[1,128]{1,...) custom-call(s32[4]{0:T(128)S(1)} %copy-done, s32[4,32]{1,0:T(4,128)} %index_in.1, ...), custom_call_target="tpu_custom_call" | custom-call | tf_op jit(solution)/shard_map/pallas_call | solution.py:379
  5.6 4.7 %collective-permute-start.2 = (bf16[141,8,128]{2,1,0:T(8,128)(2,1)S(1)}, bf16[141,8,128]{2,1,0:T(8,128)(2,1)S(1)}, u32[]{:S(2)}, u32[]{:S(2)}) collective-permute-start(bf16[141,8,128]{2,1,0:T(8,128)(2,1)S(1)} %shard_map.125), channel_id=1, source_target_pairs={{0,6},{1,25},{2,0},{3,27},{4,2},{5,29},{6,4},{7,31},{8,14},{9,1},{... | collective-permute-start | bytes 866312 | tf_op jit(solution)/shard_map/ppermute | solution.py:360
  11.3 1.4 collective-permute-start
  13.1 0.8 collective-permute-done.2.three
  13.9 7.0 %collective-permute-done.1.two = bf16[141,8,128]{2,1,0:T(8,128)(2,1)S(1)} collective-permute-done((bf16[141,8,128]{2,1,0:T(8,128)(2,1)S(1)}, bf16[141,8,128]{2,1,0:T(8,128)(2,1)S(1)}, u32[]{:S(2)}, u32[]{:S(2)}) %collective-permute-start.1) | collective-permute-done | bytes 288800 | tf_op jit(solution)/shard_map/ppermute | solution.py:360
  21.2 2.7 collective-permute-start.3
  24.3 2.3 collective-permute-start.5
  26.6 2.0 collective-permute-done.3.one
  28.6 3.1 %collective-permute-done.4.two = bf16[141,8,128]{2,1,0:T(8,128)(2,1)S(1)} collective-permute-done((bf16[141,8,128]{2,1,0:T(8,128)(2,1)S(1)}, bf16[141,8,128]{2,1,0:T(8,128)(2,1)S(1)}, u32[]{:S(2)}, u32[]{:S(2)}) %collective-permute-start.4) | collective-permute-done | bytes 288800 | tf_op jit(solution)/shard_map/ppermute | solution.py:360
  32.1 0.8 collective-permute-start.8
  34.6 3.0 %collective-permute-done.8.active = bf16[80,1792]{1,0:T(8,128)(2,1)S(1)} collective-permute-done((bf16[80,1792]{1,0:T(8,128)(2,1)S(1)}, bf16[80,1792]{1,0:T(8,128)(2,1)S(1)}, u32[]{:S(2)}, u32[]{:S(2)}) %collective-permute-start.8) | collective-permute-done | bytes 286752 | tf_op jit(solution)/shard_map/ppermute | solution.py:360
  38.1 4.8 %collective-permute-done.7.active = bf16[80,1792]{1,0:T(8,128)(2,1)S(1)} collective-permute-done((bf16[80,1792]{1,0:T(8,128)(2,1)S(1)}, bf16[80,1792]{1,0:T(8,128)(2,1)S(1)}, u32[]{:S(2)}, u32[]{:S(2)}) %collective-permute-start.7) | collective-permute-done | bytes 286752 | tf_op jit(solution)/shard_map/ppermute | solution.py:360
  43.8 4.2 %collective-permute-start.9 = (f32[80,512]{1,0:T(8,128)S(1)}, f32[80,512]{1,0:T(8,128)S(1)}, u32[]{:S(2)}, u32[]{:S(2)}) collective-permute-start(f32[80,512]{1,0:T(8,128)S(1)} %shard_map.131), channel_id=1, source_target_pairs={{0,1},{1,0},{2,3},{3,2},{4,5},{5,4},{6,7},{7,6},{8,9},{9,8},{10,11... | collective-permute-start | bytes 491528 | tf_op jit(solution)/shard_map/ppermute | solution.py:427
  48.0 1.0 collective-permute-done.9
  49.0 1.3 collective-permute-start.10
  50.3 3.7 %collective-permute-done.10.state = bf16[80,512]{1,0:T(8,128)(2,1)S(1)} collective-permute-done((bf16[80,512]{1,0:T(8,128)(2,1)S(1)}, bf16[80,512]{1,0:T(8,128)(2,1)S(1)}, u32[]{:S(2)}, u32[]{:S(2)}) %collective-permute-start.10) | collective-permute-done | bytes 81952 | tf_op jit(solution)/shard_map/ppermute | solution.py:365
  54.4 2.5 collective-permute-start.13
  57.9 1.3 collective-permute-start.11
  59.6 0.9 collective-permute-done.13.three
  60.5 6.7 %collective-permute-done.12.two = bf16[141,8,128]{2,1,0:T(8,128)(2,1)S(1)} collective-permute-done((bf16[141,8,128]{2,1,0:T(8,128)(2,1)S(1)}, bf16[141,8,128]{2,1,0:T(8,128)(2,1)S(1)}, u32[]{:S(2)}, u32[]{:S(2)}) %collective-permute-start.12) | collective-permute-done | bytes 288800 | tf_op jit(solution)/shard_map/ppermute | solution.py:360
  67.5 0.8 collective-permute-start.14
  68.3 2.7 collective-permute-start.16
  71.0 3.9 %collective-permute-done.14.one = bf16[141,8,128]{2,1,0:T(8,128)(2,1)S(1)} collective-permute-done((bf16[141,8,128]{2,1,0:T(8,128)(2,1)S(1)}, bf16[141,8,128]{2,1,0:T(8,128)(2,1)S(1)}, u32[]{:S(2)}, u32[]{:S(2)}) %collective-permute-start.14) | collective-permute-done | bytes 288800 | tf_op jit(solution)/shard_map/ppermute | solution.py:360
  75.0 3.1 %collective-permute-done.15.two = bf16[141,8,128]{2,1,0:T(8,128)(2,1)S(1)} collective-permute-done((bf16[141,8,128]{2,1,0:T(8,128)(2,1)S(1)}, bf16[141,8,128]{2,1,0:T(8,128)(2,1)S(1)}, u32[]{:S(2)}, u32[]{:S(2)}) %collective-permute-start.15) | collective-permute-done | bytes 288800 | tf_op jit(solution)/shard_map/ppermute | solution.py:360
  80.8 3.4 %collective-permute-done.19.active = bf16[80,1792]{1,0:T(8,128)(2,1)S(1)} collective-permute-done((bf16[80,1792]{1,0:T(8,128)(2,1)S(1)}, bf16[80,1792]{1,0:T(8,128)(2,1)S(1)}, u32[]{:S(2)}, u32[]{:S(2)}) %collective-permute-start.19) | collective-permute-done | bytes 286752 | tf_op jit(solution)/shard_map/ppermute | solution.py:360
  84.6 4.5 %collective-permute-done.18.active = bf16[80,1792]{1,0:T(8,128)(2,1)S(1)} collective-permute-done((bf16[80,1792]{1,0:T(8,128)(2,1)S(1)}, bf16[80,1792]{1,0:T(8,128)(2,1)S(1)}, u32[]{:S(2)}, u32[]{:S(2)}) %collective-permute-start.18) | collective-permute-done | bytes 286752 | tf_op jit(solution)/shard_map/ppermute | solution.py:360
  90.1 1.7 collective-permute-start.20
  91.7 1.0 collective-permute-done.20
  92.9 4.9 %collective-permute-done.21.state = bf16[80,512]{1,0:T(8,128)(2,1)S(1)} collective-permute-done((bf16[80,512]{1,0:T(8,128)(2,1)S(1)}, bf16[80,512]{1,0:T(8,128)(2,1)S(1)}, u32[]{:S(2)}, u32[]{:S(2)}) %collective-permute-start.21) | collective-permute-done | bytes 81952 | tf_op jit(solution)/shard_map/ppermute | solution.py:365
  98.2 2.5 collective-permute-start.24
  101.7 1.3 collective-permute-start.22
  103.4 0.9 collective-permute-done.24.three
  104.3 6.7 %collective-permute-done.23.two = bf16[141,8,128]{2,1,0:T(8,128)(2,1)S(1)} collective-permute-done((bf16[141,8,128]{2,1,0:T(8,128)(2,1)S(1)}, bf16[141,8,128]{2,1,0:T(8,128)(2,1)S(1)}, u32[]{:S(2)}, u32[]{:S(2)}) %collective-permute-start.23) | collective-permute-done | bytes 288800 | tf_op jit(solution)/shard_map/ppermute | solution.py:360
  111.3 1.2 collective-permute-start.25
  112.5 2.7 collective-permute-start.27
  115.1 3.6 %collective-permute-done.25.one = bf16[141,8,128]{2,1,0:T(8,128)(2,1)S(1)} collective-permute-done((bf16[141,8,128]{2,1,0:T(8,128)(2,1)S(1)}, bf16[141,8,128]{2,1,0:T(8,128)(2,1)S(1)}, u32[]{:S(2)}, u32[]{:S(2)}) %collective-permute-start.25) | collective-permute-done | bytes 288800 | tf_op jit(solution)/shard_map/ppermute | solution.py:360
  118.7 3.1 %collective-permute-done.26.two = bf16[141,8,128]{2,1,0:T(8,128)(2,1)S(1)} collective-permute-done((bf16[141,8,128]{2,1,0:T(8,128)(2,1)S(1)}, bf16[141,8,128]{2,1,0:T(8,128)(2,1)S(1)}, u32[]{:S(2)}, u32[]{:S(2)}) %collective-permute-start.26) | collective-permute-done | bytes 288800 | tf_op jit(solution)/shard_map/ppermute | solution.py:360
  124.5 3.4 %collective-permute-done.30.active = bf16[80,1792]{1,0:T(8,128)(2,1)S(1)} collective-permute-done((bf16[80,1792]{1,0:T(8,128)(2,1)S(1)}, bf16[80,1792]{1,0:T(8,128)(2,1)S(1)}, u32[]{:S(2)}, u32[]{:S(2)}) %collective-permute-start.30) | collective-permute-done | bytes 286752 | tf_op jit(solution)/shard_map/ppermute | solution.py:360
  128.4 4.5 %collective-permute-done.29.active = bf16[80,1792]{1,0:T(8,128)(2,1)S(1)} collective-permute-done((bf16[80,1792]{1,0:T(8,128)(2,1)S(1)}, bf16[80,1792]{1,0:T(8,128)(2,1)S(1)}, u32[]{:S(2)}, u32[]{:S(2)}) %collective-permute-start.29) | collective-permute-done | bytes 286752 | tf_op jit(solution)/shard_map/ppermute | solution.py:360
  133.8 2.4 collective-permute-start.31
  136.2 1.0 collective-permute-done.31
  137.4 4.9 %collective-permute-done.32.state = bf16[80,512]{1,0:T(8,128)(2,1)S(1)} collective-permute-done((bf16[80,512]{1,0:T(8,128)(2,1)S(1)}, bf16[80,512]{1,0:T(8,128)(2,1)S(1)}, u32[]{:S(2)}, u32[]{:S(2)}) %collective-permute-start.32) | collective-permute-done | bytes 81952 | tf_op jit(solution)/shard_map/ppermute | solution.py:365
  142.7 2.5 collective-permute-start.35
  146.1 1.3 collective-permute-start.33
  147.8 0.9 collective-permute-done.35.three
  148.8 6.7 %collective-permute-done.34.two = bf16[141,8,128]{2,1,0:T(8,128)(2,1)S(1)} collective-permute-done((bf16[141,8,128]{2,1,0:T(8,128)(2,1)S(1)}, bf16[141,8,128]{2,1,0:T(8,128)(2,1)S(1)}, u32[]{:S(2)}, u32[]{:S(2)}) %collective-permute-start.34) | collective-permute-done | bytes 288800 | tf_op jit(solution)/shard_map/ppermute | solution.py:360
  155.8 0.8 collective-permute-start.36
  156.6 2.7 collective-permute-start.38
  159.3 3.9 %collective-permute-done.36.one = bf16[141,8,128]{2,1,0:T(8,128)(2,1)S(1)} collective-permute-done((bf16[141,8,128]{2,1,0:T(8,128)(2,1)S(1)}, bf16[141,8,128]{2,1,0:T(8,128)(2,1)S(1)}, u32[]{:S(2)}, u32[]{:S(2)}) %collective-permute-start.36) | collective-permute-done | bytes 288800 | tf_op jit(solution)/shard_map/ppermute | solution.py:360
  163.2 3.1 %collective-permute-done.37.two = bf16[141,8,128]{2,1,0:T(8,128)(2,1)S(1)} collective-permute-done((bf16[141,8,128]{2,1,0:T(8,128)(2,1)S(1)}, bf16[141,8,128]{2,1,0:T(8,128)(2,1)S(1)}, u32[]{:S(2)}, u32[]{:S(2)}) %collective-permute-start.37) | collective-permute-done | bytes 288800 | tf_op jit(solution)/shard_map/ppermute | solution.py:360
  166.6 1.0 collective-permute-start.41
  169.2 3.4 %collective-permute-done.41.active = bf16[80,1792]{1,0:T(8,128)(2,1)S(1)} collective-permute-done((bf16[80,1792]{1,0:T(8,128)(2,1)S(1)}, bf16[80,1792]{1,0:T(8,128)(2,1)S(1)}, u32[]{:S(2)}, u32[]{:S(2)}) %collective-permute-start.41) | collective-permute-done | bytes 286752 | tf_op jit(solution)/shard_map/ppermute | solution.py:360
  173.1 4.5 %collective-permute-done.40.active = bf16[80,1792]{1,0:T(8,128)(2,1)S(1)} collective-permute-done((bf16[80,1792]{1,0:T(8,128)(2,1)S(1)}, bf16[80,1792]{1,0:T(8,128)(2,1)S(1)}, u32[]{:S(2)}, u32[]{:S(2)}) %collective-permute-start.40) | collective-permute-done | bytes 286752 | tf_op jit(solution)/shard_map/ppermute | solution.py:360
  178.5 1.7 collective-permute-start.42
  180.2 1.0 collective-permute-done.42.other
  182.1 2.2 collective-permute-start.45
  184.3 5.7 %collective-permute-done.43.one = bf16[112,512]{1,0:T(8,128)(2,1)S(1)} collective-permute-done((bf16[112,512]{1,0:T(8,128)(2,1)S(1)}, bf16[112,512]{1,0:T(8,128)(2,1)S(1)}, u32[]{:S(2)}, u32[]{:S(2)}) %collective-permute-start.43) | collective-permute-done | bytes 114720 | tf_op jit(solution)/shard_map/ppermute | solution.py:365
  190.0 4.0 %shard_map.163 = s16[16,656,128]{2,1,0:T(8,128)(2,1)S(1)} custom-call(bf16[112,512]{1,0:T(8,128)(2,1)S(1)} %shard_map.162.held, bf16[112,512]{1,0:T(8,128)(2,1)S(1)} %collective-permute-done.43.one, bf16[112,512]{1,0:T(8,128)(2,1)S(1)} %collective-permute-done.44.two, bf16[112,512]{1,0:T(8,128)(2,1)S(1)} %collective-permute-done.45.three, ...), custom_call_target="tpu_custom_call" | custom-call | tf_op jit(solution)/shard_map/pallas_call | solution.py:441
  194.0 37.5 %all_to_all.20.parts = s16[16,656,128]{2,1,0:T(8,128)(2,1)S(1)} all-to-all(s16[16,656,128]{2,1,0:T(8,128)(2,1)S(1)} %shard_map.163), channel_id=1, replica_groups=mesh['section'=4,'dp'=16,'mp'=2] {'dp'}, dimensions={0} | all-to-all | bytes 5373952 | tf_op jit(solution)/shard_map/all_to_all | solution.py:350
  231.5 1.3 shard_map.164
  232.9 11.2 %all_to_all.21.stats = f32[8,8,128]{2,1,0:T(8,128)S(1)} all-to-all(f32[8,8,128]{2,1,0:T(8,128)S(1)} %get-tuple-element.22), channel_id=1, replica_groups=mesh['section'=4,'dp'=16,'mp'=2] {'section','mp'}, dimensions={0} | all-to-all | bytes 65536 | tf_op jit(solution)/shard_map/all_to_all | solution.py:350
  244.4 22.6 %all_to_all.22.gaps = bf16[16,336,128]{2,1,0:T(8,128)(2,1)S(1)} all-to-all(bf16[16,336,128]{2,1,0:T(8,128)(2,1)S(1)} %shard_map.165), channel_id=1, replica_groups=mesh['section'=4,'dp'=16,'mp'=2] {'dp'}, dimensions={0} | all-to-all | bytes 2752512 | tf_op jit(solution)/shard_map/all_to_all | solution.py:350
  267.0 3.5 %shard_map.166 = (bf16[128,512]{1,0:T(8,128)(2,1)S(1)}, f32[1,8]{1,0:T(1,128)}, f32[4,16]{1,0:T(4,128)}) custom-call(bf16[16,336,128]{2,1,0:T(8,128)(2,1)S(1)} %all_to_all.22.gaps, bf16[512,8192]{1,0:T(8,128)(2,1)S(1)} %bitcast.23, f32[80,128]{1,0:T(8,128)S(1)} %get-tuple-element.20.slots, s32[1,128]{1,0:T(1,128)S(1)} %get-tuple-element.23.buckets), custom_call_target="tpu_custom_call" | custom-call | tf_op jit(solution)/shard_map/pallas_call | solution.py:466
  270.5 9.5 %all_to_all.23 = bf16[8,16,512]{2,1,0:T(8,128)(2,1)S(1)} all-to-all(bf16[8,16,512]{2,1,0:T(8,128)(2,1)S(1)} %bitcast.24), channel_id=1, replica_groups=mesh['section'=4,'dp'=16,'mp'=2] {'section','mp'}, dimensions={0} | all-to-all | bytes 262144 | tf_op jit(solution)/shard_map/all_to_all | solution.py:350
  (97 shorter events, 26.9 us)
Async XLA Ops:
  0.6 0.7 copy-start
  5.6 8.3 %collective-permute-start.2 = (bf16[141,8,128]{2,1,0:T(8,128)(2,1)S(1)}, bf16[141,8,128]{2,1,0:T(8,128)(2,1)S(1)}, u32[]{:S(2)}, u32[]{:S(2)}) collective-permute-start(bf16[141,8,128]{2,1,0:T(8,128)(2,1)S(1)} %shard_map.125), channel_id=1, source_target_pairs={{0,6},{1,25},{2,0},{3,27},{4,2},{5,29},{6,4},{7,31},{8,14},{9,1},{... | collective-permute-start | bytes 866312 | tf_op jit(solution)/shard_map/ppermute | solution.py:360
  10.7 23.4 %slice-start = ((s8[7340032]{0:T(1024)(128)(4,1)}), s8[4194304]{0:T(1024)(128)(4,1)S(1)}, s32[]{:S(2)}) async-start(s8[7340032]{0:T(1024)(128)(4,1)} %bitcast.4), calls=%async_computation.4 | async-start | bytes 8388608
  10.7 10.2 %collective-permute-start.1 = (bf16[141,8,128]{2,1,0:T(8,128)(2,1)S(1)}, bf16[141,8,128]{2,1,0:T(8,128)(2,1)S(1)}, u32[]{:S(2)}, u32[]{:S(2)}) collective-permute-start(bf16[141,8,128]{2,1,0:T(8,128)(2,1)S(1)} %shard_map.124), channel_id=1, source_target_pairs={{0,2},{1,9},{2,4},{3,11},{4,6},{5,13},{6,0},{7,15},{8,10},{9,17},{... | collective-permute-start | bytes 866312 | tf_op jit(solution)/shard_map/ppermute | solution.py:360
  11.3 22.9 %slice-start.1 = ((s8[7340032]{0:T(1024)(128)(4,1)}), s8[3145728]{0:T(1024)(128)(4,1)S(1)}, s32[]{:S(2)}) async-start(s8[7340032]{0:T(1024)(128)(4,1)} %bitcast.4), calls=%async_computation.5 | async-start | bytes 6291456
  11.3 9.6 %collective-permute-start = (bf16[141,8,128]{2,1,0:T(8,128)(2,1)S(1)}, bf16[141,8,128]{2,1,0:T(8,128)(2,1)S(1)}, u32[]{:S(2)}, u32[]{:S(2)}) collective-permute-start(bf16[141,8,128]{2,1,0:T(8,128)(2,1)S(1)} %shard_map.123), channel_id=1, source_target_pairs={{0,4},{1,17},{2,6},{3,19},{4,0},{5,21},{6,2},{7,23},{8,12},{9,25},... | collective-permute-start | bytes 866312 | tf_op jit(solution)/shard_map/ppermute | solution.py:360
  21.2 7.4 %collective-permute-start.3 = (bf16[141,8,128]{2,1,0:T(8,128)(2,1)S(1)}, bf16[141,8,128]{2,1,0:T(8,128)(2,1)S(1)}, u32[]{:S(2)}, u32[]{:S(2)}) collective-permute-start(bf16[141,8,128]{2,1,0:T(8,128)(2,1)S(1)} %shard_map.126.own), channel_id=1, source_target_pairs={{0,16},{1,5},{2,18},{3,7},{4,20},{5,1},{6,22},{7,3},{8,24},{9,13},... | collective-permute-start | bytes 866312 | tf_op jit(solution)/shard_map/ppermute | solution.py:360
  23.9 7.8 %collective-permute-start.4 = (bf16[141,8,128]{2,1,0:T(8,128)(2,1)S(1)}, bf16[141,8,128]{2,1,0:T(8,128)(2,1)S(1)}, u32[]{:S(2)}, u32[]{:S(2)}) collective-permute-start(bf16[141,8,128]{2,1,0:T(8,128)(2,1)S(1)} %shard_map.126.own), channel_id=1, source_target_pairs={{0,8},{1,3},{2,10},{3,5},{4,12},{5,7},{6,14},{7,1},{8,16},{9,11},{... | collective-permute-start | bytes 866312 | tf_op jit(solution)/shard_map/ppermute | solution.py:360
  24.3 7.4 %collective-permute-start.5 = (bf16[141,8,128]{2,1,0:T(8,128)(2,1)S(1)}, bf16[141,8,128]{2,1,0:T(8,128)(2,1)S(1)}, u32[]{:S(2)}, u32[]{:S(2)}) collective-permute-start(bf16[141,8,128]{2,1,0:T(8,128)(2,1)S(1)} %shard_map.126.own), channel_id=1, source_target_pairs={{0,24},{1,7},{2,26},{3,1},{4,28},{5,3},{6,30},{7,5},{8,0},{9,15},{... | collective-permute-start | bytes 866312 | tf_op jit(solution)/shard_map/ppermute | solution.py:360
  32.1 5.6 %collective-permute-start.8 = (bf16[80,1792]{1,0:T(8,128)(2,1)S(1)}, bf16[80,1792]{1,0:T(8,128)(2,1)S(1)}, u32[]{:S(2)}, u32[]{:S(2)}) collective-permute-start(bf16[80,1792]{1,0:T(8,128)(2,1)S(1)} %shard_map.127.active), channel_id=1, source_target_pairs={{0,6},{1,25},{2,0},{3,27},{4,2},{5,29},{6,4},{7,31},{8,14},{9,1},{... | collective-permute-start | bytes 860168 | tf_op jit(solution)/shard_map/ppermute | solution.py:360
  32.8 10.1 %collective-permute-start.7 = (bf16[80,1792]{1,0:T(8,128)(2,1)S(1)}, bf16[80,1792]{1,0:T(8,128)(2,1)S(1)}, u32[]{:S(2)}, u32[]{:S(2)}) collective-permute-start(bf16[80,1792]{1,0:T(8,128)(2,1)S(1)} %shard_map.127.active), channel_id=1, source_target_pairs={{0,2},{1,9},{2,4},{3,11},{4,6},{5,13},{6,0},{7,15},{8,10},{9,17},{... | collective-permute-start | bytes 860168 | tf_op jit(solution)/shard_map/ppermute | solution.py:360
  33.6 9.7 %collective-permute-start.6 = (bf16[80,1792]{1,0:T(8,128)(2,1)S(1)}, bf16[80,1792]{1,0:T(8,128)(2,1)S(1)}, u32[]{:S(2)}, u32[]{:S(2)}) collective-permute-start(bf16[80,1792]{1,0:T(8,128)(2,1)S(1)} %shard_map.127.active), channel_id=1, source_target_pairs={{0,4},{1,17},{2,6},{3,19},{4,0},{5,21},{6,2},{7,23},{8,12},{9,25},... | collective-permute-start | bytes 860168 | tf_op jit(solution)/shard_map/ppermute | solution.py:360
  43.8 5.2 %collective-permute-start.9 = (f32[80,512]{1,0:T(8,128)S(1)}, f32[80,512]{1,0:T(8,128)S(1)}, u32[]{:S(2)}, u32[]{:S(2)}) collective-permute-start(f32[80,512]{1,0:T(8,128)S(1)} %shard_map.131), channel_id=1, source_target_pairs={{0,1},{1,0},{2,3},{3,2},{4,5},{5,4},{6,7},{7,6},{8,9},{9,8},{10,11... | collective-permute-start | bytes 491528 | tf_op jit(solution)/shard_map/ppermute | solution.py:427
  49.0 4.9 %collective-permute-start.10 = (bf16[80,512]{1,0:T(8,128)(2,1)S(1)}, bf16[80,512]{1,0:T(8,128)(2,1)S(1)}, u32[]{:S(2)}, u32[]{:S(2)}) collective-permute-start(bf16[80,512]{1,0:T(8,128)(2,1)S(1)} %add_convert_fusion.2.first), channel_id=1, source_target_pairs={{0,32},{32,64},{64,96},{96,0},{1,33},{33,65},{65,97},{97,1},{2,34}... | collective-permute-start | bytes 245768 | tf_op jit(solution)/shard_map/ppermute | solution.py:365
  54.4 6.1 %collective-permute-start.13 = (bf16[141,8,128]{2,1,0:T(8,128)(2,1)S(1)}, bf16[141,8,128]{2,1,0:T(8,128)(2,1)S(1)}, u32[]{:S(2)}, u32[]{:S(2)}) collective-permute-start(bf16[141,8,128]{2,1,0:T(8,128)(2,1)S(1)} %shard_map.135), channel_id=1, source_target_pairs={{0,6},{1,25},{2,0},{3,27},{4,2},{5,29},{6,4},{7,31},{8,14},{9,1},{... | collective-permute-start | bytes 866312 | tf_op jit(solution)/shard_map/ppermute | solution.py:360
  57.3 9.9 %collective-permute-start.12 = (bf16[141,8,128]{2,1,0:T(8,128)(2,1)S(1)}, bf16[141,8,128]{2,1,0:T(8,128)(2,1)S(1)}, u32[]{:S(2)}, u32[]{:S(2)}) collective-permute-start(bf16[141,8,128]{2,1,0:T(8,128)(2,1)S(1)} %shard_map.134), channel_id=1, source_target_pairs={{0,2},{1,9},{2,4},{3,11},{4,6},{5,13},{6,0},{7,15},{8,10},{9,17},{... | collective-permute-start | bytes 866312 | tf_op jit(solution)/shard_map/ppermute | solution.py:360
  57.9 9.3 %collective-permute-start.11 = (bf16[141,8,128]{2,1,0:T(8,128)(2,1)S(1)}, bf16[141,8,128]{2,1,0:T(8,128)(2,1)S(1)}, u32[]{:S(2)}, u32[]{:S(2)}) collective-permute-start(bf16[141,8,128]{2,1,0:T(8,128)(2,1)S(1)} %shard_map.133), channel_id=1, source_target_pairs={{0,4},{1,17},{2,6},{3,19},{4,0},{5,21},{6,2},{7,23},{8,12},{9,25},... | collective-permute-start | bytes 866312 | tf_op jit(solution)/shard_map/ppermute | solution.py:360
  67.5 7.4 %collective-permute-start.14 = (bf16[141,8,128]{2,1,0:T(8,128)(2,1)S(1)}, bf16[141,8,128]{2,1,0:T(8,128)(2,1)S(1)}, u32[]{:S(2)}, u32[]{:S(2)}) collective-permute-start(bf16[141,8,128]{2,1,0:T(8,128)(2,1)S(1)} %shard_map.136.own), channel_id=1, source_target_pairs={{0,16},{1,5},{2,18},{3,7},{4,20},{5,1},{6,22},{7,3},{8,24},{9,13},... | collective-permute-start | bytes 866312 | tf_op jit(solution)/shard_map/ppermute | solution.py:360
  68.3 9.7 %collective-permute-start.15 = (bf16[141,8,128]{2,1,0:T(8,128)(2,1)S(1)}, bf16[141,8,128]{2,1,0:T(8,128)(2,1)S(1)}, u32[]{:S(2)}, u32[]{:S(2)}) collective-permute-start(bf16[141,8,128]{2,1,0:T(8,128)(2,1)S(1)} %shard_map.136.own), channel_id=1, source_target_pairs={{0,8},{1,3},{2,10},{3,5},{4,12},{5,7},{6,14},{7,1},{8,16},{9,11},{... | collective-permute-start | bytes 866312 | tf_op jit(solution)/shard_map/ppermute | solution.py:360
  68.3 9.7 %collective-permute-start.16 = (bf16[141,8,128]{2,1,0:T(8,128)(2,1)S(1)}, bf16[141,8,128]{2,1,0:T(8,128)(2,1)S(1)}, u32[]{:S(2)}, u32[]{:S(2)}) collective-permute-start(bf16[141,8,128]{2,1,0:T(8,128)(2,1)S(1)} %shard_map.136.own), channel_id=1, source_target_pairs={{0,24},{1,7},{2,26},{3,1},{4,28},{5,3},{6,30},{7,5},{8,0},{9,15},{... | collective-permute-start | bytes 866312 | tf_op jit(solution)/shard_map/ppermute | solution.py:360
  78.3 5.8 %collective-permute-start.19 = (bf16[80,1792]{1,0:T(8,128)(2,1)S(1)}, bf16[80,1792]{1,0:T(8,128)(2,1)S(1)}, u32[]{:S(2)}, u32[]{:S(2)}) collective-permute-start(bf16[80,1792]{1,0:T(8,128)(2,1)S(1)} %shard_map.137.active), channel_id=1, source_target_pairs={{0,6},{1,25},{2,0},{3,27},{4,2},{5,29},{6,4},{7,31},{8,14},{9,1},{... | collective-permute-start | bytes 860168 | tf_op jit(solution)/shard_map/ppermute | solution.py:360
  79.1 10.1 %collective-permute-start.18 = (bf16[80,1792]{1,0:T(8,128)(2,1)S(1)}, bf16[80,1792]{1,0:T(8,128)(2,1)S(1)}, u32[]{:S(2)}, u32[]{:S(2)}) collective-permute-start(bf16[80,1792]{1,0:T(8,128)(2,1)S(1)} %shard_map.137.active), channel_id=1, source_target_pairs={{0,2},{1,9},{2,4},{3,11},{4,6},{5,13},{6,0},{7,15},{8,10},{9,17},{... | collective-permute-start | bytes 860168 | tf_op jit(solution)/shard_map/ppermute | solution.py:360
  79.9 9.7 %collective-permute-start.17 = (bf16[80,1792]{1,0:T(8,128)(2,1)S(1)}, bf16[80,1792]{1,0:T(8,128)(2,1)S(1)}, u32[]{:S(2)}, u32[]{:S(2)}) collective-permute-start(bf16[80,1792]{1,0:T(8,128)(2,1)S(1)} %shard_map.137.active), channel_id=1, source_target_pairs={{0,4},{1,17},{2,6},{3,19},{4,0},{5,21},{6,2},{7,23},{8,12},{9,25},... | collective-permute-start | bytes 860168 | tf_op jit(solution)/shard_map/ppermute | solution.py:360
  90.1 2.7 collective-permute-start.20
  92.8 4.9 %collective-permute-start.21 = (bf16[80,512]{1,0:T(8,128)(2,1)S(1)}, bf16[80,512]{1,0:T(8,128)(2,1)S(1)}, u32[]{:S(2)}, u32[]{:S(2)}) collective-permute-start(bf16[80,512]{1,0:T(8,128)(2,1)S(1)} %add_convert_fusion.1.second), channel_id=1, source_target_pairs={{0,32},{32,64},{64,96},{96,0},{1,33},{33,65},{65,97},{97,1},{2,34}... | collective-permute-start | bytes 245768 | tf_op jit(solution)/shard_map/ppermute | solution.py:365
  98.2 6.1 %collective-permute-start.24 = (bf16[141,8,128]{2,1,0:T(8,128)(2,1)S(1)}, bf16[141,8,128]{2,1,0:T(8,128)(2,1)S(1)}, u32[]{:S(2)}, u32[]{:S(2)}) collective-permute-start(bf16[141,8,128]{2,1,0:T(8,128)(2,1)S(1)} %shard_map.145), channel_id=1, source_target_pairs={{0,6},{1,25},{2,0},{3,27},{4,2},{5,29},{6,4},{7,31},{8,14},{9,1},{... | collective-permute-start | bytes 866312 | tf_op jit(solution)/shard_map/ppermute | solution.py:360
  101.1 9.9 %collective-permute-start.23 = (bf16[141,8,128]{2,1,0:T(8,128)(2,1)S(1)}, bf16[141,8,128]{2,1,0:T(8,128)(2,1)S(1)}, u32[]{:S(2)}, u32[]{:S(2)}) collective-permute-start(bf16[141,8,128]{2,1,0:T(8,128)(2,1)S(1)} %shard_map.144), channel_id=1, source_target_pairs={{0,2},{1,9},{2,4},{3,11},{4,6},{5,13},{6,0},{7,15},{8,10},{9,17},{... | collective-permute-start | bytes 866312 | tf_op jit(solution)/shard_map/ppermute | solution.py:360
  101.7 9.3 %collective-permute-start.22 = (bf16[141,8,128]{2,1,0:T(8,128)(2,1)S(1)}, bf16[141,8,128]{2,1,0:T(8,128)(2,1)S(1)}, u32[]{:S(2)}, u32[]{:S(2)}) collective-permute-start(bf16[141,8,128]{2,1,0:T(8,128)(2,1)S(1)} %shard_map.143), channel_id=1, source_target_pairs={{0,4},{1,17},{2,6},{3,19},{4,0},{5,21},{6,2},{7,23},{8,12},{9,25},... | collective-permute-start | bytes 866312 | tf_op jit(solution)/shard_map/ppermute | solution.py:360
  111.3 7.4 %collective-permute-start.25 = (bf16[141,8,128]{2,1,0:T(8,128)(2,1)S(1)}, bf16[141,8,128]{2,1,0:T(8,128)(2,1)S(1)}, u32[]{:S(2)}, u32[]{:S(2)}) collective-permute-start(bf16[141,8,128]{2,1,0:T(8,128)(2,1)S(1)} %shard_map.146.own), channel_id=1, source_target_pairs={{0,16},{1,5},{2,18},{3,7},{4,20},{5,1},{6,22},{7,3},{8,24},{9,13},... | collective-permute-start | bytes 866312 | tf_op jit(solution)/shard_map/ppermute | solution.py:360
  112.5 9.3 %collective-permute-start.26 = (bf16[141,8,128]{2,1,0:T(8,128)(2,1)S(1)}, bf16[141,8,128]{2,1,0:T(8,128)(2,1)S(1)}, u32[]{:S(2)}, u32[]{:S(2)}) collective-permute-start(bf16[141,8,128]{2,1,0:T(8,128)(2,1)S(1)} %shard_map.146.own), channel_id=1, source_target_pairs={{0,8},{1,3},{2,10},{3,5},{4,12},{5,7},{6,14},{7,1},{8,16},{9,11},{... | collective-permute-start | bytes 866312 | tf_op jit(solution)/shard_map/ppermute | solution.py:360
  112.5 9.3 %collective-permute-start.27 = (bf16[141,8,128]{2,1,0:T(8,128)(2,1)S(1)}, bf16[141,8,128]{2,1,0:T(8,128)(2,1)S(1)}, u32[]{:S(2)}, u32[]{:S(2)}) collective-permute-start(bf16[141,8,128]{2,1,0:T(8,128)(2,1)S(1)} %shard_map.146.own), channel_id=1, source_target_pairs={{0,24},{1,7},{2,26},{3,1},{4,28},{5,3},{6,30},{7,5},{8,0},{9,15},{... | collective-permute-start | bytes 866312 | tf_op jit(solution)/shard_map/ppermute | solution.py:360
  122.1 5.8 %collective-permute-start.30 = (bf16[80,1792]{1,0:T(8,128)(2,1)S(1)}, bf16[80,1792]{1,0:T(8,128)(2,1)S(1)}, u32[]{:S(2)}, u32[]{:S(2)}) collective-permute-start(bf16[80,1792]{1,0:T(8,128)(2,1)S(1)} %shard_map.147.active), channel_id=1, source_target_pairs={{0,6},{1,25},{2,0},{3,27},{4,2},{5,29},{6,4},{7,31},{8,14},{9,1},{... | collective-permute-start | bytes 860168 | tf_op jit(solution)/shard_map/ppermute | solution.py:360
  122.8 10.1 %collective-permute-start.29 = (bf16[80,1792]{1,0:T(8,128)(2,1)S(1)}, bf16[80,1792]{1,0:T(8,128)(2,1)S(1)}, u32[]{:S(2)}, u32[]{:S(2)}) collective-permute-start(bf16[80,1792]{1,0:T(8,128)(2,1)S(1)} %shard_map.147.active), channel_id=1, source_target_pairs={{0,2},{1,9},{2,4},{3,11},{4,6},{5,13},{6,0},{7,15},{8,10},{9,17},{... | collective-permute-start | bytes 860168 | tf_op jit(solution)/shard_map/ppermute | solution.py:360
  123.6 9.7 %collective-permute-start.28 = (bf16[80,1792]{1,0:T(8,128)(2,1)S(1)}, bf16[80,1792]{1,0:T(8,128)(2,1)S(1)}, u32[]{:S(2)}, u32[]{:S(2)}) collective-permute-start(bf16[80,1792]{1,0:T(8,128)(2,1)S(1)} %shard_map.147.active), channel_id=1, source_target_pairs={{0,4},{1,17},{2,6},{3,19},{4,0},{5,21},{6,2},{7,23},{8,12},{9,25},... | collective-permute-start | bytes 860168 | tf_op jit(solution)/shard_map/ppermute | solution.py:360
  133.8 3.4 %collective-permute-start.31 = (f32[80,512]{1,0:T(8,128)S(1)}, f32[80,512]{1,0:T(8,128)S(1)}, u32[]{:S(2)}, u32[]{:S(2)}) collective-permute-start(f32[80,512]{1,0:T(8,128)S(1)} %shard_map.151), channel_id=1, source_target_pairs={{0,1},{1,0},{2,3},{3,2},{4,5},{5,4},{6,7},{7,6},{8,9},{9,8},{10,11... | collective-permute-start | bytes 491528 | tf_op jit(solution)/shard_map/ppermute | solution.py:427
  137.3 4.9 %collective-permute-start.32 = (bf16[80,512]{1,0:T(8,128)(2,1)S(1)}, bf16[80,512]{1,0:T(8,128)(2,1)S(1)}, u32[]{:S(2)}, u32[]{:S(2)}) collective-permute-start(bf16[80,512]{1,0:T(8,128)(2,1)S(1)} %add_convert_fusion.third), channel_id=1, source_target_pairs={{0,32},{32,64},{64,96},{96,0},{1,33},{33,65},{65,97},{97,1},{2,34}... | collective-permute-start | bytes 245768 | tf_op jit(solution)/shard_map/ppermute | solution.py:365
  142.7 6.1 %collective-permute-start.35 = (bf16[141,8,128]{2,1,0:T(8,128)(2,1)S(1)}, bf16[141,8,128]{2,1,0:T(8,128)(2,1)S(1)}, u32[]{:S(2)}, u32[]{:S(2)}) collective-permute-start(bf16[141,8,128]{2,1,0:T(8,128)(2,1)S(1)} %shard_map.155), channel_id=1, source_target_pairs={{0,6},{1,25},{2,0},{3,27},{4,2},{5,29},{6,4},{7,31},{8,14},{9,1},{... | collective-permute-start | bytes 866312 | tf_op jit(solution)/shard_map/ppermute | solution.py:360
  145.6 9.9 %collective-permute-start.34 = (bf16[141,8,128]{2,1,0:T(8,128)(2,1)S(1)}, bf16[141,8,128]{2,1,0:T(8,128)(2,1)S(1)}, u32[]{:S(2)}, u32[]{:S(2)}) collective-permute-start(bf16[141,8,128]{2,1,0:T(8,128)(2,1)S(1)} %shard_map.154), channel_id=1, source_target_pairs={{0,2},{1,9},{2,4},{3,11},{4,6},{5,13},{6,0},{7,15},{8,10},{9,17},{... | collective-permute-start | bytes 866312 | tf_op jit(solution)/shard_map/ppermute | solution.py:360
  146.1 9.3 %collective-permute-start.33 = (bf16[141,8,128]{2,1,0:T(8,128)(2,1)S(1)}, bf16[141,8,128]{2,1,0:T(8,128)(2,1)S(1)}, u32[]{:S(2)}, u32[]{:S(2)}) collective-permute-start(bf16[141,8,128]{2,1,0:T(8,128)(2,1)S(1)} %shard_map.153), channel_id=1, source_target_pairs={{0,4},{1,17},{2,6},{3,19},{4,0},{5,21},{6,2},{7,23},{8,12},{9,25},... | collective-permute-start | bytes 866312 | tf_op jit(solution)/shard_map/ppermute | solution.py:360
  155.8 7.4 %collective-permute-start.36 = (bf16[141,8,128]{2,1,0:T(8,128)(2,1)S(1)}, bf16[141,8,128]{2,1,0:T(8,128)(2,1)S(1)}, u32[]{:S(2)}, u32[]{:S(2)}) collective-permute-start(bf16[141,8,128]{2,1,0:T(8,128)(2,1)S(1)} %shard_map.156.own), channel_id=1, source_target_pairs={{0,16},{1,5},{2,18},{3,7},{4,20},{5,1},{6,22},{7,3},{8,24},{9,13},... | collective-permute-start | bytes 866312 | tf_op jit(solution)/shard_map/ppermute | solution.py:360
  156.6 9.7 %collective-permute-start.37 = (bf16[141,8,128]{2,1,0:T(8,128)(2,1)S(1)}, bf16[141,8,128]{2,1,0:T(8,128)(2,1)S(1)}, u32[]{:S(2)}, u32[]{:S(2)}) collective-permute-start(bf16[141,8,128]{2,1,0:T(8,128)(2,1)S(1)} %shard_map.156.own), channel_id=1, source_target_pairs={{0,8},{1,3},{2,10},{3,5},{4,12},{5,7},{6,14},{7,1},{8,16},{9,11},{... | collective-permute-start | bytes 866312 | tf_op jit(solution)/shard_map/ppermute | solution.py:360
  156.6 9.7 %collective-permute-start.38 = (bf16[141,8,128]{2,1,0:T(8,128)(2,1)S(1)}, bf16[141,8,128]{2,1,0:T(8,128)(2,1)S(1)}, u32[]{:S(2)}, u32[]{:S(2)}) collective-permute-start(bf16[141,8,128]{2,1,0:T(8,128)(2,1)S(1)} %shard_map.156.own), channel_id=1, source_target_pairs={{0,24},{1,7},{2,26},{3,1},{4,28},{5,3},{6,30},{7,5},{8,0},{9,15},{... | collective-permute-start | bytes 866312 | tf_op jit(solution)/shard_map/ppermute | solution.py:360
  166.6 6.1 %collective-permute-start.41 = (bf16[80,1792]{1,0:T(8,128)(2,1)S(1)}, bf16[80,1792]{1,0:T(8,128)(2,1)S(1)}, u32[]{:S(2)}, u32[]{:S(2)}) collective-permute-start(bf16[80,1792]{1,0:T(8,128)(2,1)S(1)} %shard_map.157.active), channel_id=1, source_target_pairs={{0,6},{1,25},{2,0},{3,27},{4,2},{5,29},{6,4},{7,31},{8,14},{9,1},{... | collective-permute-start | bytes 860168 | tf_op jit(solution)/shard_map/ppermute | solution.py:360
  167.5 10.1 %collective-permute-start.40 = (bf16[80,1792]{1,0:T(8,128)(2,1)S(1)}, bf16[80,1792]{1,0:T(8,128)(2,1)S(1)}, u32[]{:S(2)}, u32[]{:S(2)}) collective-permute-start(bf16[80,1792]{1,0:T(8,128)(2,1)S(1)} %shard_map.157.active), channel_id=1, source_target_pairs={{0,2},{1,9},{2,4},{3,11},{4,6},{5,13},{6,0},{7,15},{8,10},{9,17},{... | collective-permute-start | bytes 860168 | tf_op jit(solution)/shard_map/ppermute | solution.py:360
  168.3 9.7 %collective-permute-start.39 = (bf16[80,1792]{1,0:T(8,128)(2,1)S(1)}, bf16[80,1792]{1,0:T(8,128)(2,1)S(1)}, u32[]{:S(2)}, u32[]{:S(2)}) collective-permute-start(bf16[80,1792]{1,0:T(8,128)(2,1)S(1)} %shard_map.157.active), channel_id=1, source_target_pairs={{0,4},{1,17},{2,6},{3,19},{4,0},{5,21},{6,2},{7,23},{8,12},{9,25},... | collective-permute-start | bytes 860168 | tf_op jit(solution)/shard_map/ppermute | solution.py:360
  173.1 11.2 %copy-start.1 = (bf16[512]{0:T(512)(128)(2,1)S(1)}, bf16[512]{0:T(512)(128)(2,1)}, u32[]{:S(2)}) copy-start(bf16[512]{0:T(512)(128)(2,1)} %param.15) | copy-start | bytes 3076
  173.1 16.9 %slice-start.2 = ((s8[8388608]{0:T(1024)(128)(4,1)}), s8[4194304]{0:T(1024)(128)(4,1)S(1)}, s32[]{:S(2)}) async-start(s8[8388608]{0:T(1024)(128)(4,1)} %bitcast.22), calls=%async_computation.6 | async-start | bytes 8388608
  178.0 11.9 %slice-start.3 = ((s8[8388608]{0:T(1024)(128)(4,1)}), s8[4194304]{0:T(1024)(128)(4,1)S(1)}, s32[]{:S(2)}) async-start(s8[8388608]{0:T(1024)(128)(4,1)} %bitcast.22), calls=%async_computation.7 | async-start | bytes 8388608
  178.5 2.7 collective-permute-start.42
  181.5 8.4 %collective-permute-start.43 = (bf16[112,512]{1,0:T(8,128)(2,1)S(1)}, bf16[112,512]{1,0:T(8,128)(2,1)S(1)}, u32[]{:S(2)}, u32[]{:S(2)}) collective-permute-start(bf16[112,512]{1,0:T(8,128)(2,1)S(1)} %shard_map.162.held), channel_id=1, source_target_pairs={{0,32},{32,64},{64,96},{96,0},{1,33},{33,65},{65,97},{97,1},{2,34}... | collective-permute-start | bytes 344072 | tf_op jit(solution)/shard_map/ppermute | solution.py:365
  181.6 8.4 %collective-permute-start.44 = (bf16[112,512]{1,0:T(8,128)(2,1)S(1)}, bf16[112,512]{1,0:T(8,128)(2,1)S(1)}, u32[]{:S(2)}, u32[]{:S(2)}) collective-permute-start(bf16[112,512]{1,0:T(8,128)(2,1)S(1)} %shard_map.162.held), channel_id=1, source_target_pairs={{0,64},{32,96},{64,0},{96,32},{1,65},{33,97},{65,1},{97,33},{2,66}... | collective-permute-start | bytes 344072 | tf_op jit(solution)/shard_map/ppermute | solution.py:365
  182.1 7.9 %collective-permute-start.45 = (bf16[112,512]{1,0:T(8,128)(2,1)S(1)}, bf16[112,512]{1,0:T(8,128)(2,1)S(1)}, u32[]{:S(2)}, u32[]{:S(2)}) collective-permute-start(bf16[112,512]{1,0:T(8,128)(2,1)S(1)} %shard_map.162.held), channel_id=1, source_target_pairs={{0,96},{32,0},{64,32},{96,64},{1,97},{33,1},{65,33},{97,65},{2,98}... | collective-permute-start | bytes 344072 | tf_op jit(solution)/shard_map/ppermute | solution.py:365
